TPU v7x, 256 devices: a whole 4x4x8 slice. The times are simulated.
256 devices in a mesh: gx: 16 (over z, core), gy: 16 (over x, y).
Axes of the slice: x: 4, y: 4, z: 8, core: 2. Of those that a mesh axis runs over, the one named last changes fastest.
Arguments:
- tracers: bfloat16 [8, 128, 128, 256], P(None, 'gx', 'gy'), may hold values from -6 to 6
- velocity: float32 [2, 128, 128], P(None, 'gx', 'gy'), may hold values from -0.04 to 0.04
- inflow: int32 [4, 128, 128], P(None, 'gx', 'gy'), may hold values from 0 to 1, as said below
- leaf_solve: float32 [256, 256], replicated, may hold values from -0.375 to 0.375
- leaf_skeleton: float32 [256, 64], replicated, may hold values from -0.375 to 0.375
- leaf_lift: float32 [64, 256], replicated, may hold values from -0.75 to 0.75
- merge_first: float32 [128, 64], replicated, may hold values from -0.5 to 0.5
- merge_second: float32 [128, 128], replicated, may hold values from -0.5 to 0.5
- merge_rest: float32 [12, 256, 128], replicated, may hold values from -0.375 to 0.375
- parent_first: float32 [64, 128], replicated, may hold values from -0.75 to 0.75
- parent_second: float32 [128, 128], replicated, may hold values from -0.5 to 0.5
- parent_rest: float32 [12, 128, 256], replicated, may hold values from -0.5 to 0.5
- sibling_first: float32 [128, 128], replicated, may hold values from -0.125 to 0.125
- sibling_second: float32 [128, 128], replicated, may hold values from -0.125 to 0.125
- sibling_rest: float32 [12, 256, 256], replicated, may hold values from -0.09375 to 0.09375
- root_map: float32 [128, 128], replicated, may hold values from -0.5 to 0.5
Outputs:
- updated: bfloat16 [8, 128, 128, 256], P(None, 'gx', 'gy')
Inputs may be any that keep to these rules, and one draw needn't show every extreme that they name: inflow[0] of leaf (i, j) equals 1 minus inflow[1] of leaf (i - 1, j), and inflow[2] of leaf (i, j) equals 1 minus inflow[3] of leaf (i, j - 1); inflow[1] is 0 on the last leaves along the first dimension and inflow[3] on the last leaves along the second.
All inputs are finite; a program needn't handle non-finite values.
Results may differ from a plain program's by a relative error of at most 0.001.
Values may be sent and summed in bfloat16 or wider, within the bound.
No kernel may reach another device: no remote copies, remote signals or barrier semaphores. Data moves between devices by JAX's collectives and lax.ppermute only.
A program may use at most 64 MiB of HBM per device.

v0:
```python
import jax
import jax.numpy as jnp
from jax import lax
from jax.sharding import PartitionSpec as P

NODE = 16


highest = lax.Precision.HIGHEST


def padded_2(cells, sides, width):
    for axis, dim in sides:
        count = lax.axis_size(axis)
        ends = count - 1
        head = lax.slice_in_dim(cells, 0, width, axis=dim)
        tail = lax.slice_in_dim(cells, cells.shape[dim] - width, cells.shape[dim], axis=dim)
        cells = jnp.concatenate(
            [
                lax.ppermute(tail, axis, [(i, (i + 1) % count) for i in range(ends)]),
                cells,
                lax.ppermute(head, axis, [((i + 1) % count, i) for i in range(ends)]),
            ],
            axis=dim,
        )
    return cells


def product(left, right):
    return jnp.dot(left, right, precision=highest, preferred_element_type=jnp.float32)


def spectral_matrix(node_count):
    node_index = jnp.arange(node_count)
    points = -jnp.cos(jnp.pi * node_index.astype(jnp.float32) / (node_count - 1))
    end_weights = jnp.where((node_index == 0) | (node_index == node_count - 1), 2.0, 1.0)
    parity = jnp.where(node_index % 2 == 0, 1.0, -1.0)
    weights = (end_weights * parity).astype(jnp.float32)
    identity = jnp.eye(node_count, dtype=jnp.float32)
    offsets = points[:, None] - points[None, :] + identity
    matrix = weights[:, None] / weights[None, :] / offsets * (1.0 - identity)
    return matrix - jnp.diag(jnp.sum(matrix, axis=1))


def derivative_tables(node_count):
    spectral = spectral_matrix(node_count)
    identity = jnp.eye(node_count, dtype=jnp.float32)
    return jnp.concatenate([jnp.kron(spectral, identity).T, jnp.kron(identity, spectral).T], axis=1)


def side_table(node_count):
    node_index = jnp.arange(node_count * node_count)
    along_first = node_index // node_count
    along_second = node_index % node_count
    position = jnp.arange(node_count)[:, None]
    table_rows = [
        (along_first[None, :] == 0) & (along_second[None, :] == position),
        (along_first[None, :] == node_count - 1) & (along_second[None, :] == position),
        (along_second[None, :] == 0) & (along_first[None, :] == position),
        (along_second[None, :] == node_count - 1) & (along_first[None, :] == position),
    ]
    return jnp.concatenate(table_rows, axis=0).astype(jnp.float32)


def edge_values(tracer_field, node_count):
    node_grid = tracer_field.reshape(tracer_field.shape[:-1] + (node_count, node_count))
    return (
        node_grid[..., 0, :],
        node_grid[..., node_count - 1, :],
        node_grid[..., :, 0],
        node_grid[..., :, node_count - 1],
    )


def forcing_term(tracer_field, own_edges, neighbours, velocity, inflow):
    node_count = own_edges[0].shape[-1]
    square = node_count * node_count
    gradients = product(tracer_field, derivative_tables(node_count))
    advective = (
        velocity[0][None, :, :, None] * gradients[..., :square]
        + velocity[1][None, :, :, None] * gradients[..., square:]
    )
    penalty_terms = []
    for side_index in range(4):
        strength = inflow[side_index].astype(jnp.float32) * (
            node_count * jnp.abs(velocity[side_index // 2])
        )
        penalty_terms.append(
            strength[None, :, :, None] * (neighbours[side_index] - own_edges[side_index])
        )
    penalty = product(jnp.concatenate(penalty_terms, axis=-1), side_table(node_count))
    return tracer_field - advective + penalty


def level_operators(level, tables):
    if level == 0:
        return tables[0]
    if level == 1:
        return tables[1]
    return tuple((stacked[level - 2] for stacked in tables[2]))


def split_pairs(current, merge_axis):
    new_shape = (
        current.shape[:merge_axis]
        + (current.shape[merge_axis] // 2, 2)
        + current.shape[merge_axis + 1 :]
    )
    paired = current.reshape(new_shape)
    return (
        lax.index_in_dim(paired, 0, merge_axis + 1, False),
        lax.index_in_dim(paired, 1, merge_axis + 1, False),
    )


def join_pairs(former, latter, merge_axis):
    joined = jnp.stack([former, latter], axis=merge_axis + 1)
    new_shape = list(former.shape)
    new_shape[merge_axis] = new_shape[merge_axis] * 2
    return joined.reshape(tuple(new_shape))


def ascend(current, merge_plan, start_level, tables):
    levels = []
    for offset, merge_axis in enumerate(merge_plan):
        level = start_level + offset
        former, latter = split_pairs(current, merge_axis)
        levels.append((former, latter, merge_axis, level))
        current = product(
            jnp.concatenate([former, latter], axis=-1), level_operators(level, tables)[0]
        )
    return (current, levels)


def descend(boundary, levels, tables):
    for former, latter, merge_axis, level in reversed(levels):
        operators = level_operators(level, tables)
        joined_pair = product(boundary, operators[1]) + product(
            jnp.concatenate([former, latter], axis=-1), operators[2]
        )
        half_width = joined_pair.shape[-1] // 2
        boundary = join_pairs(
            joined_pair[..., :half_width], joined_pair[..., half_width:], merge_axis
        )
    return boundary


def local_plan(leaf_side):
    merge_plan = []
    block_span = leaf_side
    while block_span > 1:
        merge_plan = merge_plan + [1, 2]
        block_span = block_span // 2
    return merge_plan


def cross_plan(count_first, count_second):
    merge_plan = []
    while count_first * count_second > 1:
        if count_first >= count_second:
            merge_plan.append(1)
            count_first = count_first // 2
        else:
            merge_plan.append(2)
            count_second = count_second // 2
    return merge_plan


def local(
    tracers,
    velocity,
    inflow,
    leaf_solve,
    leaf_skeleton,
    leaf_lift,
    merge_first,
    merge_second,
    merge_rest,
    parent_first,
    parent_second,
    parent_rest,
    sibling_first,
    sibling_second,
    sibling_rest,
    root_map,
):
    tables = (
        (merge_first, parent_first, sibling_first),
        (merge_second, parent_second, sibling_second),
        (merge_rest, parent_rest, sibling_rest),
    )
    tracer_count, leaf_side = (tracers.shape[0], tracers.shape[1])
    tracer_field = tracers.astype(jnp.float32)
    own_edges = edge_values(tracer_field, NODE)
    padded = padded_2(tracers, (("gx", 1), ("gy", 2)), 1)
    node_grid = padded.reshape(padded.shape[:-1] + (NODE, NODE))
    neighbours = (
        node_grid[:, :leaf_side, 1 : leaf_side + 1, NODE - 1, :],
        node_grid[:, 2:, 1 : leaf_side + 1, 0, :],
        node_grid[:, 1 : leaf_side + 1, :leaf_side, :, NODE - 1],
        node_grid[:, 1 : leaf_side + 1, 2:, :, 0],
    )
    neighbours = tuple((edge_line.astype(jnp.float32) for edge_line in neighbours))
    forcing = forcing_term(tracer_field, own_edges, neighbours, velocity, inflow)
    skeleton = product(forcing, leaf_skeleton)
    block_plan = local_plan(leaf_side)
    block_root, local_levels = ascend(skeleton, block_plan, 0, tables)
    first_cross = len(block_plan)
    device_root = block_root[:, 0, 0]
    count_first, count_second = (lax.axis_size("gx"), lax.axis_size("gy"))
    merge_plan = cross_plan(count_first, count_second)
    gathered = lax.all_gather(device_root[:, None, :], ("gx", "gy"), axis=1, tiled=True)
    root_grid = gathered.reshape(tracer_count, count_first, count_second, device_root.shape[-1])
    tree_root, cross_levels = ascend(root_grid, merge_plan, first_cross, tables)
    boundary_grid = descend(product(tree_root, root_map), cross_levels, tables)
    along_first = lax.dynamic_index_in_dim(boundary_grid, lax.axis_index("gx"), 1, False)
    boundary = lax.dynamic_index_in_dim(along_first, lax.axis_index("gy"), 1, False)
    leaf_boundary = descend(boundary[:, None, None, :], local_levels, tables)
    updated = product(forcing, leaf_solve) + product(leaf_boundary, leaf_lift)
    return updated.astype(jnp.bfloat16)


def solution(mesh):
    in_specs = (
        P(None, "gx", "gy", None),
        P(None, "gx", "gy"),
        P(None, "gx", "gy"),
        P(),
        P(),
        P(),
        P(),
        P(),
        P(),
        P(),
        P(),
        P(),
        P(),
        P(),
        P(),
        P(),
    )
    out_specs = P(None, "gx", "gy", None)
    return jax.shard_map(local, mesh=mesh, in_specs=in_specs, out_specs=out_specs, check_vma=False)
```

profile of v0, /device:TPU:2, one launch (start us, length us, event | category | flops | bytes accessed | tf_op | source)
XLA Modules:
  0.0 204.0 jit_solution(10146088944830263196)
XLA Ops:
  7.4 1.7 collective-permute-start
  9.1 1.3 collective-permute-start.1
  10.4 3.7 %reshape.472 = f32[8,8,8,16,16]{4,3,2,1,0:T(8,128)} reshape(bf16[8,8,8,256]{3,2,1,0:T(8,128)(2,1)} %param.16) | data formatting | bytes 786432 | tf_op jit(solution)/shard_map/reshape | solution.py:66
  14.1 3.6 %fusion.220 = (f32[8,8,8,1,16]{4,3,2,1,0:T(1,128)}, f32[8,8,8,1,16]{4,3,2,1,0:T(1,128)}) fusion(f32[8,8,8,16,16]{4,3,2,1,0:T(8,128)} %reshape.472), kind=kLoop, calls=%fused_computation.362 | loop fusion | bytes 131072 | tf_op jit(solution)/shard_map/slice | solution.py:68
  17.7 8.2 %fusion.221 = (f32[8,8,8,16,1]{4,3,2,1,0:T(8,128)}, f32[8,8,8,16,1]{4,3,2,1,0:T(8,128)}) fusion(f32[8,8,8,16,16]{4,3,2,1,0:T(8,128)} %reshape.472), kind=kLoop, calls=%fused_computation.363 | loop fusion | bytes 131072 | tf_op jit(solution)/shard_map/slice | solution.py:70
  26.8 1.6 broadcast_multiply_fusion.1
  28.4 2.4 %mul.179 = f32[256,256]{0,1:T(8,128)S(1)} reshape(f32[16,16,16,16]{1,0,3,2:T(8,128)} %get-tuple-element.81) | data formatting | bytes 524288 | tf_op jit(solution)/shard_map/jit(kron)/mul | solution.py:48
  31.8 1.6 convolution_bitcast_fusion
  34.2 3.5 %collective-permute-start.2 = (bf16[8,10,1,256]{3,2,1,0:T(2,128)(2,1)S(1)}, bf16[8,10,1,256]{3,2,1,0:T(2,128)(2,1)S(1)}, u32[]{:S(2)}, u32[]{:S(2)}) collective-permute-start(bf16[8,10,1,256]{3,2,1,0:T(2,128)(2,1)S(1)} %get-tuple-element.25), channel_id=1, source_target_pairs={{0,1},{1,2},{2,3},{3,4},{4,5},{5,6},{6,7},{7,8},{8,9},{9,10},{10,1... | collective-permute-start | bytes 122888 | tf_op jit(solution)/shard_map/ppermute | solution.py:20
  37.6 4.5 %collective-permute-start.3 = (bf16[8,10,1,256]{3,2,1,0:T(2,128)(2,1)S(1)}, bf16[8,10,1,256]{3,2,1,0:T(2,128)(2,1)S(1)}, u32[]{:S(2)}, u32[]{:S(2)}) collective-permute-start(bf16[8,10,1,256]{3,2,1,0:T(2,128)(2,1)S(1)} %get-tuple-element.26), channel_id=1, source_target_pairs={{1,0},{2,1},{3,2},{4,3},{5,4},{6,5},{7,6},{8,7},{9,8},{10,9},{11,1... | collective-permute-start | bytes 122888 | tf_op jit(solution)/shard_map/ppermute | solution.py:22
  42.7 5.4 %copy.209 = f32[8,8,8,16,1]{3,2,1,0,4:T(8,128)} copy(f32[8,8,8,16,1]{4,3,2,1,0:T(8,128)} %get-tuple-element.7) | data formatting | bytes 65536
  48.5 1.0 copy.123
  49.5 3.6 %reshape.471 = bf16[8,10,10,16,16]{4,3,0,2,1:T(8,128)(2,1)S(1)} reshape(bf16[8,10,10,256]{3,0,2,1:T(8,128)(2,1)} %copy.123) | data formatting | bytes 819200 | tf_op jit(solution)/shard_map/reshape | solution.py:196
  53.1 1.3 fusion.222
  54.4 2.1 %slice.460 = bf16[8,8,8,16,1]{4,3,0,2,1:T(8,128)(2,1)} slice(bf16[8,10,10,16,16]{4,3,0,2,1:T(8,128)(2,1)S(1)} %reshape.471), slice={[0:8], [1:9], [0:8], [0:16], [15:16]} | slice | bytes 32768 | tf_op jit(solution)/shard_map/slice | solution.py:200
  57.4 2.7 %copy_subtract_fusion = f32[8,8,8,16,1]{4,3,0,2,1:T(8,128)} fusion(f32[8,8,8,16,1]{4,3,2,1,0:T(8,128)S(1)} %copy-done.1, bf16[8,10,10,16,16]{4,3,0,2,1:T(8,128)(2,1)S(1)} %reshape.471), kind=kLoop, calls=%fused_computation | loop fusion | flops 16384 | bytes 81920 | tf_op jit(solution)/shard_map/sub | solution.py:89
  60.1 4.9 %copy.131 = f32[8,8,8,16,1]{3,2,1,0,4:T(8,128)S(1)} copy(f32[8,8,8,16,1]{4,3,0,2,1:T(8,128)} %copy_subtract_fusion) | data formatting | bytes 65536 | tf_op jit(solution)/shard_map/sub | solution.py:89
  65.0 3.5 %copy.208 = bf16[8,8,8,16,1]{3,2,1,0,4:T(8,128)(2,1)S(1)} copy(bf16[8,8,8,16,1]{4,3,0,2,1:T(8,128)(2,1)S(1)} %copy-done.2) | data formatting | bytes 32768
  68.7 1.3 bitcast_multiply_fusion.2
  73.7 1.2 fusion.40
  75.5 104.9 %all-gather.3.cloned.1.call-done = f32[8,32768]{1,0:T(8,128)} async-done(((f32[8,128]{1,0:T(8,128)}), f32[8,32768]{1,0:T(8,128)}) %all-gather.3.cloned.1.call-update) | async-done | bytes 1048592 | tf_op jit(solution)/shard_map/all_gather | solution.py:212
  180.4 1.3 fusion.223
  191.3 1.2 convolution_add_fusion
  195.9 1.3 fusion
  (184 shorter events, 21.8 us)
Async XLA Ops:
  6.5 68.4 %copy-start = (f32[256,256]{1,0:T(8,128)S(1)}, f32[256,256]{1,0:T(8,128)}, u32[]{:S(2)}) copy-start(f32[256,256]{1,0:T(8,128)} %param.19) | copy-start | bytes 786436
  6.5 173.9 %all-gather.3.cloned.1.call-start = ((), (), s32[]{:S(2)}) async-start(), calls=%async_computation | async-start | bytes 1052672 | tf_op jit(solution)/shard_map/all_gather | solution.py:212
  7.4 26.6 %collective-permute-start = (bf16[8,1,8,256]{3,2,1,0:T(8,128)(2,1)S(1)}, bf16[8,1,8,256]{3,2,1,0:T(8,128)(2,1)S(1)}, u32[]{:S(2)}, u32[]{:S(2)}) collective-permute-start(bf16[8,1,8,256]{3,2,1,0:T(8,128)(2,1)S(1)} %get-tuple-element.36), channel_id=1, source_target_pairs={{0,16},{16,32},{32,48},{48,64},{64,80},{80,96},{96,112},{112,128},... | collective-permute-start | bytes 98312 | tf_op jit(solution)/shard_map/ppermute | solution.py:20
  9.1 24.9 %collective-permute-start.1 = (bf16[8,1,8,256]{3,2,1,0:T(8,128)(2,1)S(1)}, bf16[8,1,8,256]{3,2,1,0:T(8,128)(2,1)S(1)}, u32[]{:S(2)}, u32[]{:S(2)}) collective-permute-start(bf16[8,1,8,256]{3,2,1,0:T(8,128)(2,1)S(1)} %get-tuple-element.35), channel_id=1, source_target_pairs={{16,0},{32,16},{48,32},{64,48},{80,64},{96,80},{112,96},{128,112},... | collective-permute-start | bytes 98312 | tf_op jit(solution)/shard_map/ppermute | solution.py:22
  17.7 8.3 %copy-start.20 = (f32[2,8,8]{2,1,0:T(8,128)S(1)}, f32[2,8,8]{2,1,0:T(8,128)}, u32[]{:S(2)}) copy-start(f32[2,8,8]{2,1,0:T(8,128)} %param.17) | copy-start | bytes 1540
  17.7 8.9 %copy-start.28 = (s32[4,8,8]{2,1,0:T(8,128)S(1)}, s32[4,8,8]{2,1,0:T(8,128)}, u32[]{:S(2)}) copy-start(s32[4,8,8]{2,1,0:T(8,128)} %param.18) | copy-start | bytes 3076
  34.2 13.9 %collective-permute-start.2 = (bf16[8,10,1,256]{3,2,1,0:T(2,128)(2,1)S(1)}, bf16[8,10,1,256]{3,2,1,0:T(2,128)(2,1)S(1)}, u32[]{:S(2)}, u32[]{:S(2)}) collective-permute-start(bf16[8,10,1,256]{3,2,1,0:T(2,128)(2,1)S(1)} %get-tuple-element.25), channel_id=1, source_target_pairs={{0,1},{1,2},{2,3},{3,4},{4,5},{5,6},{6,7},{7,8},{8,9},{9,10},{10,1... | collective-permute-start | bytes 122888 | tf_op jit(solution)/shard_map/ppermute | solution.py:20
  37.6 10.4 %collective-permute-start.3 = (bf16[8,10,1,256]{3,2,1,0:T(2,128)(2,1)S(1)}, bf16[8,10,1,256]{3,2,1,0:T(2,128)(2,1)S(1)}, u32[]{:S(2)}, u32[]{:S(2)}) collective-permute-start(bf16[8,10,1,256]{3,2,1,0:T(2,128)(2,1)S(1)} %get-tuple-element.26), channel_id=1, source_target_pairs={{1,0},{2,1},{3,2},{4,3},{5,4},{6,5},{7,6},{8,7},{9,8},{10,9},{11,1... | collective-permute-start | bytes 122888 | tf_op jit(solution)/shard_map/ppermute | solution.py:22
  54.4 2.9 %copy-start.1 = (f32[8,8,8,16,1]{4,3,2,1,0:T(8,128)S(1)}, f32[8,8,8,16,1]{4,3,2,1,0:T(8,128)}, u32[]{:S(2)}) copy-start(f32[8,8,8,16,1]{4,3,2,1,0:T(8,128)} %get-tuple-element.8) | copy-start | bytes 98308
  60.1 4.9 %copy-start.2 = (bf16[8,8,8,16,1]{4,3,0,2,1:T(8,128)(2,1)S(1)}, bf16[8,8,8,16,1]{4,3,0,2,1:T(8,128)(2,1)}, u32[]{:S(2)}) copy-start(bf16[8,8,8,16,1]{4,3,0,2,1:T(8,128)(2,1)} %slice.460) | copy-start | bytes 49156
  64.9 3.6 %copy-start.8 = (f32[8,8,8,16,1]{3,2,1,0,4:T(8,128)S(1)}, f32[8,8,8,16,1]{3,2,1,0,4:T(8,128)}, u32[]{:S(2)}) copy-start(f32[8,8,8,16,1]{3,2,1,0,4:T(8,128)} %copy.209) | copy-start | bytes 98308
  65.0 3.7 %copy-start.9 = (f32[8,8,8,1,16]{4,3,2,1,0:T(1,128)S(1)}, f32[8,8,8,1,16]{4,3,2,1,0:T(1,128)}, u32[]{:S(2)}) copy-start(f32[8,8,8,1,16]{4,3,2,1,0:T(1,128)} %get-tuple-element.5) | copy-start | bytes 98308
  65.0 3.7 %copy-start.10 = (f32[8,8,8,1,16]{4,3,2,1,0:T(1,128)S(1)}, f32[8,8,8,1,16]{4,3,2,1,0:T(1,128)}, u32[]{:S(2)}) copy-start(f32[8,8,8,1,16]{4,3,2,1,0:T(1,128)} %get-tuple-element.6) | copy-start | bytes 98308
  68.4 1.6 copy-start.5
  68.5 1.6 copy-start.11
  68.5 1.6 copy-start.22
  68.5 1.6 copy-start.23
  183.0 2.5 %copy-start.16 = (f32[128,128]{1,0:T(8,128)S(1)}, f32[128,128]{1,0:T(8,128)}, u32[]{:S(2)}) copy-start(f32[128,128]{1,0:T(8,128)} %param.31) | copy-start | bytes 196612
  183.1 2.5 %copy-start.7 = (f32[12,128,256]{2,1,0:T(8,128)S(1)}, f32[12,128,256]{2,1,0:T(8,128)}, u32[]{:S(2)}) copy-start(f32[12,128,256]{2,1,0:T(8,128)} %param.27) | copy-start | bytes 4718596
  183.7 2.1 %copy-start.3 = (f32[12,256,256]{2,1,0:T(8,128)S(1)}, f32[12,256,256]{2,1,0:T(8,128)}, u32[]{:S(2)}) copy-start(f32[12,256,256]{2,1,0:T(8,128)} %param.30) | copy-start | bytes 9437188
  192.9 1.6 copy-start.12
  192.9 1.8 copy-start.13
  193.5 1.6 copy-start.19
  193.7 1.7 copy-start.14
  (10 other events, 12.8 us)
Sparse Core Ops, SparseCore 0:
  73.8 106.5 all-gather.2
where the time goes:
time: 206 us; the launch traced here: 204 us
  waiting for transfers between devices  105 us (51%)
  local copies, waits for them, and re-layouts  46.2 us (22%)
  matrix products  19.5 us (9%)
  between operations  14.6 us (7%)
  starting transfers between devices  11 us (5%)
  other arithmetic  7.81 us (4%)
    all_gather x1, waiting for transfers between devices, local(): lax.all_gather(device_root[:, None, :], ('gx', 'gy'), axis=1, tiled=True)  105 us
    dot_general x48, matrix products, product(): jnp.dot(left, right, precision=highest, preferred_element_type=jnp.float32)  19.5 us
    unnamed x66, local copies, waits for them, and re-layouts  10.4 us
    slice x1, local copies, waits for them, and re-layouts, edge_values(): node_grid[..., :, 0]  8.2 us
    ppermute x2, starting transfers between devices, padded_2(): lax.ppermute(head, axis, [((i + 1) % count, i) for i in range(ends)])  5.76 us
    ppermute x2, starting transfers between devices, padded_2(): lax.ppermute(tail, axis, [(i, (i + 1) % count) for i in range(ends)])  5.21 us
    sub x1, local copies, waits for them, and re-layouts, forcing_term(): neighbours[side_index] - own_edges[side_index]  4.86 us
  transfers between devices with their start and end apart: 5, of which 1 were waited for; matrix products, arithmetic and copies ran while one was open for 15% of the time, Pallas kernels for 0%

commit v1 on v0

v1 whole, which is shorter than its diff:
```python
import functools

import jax
import jax.numpy as jnp
import ml_dtypes
import numpy as np
from jax import lax
from jax.experimental import pallas as pl
from jax.experimental.pallas import tpu as pltpu
from jax.sharding import PartitionSpec as P

NODE = 16
SIDE = 8
BOTH = ("gx", "gy")
BF = jnp.bfloat16
F32 = jnp.float32
BITS = (16, 1, 32, 2, 64, 4, 128, 8)
PARAMS = pltpu.CompilerParams(vmem_limit_bytes=48 * 1024 * 1024)
VM = pl.BlockSpec(memory_space=pltpu.VMEM)


def derivative_pieces():
    index = np.arange(NODE)
    points = -np.cos(np.pi * index / (NODE - 1))
    weights = np.where((index == 0) | (index == NODE - 1), 2.0, 1.0) * np.where(index % 2 == 0, 1.0, -1.0)
    eye = np.eye(NODE)
    matrix = weights[:, None] / weights[None, :] / (points[:, None] - points[None, :] + eye) * (1.0 - eye)
    matrix = matrix - np.diag(matrix.sum(axis=1))
    table = np.concatenate([np.kron(matrix, eye).T, np.kron(eye, matrix).T], axis=1).astype(np.float32)
    high = table.astype(ml_dtypes.bfloat16)
    low = (table - high.astype(np.float32)).astype(ml_dtypes.bfloat16)
    return np.concatenate([high, low], axis=0)


def dot(left, right):
    return jnp.dot(left, right, preferred_element_type=F32)


def split(value):
    high = value.astype(BF)
    return high, (value - high.astype(F32)).astype(BF)


def mm(left, right):
    left_high, left_low = split(left)
    right_high, right_low = split(right)
    return dot(left_high, right_high) + dot(left_low, right_high) + dot(left_high, right_low)


def pair_up(rows, outer, inner):
    width = rows.shape[-1]
    paired = rows.reshape(outer, 2, inner, width)
    former = paired[:, 0].reshape(outer * inner, width)
    latter = paired[:, 1].reshape(outer * inner, width)
    return jnp.concatenate([former, latter], axis=-1)


def pair_down(joined, outer, inner):
    half = joined.shape[-1] // 2
    former = joined[:, :half].reshape(outer, 1, inner, half)
    latter = joined[:, half:].reshape(outer, 1, inner, half)
    return jnp.concatenate([former, latter], axis=1).reshape(outer * 2 * inner, half)


LOCAL = ((4, 64), (16, 8), (2, 32), (4, 8), (1, 16), (1, 8))


def up_kernel(u_ref, vel_ref, flow_ref, west_ref, east_ref, south_ref, north_ref, table_ref, skel_ref,
              first_ref, second_ref, rest_ref,
              forcing_ref, c0_ref, c1_ref, c2_ref, c3_ref, c4_ref, c5_ref, root_ref, turn_ref):
    ub = u_ref[...]
    u = ub.astype(F32)
    lane_j = lax.broadcasted_iota(jnp.int32, (64, SIDE), 1)
    row_j = lax.broadcasted_iota(jnp.int32, (64, SIDE), 0) % SIDE

    def column(plane):
        spread = jnp.broadcast_to(plane[:, None, :], (SIDE, SIDE, SIDE)).reshape(64, SIDE)
        return jnp.sum(jnp.where(lane_j == row_j, spread, 0.0), axis=1, keepdims=True)

    vel = [column(vel_ref[k]) for k in range(2)]
    force = [column(flow_ref[s].astype(F32)) * (NODE * jnp.abs(vel[s // 2])) for s in range(4)]
    grads = dot(ub, table_ref[:256]) + dot(ub, table_ref[256:])

    u4 = u.reshape(8, SIDE, SIDE, 256)
    before_i = jnp.concatenate([west_ref[...].astype(F32).reshape(8, 1, SIDE, 256), u4[:, :7]], axis=1).reshape(512, 256)
    after_i = jnp.concatenate([u4[:, 1:], east_ref[...].astype(F32).reshape(8, 1, SIDE, 256)], axis=1).reshape(512, 256)
    u3 = u.reshape(64, SIDE, 256)
    place = lax.broadcasted_iota(jnp.int32, (64, SIDE, 256), 1)
    before_j = jnp.where(place == 0, south_ref[...].astype(F32)[:, None, :], pltpu.roll(u3, 1, 1)).reshape(512, 256)
    after_j = jnp.where(place == 7, north_ref[...].astype(F32)[:, None, :], pltpu.roll(u3, 7, 1)).reshape(512, 256)
    lane = lax.broadcasted_iota(jnp.int32, (1, 256), 1)
    on = [lane < NODE, lane >= 256 - NODE, lane % NODE == 0, lane % NODE == NODE - 1]
    src_i = jnp.where(on[1], before_i, jnp.where(on[0], after_i, 0.0)).astype(BF)
    src_j = jnp.where(on[3], before_j, jnp.where(on[2], after_j, 0.0)).astype(BF)
    r = lax.broadcasted_iota(jnp.int32, (256, 256), 0)
    c = lax.broadcasted_iota(jnp.int32, (256, 256), 1)
    swap_i = ((r - c == 240) | (c - r == 240)).astype(F32).astype(BF)
    swap_j = (((r - c == 15) & (c % NODE == 0)) | ((c - r == 15) & (r % NODE == 0))).astype(F32).astype(BF)
    gap_i = dot(src_i, swap_i) - u
    gap_j = dot(src_j, swap_j) - u
    str_i = jnp.where(on[0], force[0], jnp.where(on[1], force[1], 0.0))
    str_j = jnp.where(on[2], force[2], jnp.where(on[3], force[3], 0.0))

    def leafwise(coefficient, field):
        return coefficient[None] * field.reshape(8, 64, 256)

    forcing = (
        u.reshape(8, 64, 256)
        - leafwise(vel[0], grads[:, :256])
        - leafwise(vel[1], grads[:, 256:])
        + leafwise(str_i, gap_i)
        + leafwise(str_j, gap_j)
    ).reshape(512, 256)
    forcing_ref[...] = forcing
    skel = skel_ref[...]
    turn_ref[...] = mm(forcing, jnp.concatenate([skel, jnp.zeros_like(skel)], axis=1))
    current = jnp.concatenate([turn_ref[pl.ds(q, 8, stride=64), :] for q in range(64)], axis=0)[:, :64]
    outs = (c0_ref, c1_ref, c2_ref, c3_ref, c4_ref, c5_ref)
    for k in range(6):
        both = pair_up(current, *LOCAL[k])
        outs[k][...] = both
        current = mm(both, first_ref[...] if k == 0 else second_ref[...] if k == 1 else rest_ref[k - 2])
    for g in range(16):
        root_ref[g] = current


def merge_all(current, weights, outs):
    for k, weight in enumerate(weights):
        outs[k][...] = current
        boxes = current.shape[0] // 8
        current = mm(pair_up(current, boxes // 2, 8), weight)
    return current


def mid_kernel(got_ref, rest_ref, s0_ref, s1_ref, s2_ref, s3_ref, root_ref):
    current = merge_all(
        got_ref[...].reshape(128, 128), [rest_ref[k] for k in range(4, 8)], (s0_ref, s1_ref, s2_ref, s3_ref)
    )
    for g in range(16):
        root_ref[g] = current


def down_kernel(got_ref, s0_ref, s1_ref, s2_ref, s3_ref, c0_ref, c1_ref, c2_ref, c3_ref, c4_ref, c5_ref, forcing_ref,
                rest_ref, pfirst_ref, psecond_ref, prest_ref, sfirst_ref, ssecond_ref, srest_ref, rootmap_ref,
                solve_ref, lift_ref, out_ref, h0_ref, h1_ref, h2_ref, h3_ref, turn_ref):
    spot = lax.axis_index("gx") * 16 + lax.axis_index("gy")
    top = merge_all(got_ref[...].reshape(128, 128), [rest_ref[k] for k in range(8, 12)], (h0_ref, h1_ref, h2_ref, h3_ref))
    boundary = mm(top, rootmap_ref[...])
    levels = (s0_ref, s1_ref, s2_ref, s3_ref, h0_ref, h1_ref, h2_ref, h3_ref)
    bit = [(spot // b) % 2 for b in BITS]
    for k in range(7, -1, -1):
        first = 4 * (k // 4)
        pair = jnp.int32(0)
        for q in range(first + 3, k, -1):
            pair = pair * 2 + bit[q]
        both = levels[k][pl.ds(pl.multiple_of(pair * 16, 16), 16), :]
        both = jnp.concatenate([both[:8], both[8:]], axis=1)
        joined = mm(boundary, prest_ref[k + 4]) + mm(both, srest_ref[k + 4])
        boundary = jnp.where(bit[k] == 1, joined[:, 128:], joined[:, :128])
    saved = (c0_ref, c1_ref, c2_ref, c3_ref, c4_ref, c5_ref)
    for k in range(5, -1, -1):
        down = pfirst_ref[...] if k == 0 else psecond_ref[...] if k == 1 else prest_ref[k - 2]
        across = sfirst_ref[...] if k == 0 else ssecond_ref[...] if k == 1 else srest_ref[k - 2]
        boundary = pair_down(mm(boundary, down) + mm(saved[k][...], across), *LOCAL[k])
    wide = jnp.concatenate([boundary, jnp.zeros_like(boundary)], axis=1)
    for q in range(64):
        turn_ref[pl.ds(q, 8, stride=64), :] = wide[8 * q : 8 * q + 8]
    updated = mm(forcing_ref[...], solve_ref[...]) + mm(turn_ref[:, :64], lift_ref[...])
    out_ref[...] = updated.astype(BF)


def groups_of(bits):
    every = sum(bits)
    groups = []
    for base in range(256):
        if base & every == 0:
            groups.append([base | sum(b for q, b in enumerate(bits) if c >> q & 1) for c in range(16)])
    return groups


def swap_roots(copies, bits):
    return lax.all_to_all(copies, BOTH, 0, 0, axis_index_groups=groups_of(bits))


def shape(*dims, dtype=F32):
    return jax.ShapeDtypeStruct(dims, dtype)


def call(kernel, outs, scratch=()):
    many = isinstance(outs, list)
    return pl.pallas_call(
        kernel,
        out_shape=outs,
        out_specs=[VM] * len(outs) if many else VM,
        scratch_shapes=list(scratch),
        compiler_params=PARAMS,
    )


def local(
    tracers,
    velocity,
    inflow,
    leaf_solve,
    leaf_skeleton,
    leaf_lift,
    merge_first,
    merge_second,
    merge_rest,
    parent_first,
    parent_second,
    parent_rest,
    sibling_first,
    sibling_second,
    sibling_rest,
    root_map,
):
    forward = [(i, i + 1) for i in range(15)]
    backward = [(i + 1, i) for i in range(15)]
    west = lax.ppermute(tracers[:, 7], "gx", forward)
    east = lax.ppermute(tracers[:, 0], "gx", backward)
    south = lax.ppermute(tracers[:, :, 7].reshape(64, 256), "gy", forward)
    north = lax.ppermute(tracers[:, :, 0].reshape(64, 256), "gy", backward)
    table = jnp.asarray(derivative_pieces())
    forcing, c0, c1, c2, c3, c4, c5, roots = call(
        up_kernel,
        [shape(512, 256), shape(256, 128), shape(128, 128), shape(64, 256), shape(32, 256), shape(16, 256),
         shape(8, 256), shape(16, 8, 128)],
        [pltpu.VMEM((512, 128), F32)],
    )(tracers.reshape(512, 256), velocity, inflow, west, east, south, north, table, leaf_skeleton,
      merge_first, merge_second, merge_rest[:4])
    got = swap_roots(roots, BITS[:4])
    s0, s1, s2, s3, roots = call(
        mid_kernel,
        [shape(128, 128), shape(64, 128), shape(32, 128), shape(16, 128), shape(16, 8, 128)],
    )(got, merge_rest)
    got = swap_roots(roots, BITS[4:])
    out = call(
        down_kernel,
        shape(512, 256, dtype=BF),
        [pltpu.VMEM((128, 128), F32), pltpu.VMEM((64, 128), F32), pltpu.VMEM((32, 128), F32),
         pltpu.VMEM((16, 128), F32), pltpu.VMEM((512, 128), F32)],
    )(got, s0, s1, s2, s3, c0, c1, c2, c3, c4, c5, forcing, merge_rest, parent_first, parent_second, parent_rest,
      sibling_first, sibling_second, sibling_rest, root_map, leaf_solve, leaf_lift)
    return out.reshape(tracers.shape)


def solution(mesh):
    whole = P()
    in_specs = (P(None, "gx", "gy", None), P(None, "gx", "gy"), P(None, "gx", "gy")) + (whole,) * 13
    out_specs = P(None, "gx", "gy", None)
    return jax.shard_map(local, mesh=mesh, in_specs=in_specs, out_specs=out_specs, check_vma=False)
```

time: 206 us -> 60 us (0.29)
  the two profiles are of different devices: /device:TPU:2 before, /device:TPU:1 now
where the time goes in v1:
time: 60 us; the launch traced here: 59.6 us
  blocking collectives  32 us (53%)
  starting transfers between devices  11.3 us (19%)
  Pallas kernels  10.5 us (18%)
  local copies, waits for them, and re-layouts  5.06 us (8%)
    all_to_all x2, blocking collectives, swap_roots(): return lax.all_to_all(copies, BOTH, 0, 0, axis_index_groups=groups_of(bits))  32 us
    pallas_call x1, Pallas kernels, local(): call(down_kernel, shape(512, 256, dtype=BF), [pltpu.VMEM((128, 128), F32)...  7.66 us
    ppermute x1, starting transfers between devices, local(): east = lax.ppermute(tracers[:, 0], 'gx', backward)  5.12 us
    ppermute x1, starting transfers between devices, local(): south = lax.ppermute(tracers[:, :, 7].reshape(64, 256), 'gy', forward)  3 us
    pallas_call x1, Pallas kernels, local(): call(up_kernel, [shape(512, 256), shape(256, 128), shape(128, 128), shape...  2.25 us
    unnamed x32, local copies, waits for them, and re-layouts  1.99 us
    ppermute x1, starting transfers between devices, local(): west = lax.ppermute(tracers[:, 7], 'gx', forward)  1.92 us
    ppermute x1, starting transfers between devices, local(): north = lax.ppermute(tracers[:, :, 0].reshape(64, 256), 'gy', backward)  1.29 us
  transfers between devices with their start and end apart: 4, of which 1 were waited for; matrix products, arithmetic and copies ran while one was open for 7% of the time, Pallas kernels for 0%

profile of v1, /device:TPU:1, one launch (start us, length us, event | category | flops | bytes accessed | tf_op | source)
XLA Modules:
  0.0 59.6 jit_solution(12803484026393572661)
XLA Ops:
  0.0 0.9 %slice_bitcast_fusion = (bf16[8,8,256]{2,1,0:T(8,128)(2,1)S(1)}, bf16[8,8,256]{2,1,0:T(8,128)(2,1)S(1)}) fusion(bf16[8,8,8,256]{3,2,1,0:T(8,128)(2,1)} %param.17), kind=kLoop, calls=%fused_computation.2 | loop fusion | bytes 131072 | tf_op jit(solution)/shard_map/squeeze | solution.py:221
  0.9 5.1 %collective-permute-start.1 = (bf16[8,8,256]{2,1,0:T(8,128)(2,1)S(1)}, bf16[8,8,256]{2,1,0:T(8,128)(2,1)S(1)}, u32[]{:S(2)}, u32[]{:S(2)}) collective-permute-start(bf16[8,8,256]{2,1,0:T(8,128)(2,1)S(1)} %get-tuple-element.33), channel_id=1, source_target_pairs={{16,0},{32,16},{48,32},{64,48},{80,64},{96,80},{112,96},{128,112},... | collective-permute-start | bytes 98312 | tf_op jit(solution)/shard_map/ppermute | solution.py:221
  6.0 1.9 %collective-permute-start = (bf16[8,8,256]{2,1,0:T(8,128)(2,1)S(1)}, bf16[8,8,256]{2,1,0:T(8,128)(2,1)S(1)}, u32[]{:S(2)}, u32[]{:S(2)}) collective-permute-start(bf16[8,8,256]{2,1,0:T(8,128)(2,1)S(1)} %get-tuple-element.34), channel_id=1, source_target_pairs={{0,16},{16,32},{32,48},{48,64},{64,80},{80,96},{96,112},{112,128},... | collective-permute-start | bytes 98312 | tf_op jit(solution)/shard_map/ppermute | solution.py:220
  7.9 1.1 %fusion = (bf16[8,8,1,256]{3,2,1,0:T(2,128)(2,1)S(1)}, bf16[8,8,1,256]{3,2,1,0:T(2,128)(2,1)S(1)}) fusion(bf16[8,8,8,256]{3,2,1,0:T(8,128)(2,1)} %param.17), kind=kLoop, calls=%fused_computation.4 | loop fusion | bytes 131072 | tf_op jit(solution)/shard_map/slice | solution.py:223
  9.1 3.0 %collective-permute-start.2 = (bf16[64,256]{1,0:T(8,128)(2,1)S(1)}, bf16[64,256]{1,0:T(8,128)(2,1)S(1)}, u32[]{:S(2)}, u32[]{:S(2)}) collective-permute-start(bf16[64,256]{1,0:T(8,128)(2,1)S(1)} %bitcast.17), channel_id=1, source_target_pairs={{0,1},{1,2},{2,3},{3,4},{4,5},{5,6},{6,7},{7,8},{8,9},{9,10},{10,1... | collective-permute-start | bytes 98312 | tf_op jit(solution)/shard_map/ppermute | solution.py:222
  12.1 1.3 %collective-permute-start.3 = (bf16[64,256]{1,0:T(8,128)(2,1)S(1)}, bf16[64,256]{1,0:T(8,128)(2,1)S(1)}, u32[]{:S(2)}, u32[]{:S(2)}) collective-permute-start(bf16[64,256]{1,0:T(8,128)(2,1)S(1)} %bitcast.18), channel_id=1, source_target_pairs={{1,0},{2,1},{3,2},{4,3},{5,4},{6,5},{7,6},{8,7},{9,8},{10,9},{11,1... | collective-permute-start | bytes 98312 | tf_op jit(solution)/shard_map/ppermute | solution.py:223
  13.4 0.8 %copy.27.first_ref = f32[128,64]{1,0:T(8,128)S(1)} copy(f32[128,64]{0,1:T(8,128)} %param.23) | data formatting | bytes 65536 | tf_op args[6]
  14.3 0.0 copy-start
  14.3 1.1 %copy.26.skel_ref = f32[256,64]{1,0:T(8,128)S(1)} copy(f32[256,64]{0,1:T(8,128)} %param.21) | data formatting | bytes 131072 | tf_op args[4]
  15.3 1.1 %slice.19.rest_ref = f32[4,256,128]{2,1,0:T(8,128)S(1)} slice(f32[12,256,128]{2,1,0:T(8,128)} %rest_ref.3), slice={[0:4], [0:256], [0:128]} | slice | bytes 1048576 | tf_op jit(solution)/shard_map/slice | solution.py:231
  16.5 0.4 collective-permute-done.3.north_ref
  16.9 0.0 copy-start.1
  16.9 0.0 copy-start.4
  16.9 0.0 copy-start.5
  16.9 0.0 copy-start.6
  16.9 0.0 copy-start.7
  16.9 0.0 copy-start.8
  17.0 0.0 copy-start.9
  17.0 0.0 copy-start.11
  17.0 2.3 %shard_map.163 = (f32[512,256]{1,0:T(8,128)S(1)}, f32[256,128]{1,0:T(8,128)S(1)}, f32[128,128]{1,0:T(8,128)S(1)}, f32[64,256]{1,0:T(8,128)S(1)}, f32[32,256]{1,0...) custom-call(bf16[512,256]{1,0:T(8,128)(2,1)S(1)} %bitcast.16, ...), custom_call_target="tpu_custom_call" | custom-call | tf_op jit(solution)/shard_map/pallas_call | solution.py:225
  19.2 13.4 %all_to_all.10.got_ref = f32[16,8,128]{2,1,0:T(8,128)S(1)} all-to-all(f32[16,8,128]{2,1,0:T(8,128)S(1)} %get-tuple-element.18), channel_id=1, replica_groups={{0,16,1,17,32,48,33,49,2,18,3,19,34,50,35,51},{4,20,5,21,36,52,37,53,6,..., dimensions={0} | all-to-all | bytes 131072 | tf_op jit(solution)/shard_map/all_to_all | solution.py:182
  32.6 0.6 shard_map.164
  33.2 18.7 %all_to_all.11.got_ref = f32[16,8,128]{2,1,0:T(8,128)S(1)} all-to-all(f32[16,8,128]{2,1,0:T(8,128)S(1)} %get-tuple-element.19), channel_id=1, replica_groups={{0,64,4,68,128,192,132,196,8,72,12,76,136,200,140,204},{1,65,5,69,129,1..., dimensions={0} | all-to-all | bytes 131072 | tf_op jit(solution)/shard_map/all_to_all | solution.py:182
  51.9 7.7 %shard_map.165 = bf16[512,256]{1,0:T(8,128)(2,1)} custom-call(f32[16,8,128]{2,1,0:T(8,128)S(1)} %all_to_all.11.got_ref, f32[128,128]{1,0:T(8,128)S(1)} %get-tuple-element.20.s0_ref, f32[64,128]{1,0:T(8,128)S(1)} %get-tuple-element.21.s1_ref, f32[32,128]{1,0:T(8,128)S(1)} %get-tuple-element.22.s2_ref, f32[16,128]{1,0:T(8,128)S(1)} %get-tuple-element.23.s3_ref, ...), custom_call_target="tpu_custom_call" | custom-call | tf_op jit(solution)/shard_map/pallas_call | solution.py:238
  (24 shorter events, 0.1 us)
Async XLA Ops:
  0.0 16.9 %copy-start.3 = (bf16[512,512]{1,0:T(8,128)(2,1)S(1)}, bf16[512,512]{1,0:T(8,128)(2,1)}, u32[]{:S(2)}) copy-start(bf16[512,512]{1,0:T(8,128)(2,1)} %constant.2.clone.table_ref) | copy-start | bytes 1572868
  0.0 16.9 %copy-start.2 = (bf16[8,8,8,256]{3,2,1,0:T(8,128)(2,1)S(1)}, bf16[8,8,8,256]{3,2,1,0:T(8,128)(2,1)}, u32[]{:S(2)}) copy-start(bf16[8,8,8,256]{3,2,1,0:T(8,128)(2,1)} %param.17) | copy-start | bytes 786436
  0.0 16.9 %copy-start.10 = (f32[128,128]{1,0:T(8,128)S(1)}, f32[128,128]{1,0:T(8,128)}, u32[]{:S(2)}) copy-start(f32[128,128]{1,0:T(8,128)} %second_ref.1) | copy-start | bytes 196612
  0.0 16.9 %copy-start.12 = (s32[4,8,8]{2,1,0:T(8,128)S(1)}, s32[4,8,8]{2,1,0:T(8,128)}, u32[]{:S(2)}) copy-start(s32[4,8,8]{2,1,0:T(8,128)} %flow_ref.1) | copy-start | bytes 3076
  0.0 16.9 %copy-start.13 = (f32[2,8,8]{2,1,0:T(8,128)S(1)}, f32[2,8,8]{2,1,0:T(8,128)}, u32[]{:S(2)}) copy-start(f32[2,8,8]{2,1,0:T(8,128)} %vel_ref.1) | copy-start | bytes 1540
  0.9 15.6 %collective-permute-start.1 = (bf16[8,8,256]{2,1,0:T(8,128)(2,1)S(1)}, bf16[8,8,256]{2,1,0:T(8,128)(2,1)S(1)}, u32[]{:S(2)}, u32[]{:S(2)}) collective-permute-start(bf16[8,8,256]{2,1,0:T(8,128)(2,1)S(1)} %get-tuple-element.33), channel_id=1, source_target_pairs={{16,0},{32,16},{48,32},{64,48},{80,64},{96,80},{112,96},{128,112},... | collective-permute-start | bytes 98312 | tf_op jit(solution)/shard_map/ppermute | solution.py:221
  6.0 10.4 %collective-permute-start = (bf16[8,8,256]{2,1,0:T(8,128)(2,1)S(1)}, bf16[8,8,256]{2,1,0:T(8,128)(2,1)S(1)}, u32[]{:S(2)}, u32[]{:S(2)}) collective-permute-start(bf16[8,8,256]{2,1,0:T(8,128)(2,1)S(1)} %get-tuple-element.34), channel_id=1, source_target_pairs={{0,16},{16,32},{32,48},{48,64},{64,80},{80,96},{96,112},{112,128},... | collective-permute-start | bytes 98312 | tf_op jit(solution)/shard_map/ppermute | solution.py:220
  9.1 7.4 %collective-permute-start.2 = (bf16[64,256]{1,0:T(8,128)(2,1)S(1)}, bf16[64,256]{1,0:T(8,128)(2,1)S(1)}, u32[]{:S(2)}, u32[]{:S(2)}) collective-permute-start(bf16[64,256]{1,0:T(8,128)(2,1)S(1)} %bitcast.17), channel_id=1, source_target_pairs={{0,1},{1,2},{2,3},{3,4},{4,5},{5,6},{6,7},{7,8},{8,9},{9,10},{10,1... | collective-permute-start | bytes 98312 | tf_op jit(solution)/shard_map/ppermute | solution.py:222
  12.1 4.7 %collective-permute-start.3 = (bf16[64,256]{1,0:T(8,128)(2,1)S(1)}, bf16[64,256]{1,0:T(8,128)(2,1)S(1)}, u32[]{:S(2)}, u32[]{:S(2)}) collective-permute-start(bf16[64,256]{1,0:T(8,128)(2,1)S(1)} %bitcast.18), channel_id=1, source_target_pairs={{1,0},{2,1},{3,2},{4,3},{5,4},{6,5},{7,6},{8,7},{9,8},{10,9},{11,1... | collective-permute-start | bytes 98312 | tf_op jit(solution)/shard_map/ppermute | solution.py:223
  14.3 18.3 %copy-start = (f32[12,256,128]{2,1,0:T(8,128)S(1)}, f32[12,256,128]{2,1,0:T(8,128)}, u32[]{:S(2)}) copy-start(f32[12,256,128]{2,1,0:T(8,128)} %rest_ref.3) | copy-start | bytes 4718596
  16.9 35.0 %copy-start.1 = (f32[12,128,256]{2,1,0:T(8,128)S(1)}, f32[12,128,256]{2,1,0:T(8,128)}, u32[]{:S(2)}) copy-start(f32[12,128,256]{2,1,0:T(8,128)} %prest_ref.1) | copy-start | bytes 4718596
  16.9 35.0 %copy-start.4 = (f32[256,256]{1,0:T(8,128)S(1)}, f32[256,256]{1,0:T(8,128)}, u32[]{:S(2)}) copy-start(f32[256,256]{1,0:T(8,128)} %solve_ref.1) | copy-start | bytes 786436
  16.9 34.9 %copy-start.5 = (f32[128,128]{1,0:T(8,128)S(1)}, f32[128,128]{1,0:T(8,128)}, u32[]{:S(2)}) copy-start(f32[128,128]{1,0:T(8,128)} %psecond_ref.1) | copy-start | bytes 196612
  16.9 34.9 %copy-start.6 = (f32[128,128]{1,0:T(8,128)S(1)}, f32[128,128]{1,0:T(8,128)}, u32[]{:S(2)}) copy-start(f32[128,128]{1,0:T(8,128)} %sfirst_ref.1) | copy-start | bytes 196612
  16.9 34.9 %copy-start.7 = (f32[128,128]{1,0:T(8,128)S(1)}, f32[128,128]{1,0:T(8,128)}, u32[]{:S(2)}) copy-start(f32[128,128]{1,0:T(8,128)} %ssecond_ref.1) | copy-start | bytes 196612
  16.9 34.9 %copy-start.8 = (f32[128,128]{1,0:T(8,128)S(1)}, f32[128,128]{1,0:T(8,128)}, u32[]{:S(2)}) copy-start(f32[128,128]{1,0:T(8,128)} %rootmap_ref.1) | copy-start | bytes 196612
  17.0 34.9 %copy-start.9 = (f32[64,256]{1,0:T(8,128)S(1)}, f32[64,256]{1,0:T(8,128)}, u32[]{:S(2)}) copy-start(f32[64,256]{1,0:T(8,128)} %lift_ref.1) | copy-start | bytes 196612
  17.0 34.9 %copy-start.11 = (f32[64,128]{1,0:T(8,128)S(1)}, f32[64,128]{1,0:T(8,128)}, u32[]{:S(2)}) copy-start(f32[64,128]{1,0:T(8,128)} %pfirst_ref.1) | copy-start | bytes 98308

commit v2 on v1

--- a/solution.py
+++ b/solution.py
@@ -43,8 +43,19 @@
 
 def mm(left, right):
     left_high, left_low = split(left)
-    right_high, right_low = split(right)
+    right_high, right_low = right if isinstance(right, tuple) else split(right)
     return dot(left_high, right_high) + dot(left_low, right_high) + dot(left_high, right_low)
+
+
+def mm_t(left, right):
+    sides = (((1,), (1,)), ((), ()))
+    left_high, left_low = split(left)
+    right_high, right_low = right[0], right[1]
+
+    def times(a, b):
+        return lax.dot_general(a, b, sides, preferred_element_type=F32)
+
+    return times(left_high, right_high) + times(left_low, right_high) + times(left_high, right_low)
 
 
 def pair_up(rows, outer, inner):
@@ -65,61 +76,114 @@
 LOCAL = ((4, 64), (16, 8), (2, 32), (4, 8), (1, 16), (1, 8))
 
 
-def up_kernel(u_ref, vel_ref, flow_ref, west_ref, east_ref, south_ref, north_ref, table_ref, skel_ref,
-              first_ref, second_ref, rest_ref,
-              forcing_ref, c0_ref, c1_ref, c2_ref, c3_ref, c4_ref, c5_ref, root_ref, turn_ref):
+def pack_kernel(u_ref, xa_ref, xb_ref, ya_ref, yb_ref):
+    even_x = lax.axis_index("gx") % 2 == 0
+    even_y = lax.axis_index("gy") % 2 == 0
+    u = u_ref[...].astype(F32)
+    low, high = u[:, 0], u[:, SIDE - 1]
+    xa_ref[...] = jnp.where(even_x, high, low).astype(BF)
+    xb_ref[...] = jnp.where(even_x, low, high).astype(BF)
+    low, high = u[:, :, 0], u[:, :, SIDE - 1]
+    ya_ref[...] = jnp.where(even_y, high, low).astype(BF)
+    yb_ref[...] = jnp.where(even_y, low, high).astype(BF)
+
+
+def lane_marks():
+    lane = lax.broadcasted_iota(jnp.int32, (1, 256), 1)
+    return lane < NODE, lane >= 256 - NODE, lane % NODE == 0, lane % NODE == NODE - 1
+
+
+def leafwise(coefficient, field):
+    return (coefficient[None] * field.reshape(8, 64, 256)).reshape(512, 256)
+
+
+def halo_rows(ref, turn, mark):
+    return jnp.where(mark, pltpu.roll(ref[...].astype(F32).reshape(64, 256), turn, 1), 0.0)
+
+
+def base_kernel(u_ref, vel_ref, flow_ref, table_ref, skel_ref, first_ref, second_ref, rest_ref, xa_ref,
+                base_ref, stri_ref, strj_ref, skel_out, first_out, second_out, rest_out):
     ub = u_ref[...]
     u = ub.astype(F32)
-    lane_j = lax.broadcasted_iota(jnp.int32, (64, SIDE), 1)
-    row_j = lax.broadcasted_iota(jnp.int32, (64, SIDE), 0) % SIDE
-
-    def column(plane):
-        spread = jnp.broadcast_to(plane[:, None, :], (SIDE, SIDE, SIDE)).reshape(64, SIDE)
-        return jnp.sum(jnp.where(lane_j == row_j, spread, 0.0), axis=1, keepdims=True)
-
-    vel = [column(vel_ref[k]) for k in range(2)]
-    force = [column(flow_ref[s].astype(F32)) * (NODE * jnp.abs(vel[s // 2])) for s in range(4)]
-    grads = dot(ub, table_ref[:256]) + dot(ub, table_ref[256:])
-
-    u4 = u.reshape(8, SIDE, SIDE, 256)
-    before_i = jnp.concatenate([west_ref[...].astype(F32).reshape(8, 1, SIDE, 256), u4[:, :7]], axis=1).reshape(512, 256)
-    after_i = jnp.concatenate([u4[:, 1:], east_ref[...].astype(F32).reshape(8, 1, SIDE, 256)], axis=1).reshape(512, 256)
-    u3 = u.reshape(64, SIDE, 256)
-    place = lax.broadcasted_iota(jnp.int32, (64, SIDE, 256), 1)
-    before_j = jnp.where(place == 0, south_ref[...].astype(F32)[:, None, :], pltpu.roll(u3, 1, 1)).reshape(512, 256)
-    after_j = jnp.where(place == 7, north_ref[...].astype(F32)[:, None, :], pltpu.roll(u3, 7, 1)).reshape(512, 256)
-    lane = lax.broadcasted_iota(jnp.int32, (1, 256), 1)
-    on = [lane < NODE, lane >= 256 - NODE, lane % NODE == 0, lane % NODE == NODE - 1]
-    src_i = jnp.where(on[1], before_i, jnp.where(on[0], after_i, 0.0)).astype(BF)
-    src_j = jnp.where(on[3], before_j, jnp.where(on[2], after_j, 0.0)).astype(BF)
+    on = lane_marks()
     r = lax.broadcasted_iota(jnp.int32, (256, 256), 0)
     c = lax.broadcasted_iota(jnp.int32, (256, 256), 1)
     swap_i = ((r - c == 240) | (c - r == 240)).astype(F32).astype(BF)
     swap_j = (((r - c == 15) & (c % NODE == 0)) | ((c - r == 15) & (r % NODE == 0))).astype(F32).astype(BF)
+    u4 = u.reshape(8, SIDE, SIDE, 256)
+    even_x = lax.axis_index("gx") % 2 == 0
+    beside = xa_ref[...].astype(F32).reshape(8, 1, SIDE, 256)
+    before_i = jnp.concatenate([jnp.where(even_x, 0.0, beside), u4[:, :7]], axis=1).reshape(512, 256)
+    after_i = jnp.concatenate([u4[:, 1:], jnp.where(even_x, beside, 0.0)], axis=1).reshape(512, 256)
+    u3 = u.reshape(64, SIDE, 256)
+    place = lax.broadcasted_iota(jnp.int32, (64, SIDE, 256), 1)
+    before_j = jnp.where(place == 0, 0.0, pltpu.roll(u3, 1, 1)).reshape(512, 256)
+    after_j = jnp.where(place == 7, 0.0, pltpu.roll(u3, 7, 1)).reshape(512, 256)
+    src_i = jnp.where(on[1], before_i, jnp.where(on[0], after_i, 0.0)).astype(BF)
+    src_j = jnp.where(on[3], before_j, jnp.where(on[2], after_j, 0.0)).astype(BF)
     gap_i = dot(src_i, swap_i) - u
     gap_j = dot(src_j, swap_j) - u
+    lane_j = lax.broadcasted_iota(jnp.int32, (64, SIDE), 1)
+    row_j = lax.broadcasted_iota(jnp.int32, (64, SIDE), 0) % SIDE
+
+    def column(plane):
+        spread = jnp.broadcast_to(plane[:, None, :], (SIDE, SIDE, SIDE)).reshape(64, SIDE)
+        return jnp.sum(jnp.where(lane_j == row_j, spread, 0.0), axis=1, keepdims=True)
+
+    vel = [column(vel_ref[k]) for k in range(2)]
+    force = [column(flow_ref[s].astype(F32)) * (NODE * jnp.abs(vel[s // 2])) for s in range(4)]
     str_i = jnp.where(on[0], force[0], jnp.where(on[1], force[1], 0.0))
     str_j = jnp.where(on[2], force[2], jnp.where(on[3], force[3], 0.0))
-
-    def leafwise(coefficient, field):
-        return coefficient[None] * field.reshape(8, 64, 256)
-
-    forcing = (
-        u.reshape(8, 64, 256)
+    stri_ref[...] = str_i
+    strj_ref[...] = str_j
+    grads = dot(ub, table_ref[:256]) + dot(ub, table_ref[256:])
+    base_ref[...] = (
+        u
         - leafwise(vel[0], grads[:, :256])
         - leafwise(vel[1], grads[:, 256:])
         + leafwise(str_i, gap_i)
         + leafwise(str_j, gap_j)
+    )
+    skel = skel_ref[...]
+    skel_out[0], skel_out[1] = split(jnp.concatenate([skel, jnp.zeros_like(skel)], axis=0))
+    first_out[0], first_out[1] = split(first_ref[...])
+    second_out[0], second_out[1] = split(second_ref[...])
+    for k in range(4):
+        rest_out[0, k], rest_out[1, k] = split(rest_ref[k])
+
+
+def up_kernel(base_ref, stri_ref, strj_ref, xb_ref, ya_ref, yb_ref, skel_ref, first_ref, second_ref, rest_ref,
+              forcing_ref, c0_ref, c1_ref, c2_ref, c3_ref, c4_ref, c5_ref, root_ref, turn_ref):
+    even_x = lax.axis_index("gx") % 2 == 0
+    even_y = lax.axis_index("gy") % 2 == 0
+    on = lane_marks()
+
+    west = jnp.where(even_x, halo_rows(xb_ref, 16, on[0]), 0.0).reshape(8, 1, SIDE, 256)
+    east = jnp.where(even_x, 0.0, halo_rows(xb_ref, 240, on[1])).reshape(8, 1, SIDE, 256)
+    south = jnp.where(even_y, halo_rows(yb_ref, 241, on[2]), halo_rows(ya_ref, 241, on[2]))
+    north = jnp.where(even_y, halo_rows(ya_ref, 15, on[3]), halo_rows(yb_ref, 15, on[3]))
+    place = lax.broadcasted_iota(jnp.int32, (64, SIDE, 256), 1)
+    side_j = jnp.where(place == 0, south[:, None, :], jnp.where(place == 7, north[:, None, :], 0.0))
+    inner = base_ref[...] + leafwise(strj_ref[...], side_j)
+    inner = inner.reshape(8, SIDE, SIDE, 256)
+    lower = stri_ref[:SIDE].reshape(1, 1, SIDE, 256)
+    upper = stri_ref[7 * SIDE :].reshape(1, 1, SIDE, 256)
+    forcing = jnp.concatenate(
+        [inner[:, :1] + lower * west, inner[:, 1:7], inner[:, 7:] + upper * east], axis=1
     ).reshape(512, 256)
     forcing_ref[...] = forcing
-    skel = skel_ref[...]
-    turn_ref[...] = mm(forcing, jnp.concatenate([skel, jnp.zeros_like(skel)], axis=1))
+    turn_ref[...] = mm_t(forcing, skel_ref)
     current = jnp.concatenate([turn_ref[pl.ds(q, 8, stride=64), :] for q in range(64)], axis=0)[:, :64]
     outs = (c0_ref, c1_ref, c2_ref, c3_ref, c4_ref, c5_ref)
     for k in range(6):
         both = pair_up(current, *LOCAL[k])
         outs[k][...] = both
-        current = mm(both, first_ref[...] if k == 0 else second_ref[...] if k == 1 else rest_ref[k - 2])
+        if k == 0:
+            current = mm_t(both, first_ref)
+        elif k == 1:
+            current = mm(both, (second_ref[0], second_ref[1]))
+        else:
+            current = mm(both, (rest_ref[0, k - 2], rest_ref[1, k - 2]))
     for g in range(16):
         root_ref[g] = current
 
@@ -186,7 +250,11 @@
     return jax.ShapeDtypeStruct(dims, dtype)
 
 
-def call(kernel, outs, scratch=()):
+def cost_of(mebibytes):
+    return pl.CostEstimate(flops=0, transcendentals=0, bytes_accessed=mebibytes * 2**20)
+
+
+def call(kernel, outs, scratch=(), cost=None):
     many = isinstance(outs, list)
     return pl.pallas_call(
         kernel,
@@ -194,6 +262,7 @@
         out_specs=[VM] * len(outs) if many else VM,
         scratch_shapes=list(scratch),
         compiler_params=PARAMS,
+        cost_estimate=cost,
     )
 
 
@@ -215,20 +284,26 @@
     sibling_rest,
     root_map,
 ):
-    forward = [(i, i + 1) for i in range(15)]
-    backward = [(i + 1, i) for i in range(15)]
-    west = lax.ppermute(tracers[:, 7], "gx", forward)
-    east = lax.ppermute(tracers[:, 0], "gx", backward)
-    south = lax.ppermute(tracers[:, :, 7].reshape(64, 256), "gy", forward)
-    north = lax.ppermute(tracers[:, :, 0].reshape(64, 256), "gy", backward)
+    swap = [(i, i ^ 1) for i in range(16)]
+    across = [(i, i + 1) for i in range(1, 15, 2)] + [(i + 1, i) for i in range(1, 15, 2)]
+    edge = shape(8, SIDE, 256, dtype=BF)
+    xa, xb, ya, yb = call(pack_kernel, [edge] * 4, cost=pl.CostEstimate(flops=10**10, transcendentals=0, bytes_accessed=2**25))(tracers)
+    yb = lax.ppermute(yb, "gy", across)
+    xb = lax.ppermute(xb, "gx", across)
+    ya = lax.ppermute(ya, "gy", swap)
+    xa = lax.ppermute(xa, "gx", swap)
     table = jnp.asarray(derivative_pieces())
+    base, str_i, str_j, skel, first, second, rest = call(
+        base_kernel,
+        [shape(512, 256), shape(64, 256), shape(64, 256), shape(2, 128, 256, dtype=BF),
+         shape(2, 64, 128, dtype=BF), shape(2, 128, 128, dtype=BF), shape(2, 4, 256, 128, dtype=BF)],
+    )(tracers.reshape(512, 256), velocity, inflow, table, leaf_skeleton.T, merge_first.T, merge_second, merge_rest, xa)
     forcing, c0, c1, c2, c3, c4, c5, roots = call(
         up_kernel,
         [shape(512, 256), shape(256, 128), shape(128, 128), shape(64, 256), shape(32, 256), shape(16, 256),
          shape(8, 256), shape(16, 8, 128)],
         [pltpu.VMEM((512, 128), F32)],
-    )(tracers.reshape(512, 256), velocity, inflow, west, east, south, north, table, leaf_skeleton,
-      merge_first, merge_second, merge_rest[:4])
+    )(base, str_i, str_j, xb, ya, yb, skel, first, second, rest)
     got = swap_roots(roots, BITS[:4])
     s0, s1, s2, s3, roots = call(
         mid_kernel,

time: 60 us -> 55.3 us (0.922)
  starting transfers between devices: 11.3 us -> 7.07 us
  local copies, waits for them, and re-layouts: 5.06 us -> 1.17 us
  blocking collectives: 32 us -> 34.9 us
    ppermute x4, starting transfers between devices: 11.3 us -> 7.07 us  [the longest x1 3.33 us: local(): xa = lax.ppermute(xa, 'gx', swap)]
    all_to_all x2, blocking collectives: 32 us -> 34.9 us  [swap_roots(): return lax.all_to_all(copies, BOTH, 0, 0, axis_index_groups=groups_of(bits))]
    slice x2 -> x0, local copies, waits for them, and re-layouts: 2.22 us -> none  [the longest x1 1.14 us: local(): north = lax.ppermute(tracers[:, :, 0].reshape(64, 256), 'gy', backward)]
    pallas_call x0 -> x2, Pallas kernels: none -> 1.01 us  [the longest x1 0.77 us: local(): call(base_kernel, [shape(512, 256), shape(64, 256), shape(64, 256), shape...]
    squeeze x1 -> x0, local copies, waits for them, and re-layouts: 0.85 us -> none  [local(): east = lax.ppermute(tracers[:, 0], 'gx', backward)]
    unnamed x32, local copies, waits for them, and re-layouts: 1.99 us -> 1.17 us
  transfers between devices with their start and end apart: 4 -> 4, of which waited for: 1 -> 1; matrix products, arithmetic and copies ran while one was open for 7% -> 0% of each run, Pallas kernels for 0% -> 1%
where the time goes in v2:
time: 55.3 us; the launch traced here: 55 us
  blocking collectives  34.9 us (63%)
  Pallas kernels  11.1 us (20%)
  starting transfers between devices  7.07 us (13%)
  local copies, waits for them, and re-layouts  1.17 us (2%)
  waiting for transfers between devices  0.61 us (1%)
    all_to_all x2, blocking collectives, swap_roots(): return lax.all_to_all(copies, BOTH, 0, 0, axis_index_groups=groups_of(bits))  34.9 us
    pallas_call x1, Pallas kernels, local(): call(down_kernel, shape(512, 256, dtype=BF), [pltpu.VMEM((128, 128), F32)...  7.66 us
    ppermute x1, starting transfers between devices, local(): xa = lax.ppermute(xa, 'gx', swap)  3.33 us
    ppermute x1, starting transfers between devices, local(): xb = lax.ppermute(xb, 'gx', across)  1.91 us
    pallas_call x1, Pallas kernels, local(): call(up_kernel, [shape(512, 256), shape(256, 128), shape(128, 128), shape...  1.82 us
    ppermute x1, starting transfers between devices, local(): ya = lax.ppermute(ya, 'gy', swap)  1.18 us
    unnamed x32, local copies, waits for them, and re-layouts  1.17 us
  transfers between devices with their start and end apart: 4, of which 1 were waited for; matrix products, arithmetic and copies ran while one was open for 0% of the time, Pallas kernels for 1%

profile of v2, /device:TPU:1, one launch (start us, length us, event | category | flops | bytes accessed | tf_op | source)
XLA Modules:
  0.0 55.0 jit_solution(18239241001257086394)
XLA Ops:
  0.0 1.1 %copy-done.3 = bf16[8,8,8,256]{3,2,1,0:T(8,128)(2,1)S(1)} copy-done((bf16[8,8,8,256]{3,2,1,0:T(8,128)(2,1)S(1)}, bf16[8,8,8,256]{3,2,1,0:T(8,128)(2,1)}, u32[]{:S(2)}) %copy-start.3) | copy-done | bytes 262168
  1.1 0.0 copy-start.15
  1.1 0.2 shard_map.163
  1.4 3.3 %collective-permute-start = (bf16[8,8,256]{2,1,0:T(8,128)(2,1)S(1)}, bf16[8,8,256]{2,1,0:T(8,128)(2,1)S(1)}, u32[]{:S(2)}, u32[]{:S(2)}) collective-permute-start(bf16[8,8,256]{2,1,0:T(8,128)(2,1)S(1)} %get-tuple-element.29), channel_id=1, source_target_pairs={{0,16},{16,0},{32,48},{48,32},{64,80},{80,64},{96,112},{112,96},{1... | collective-permute-start | bytes 98312 | tf_op jit(solution)/shard_map/ppermute | solution.py:294
  4.7 1.9 %collective-permute-start.1 = (bf16[8,8,256]{2,1,0:T(8,128)(2,1)S(1)}, bf16[8,8,256]{2,1,0:T(8,128)(2,1)S(1)}, u32[]{:S(2)}, u32[]{:S(2)}) collective-permute-start(bf16[8,8,256]{2,1,0:T(8,128)(2,1)S(1)} %get-tuple-element.33), channel_id=1, source_target_pairs={{16,32},{48,64},{80,96},{112,128},{144,160},{176,192},{208,224},{3... | collective-permute-start | bytes 98312 | tf_op jit(solution)/shard_map/ppermute | solution.py:292
  6.6 1.2 %collective-permute-start.2 = (bf16[8,8,256]{2,1,0:T(8,128)(2,1)S(1)}, bf16[8,8,256]{2,1,0:T(8,128)(2,1)S(1)}, u32[]{:S(2)}, u32[]{:S(2)}) collective-permute-start(bf16[8,8,256]{2,1,0:T(8,128)(2,1)S(1)} %get-tuple-element.34), channel_id=1, source_target_pairs={{0,1},{1,0},{2,3},{3,2},{4,5},{5,4},{6,7},{7,6},{8,9},{9,8},{10,11... | collective-permute-start | bytes 98312 | tf_op jit(solution)/shard_map/ppermute | solution.py:293
  7.8 0.7 %collective-permute-start.3 = (bf16[8,8,256]{2,1,0:T(8,128)(2,1)S(1)}, bf16[8,8,256]{2,1,0:T(8,128)(2,1)S(1)}, u32[]{:S(2)}, u32[]{:S(2)}) collective-permute-start(bf16[8,8,256]{2,1,0:T(8,128)(2,1)S(1)} %get-tuple-element.35), channel_id=1, source_target_pairs={{1,2},{3,4},{5,6},{7,8},{9,10},{11,12},{13,14},{2,1},{4,3},{6,5},{... | collective-permute-start | bytes 98312 | tf_op jit(solution)/shard_map/ppermute | solution.py:291
  8.5 0.0 collective-permute-done.xa_ref
  8.5 0.8 %shard_map.164 = (f32[512,256]{1,0:T(8,128)S(1)}, f32[64,256]{1,0:T(8,128)S(1)}, f32[64,256]{1,0:T(8,128)S(1)}, bf16[2,128,256]{2,1,0:T(8,128)(2,1)S(1)}, bf16[2...) custom-call(bf16[512,256]{1,0:T(8,128)(2,1)S(1)} %bitcast.4, ...), custom_call_target="tpu_custom_call" | custom-call | tf_op jit(solution)/shard_map/pallas_call | solution.py:296
  9.3 0.6 %collective-permute-done.1.xb_ref = bf16[8,8,256]{2,1,0:T(8,128)(2,1)S(1)} collective-permute-done((bf16[8,8,256]{2,1,0:T(8,128)(2,1)S(1)}, bf16[8,8,256]{2,1,0:T(8,128)(2,1)S(1)}, u32[]{:S(2)}, u32[]{:S(2)}) %collective-permute-start.1) | collective-permute-done | bytes 32800 | tf_op jit(solution)/shard_map/ppermute | solution.py:292
  9.9 0.0 collective-permute-done.2.ya_ref
  9.9 0.0 collective-permute-done.3.yb_ref
  9.9 0.0 copy-start.4
  9.9 0.0 copy-start.5
  9.9 0.0 copy-start.6
  10.0 0.0 copy-start.7
  10.0 0.0 copy-start.8
  10.0 0.0 copy-start.9
  10.0 0.0 copy-start.13
  10.0 1.8 %shard_map.165 = (f32[512,256]{1,0:T(8,128)S(1)}, f32[256,128]{1,0:T(8,128)S(1)}, f32[128,128]{1,0:T(8,128)S(1)}, f32[64,256]{1,0:T(8,128)S(1)}, f32[32,256]{1,0...) custom-call(f32[512,256]{1,0:T(8,128)S(1)} %get-tuple-element.30.base_ref, ...), custom_call_target="tpu_custom_call" | custom-call | tf_op jit(solution)/shard_map/pallas_call | solution.py:301
  11.8 15.2 %all_to_all.10.got_ref = f32[16,8,128]{2,1,0:T(8,128)S(1)} all-to-all(f32[16,8,128]{2,1,0:T(8,128)S(1)} %get-tuple-element.40), channel_id=1, replica_groups={{0,16,1,17,32,48,33,49,2,18,3,19,34,50,35,51},{4,20,5,21,36,52,37,53,6,..., dimensions={0} | all-to-all | bytes 131072 | tf_op jit(solution)/shard_map/all_to_all | solution.py:246
  27.0 0.6 %shard_map.166 = (f32[128,128]{1,0:T(8,128)S(1)}, f32[64,128]{1,0:T(8,128)S(1)}, f32[32,128]{1,0:T(8,128)S(1)}, f32[16,128]{1,0:T(8,128)S(1)}, f32[16,8,128]{2,1,0:T(8,128)S(1)}) custom-call(f32[16,8,128]{2,1,0:T(8,128)S(1)} %all_to_all.10.got_ref, f32[12,256,128]{2,1,0:T(8,128)S(1)} %copy-done), custom_call_target="tpu_custom_call" | custom-call | tf_op jit(solution)/shard_map/pallas_call | solution.py:308
  27.6 19.7 %all_to_all.11.got_ref = f32[16,8,128]{2,1,0:T(8,128)S(1)} all-to-all(f32[16,8,128]{2,1,0:T(8,128)S(1)} %get-tuple-element.41), channel_id=1, replica_groups={{0,64,4,68,128,192,132,196,8,72,12,76,136,200,140,204},{1,65,5,69,129,1..., dimensions={0} | all-to-all | bytes 131072 | tf_op jit(solution)/shard_map/all_to_all | solution.py:246
  47.4 7.7 %shard_map.167 = bf16[512,256]{1,0:T(8,128)(2,1)} custom-call(f32[16,8,128]{2,1,0:T(8,128)S(1)} %all_to_all.11.got_ref, f32[128,128]{1,0:T(8,128)S(1)} %get-tuple-element.42.s0_ref, f32[64,128]{1,0:T(8,128)S(1)} %get-tuple-element.43.s1_ref, f32[32,128]{1,0:T(8,128)S(1)} %get-tuple-element.44.s2_ref, f32[16,128]{1,0:T(8,128)S(1)} %get-tuple-element.45.s3_ref, ...), custom_call_target="tpu_custom_call" | custom-call | tf_op jit(solution)/shard_map/pallas_call | solution.py:313
  (23 shorter events, 0.0 us)
Async XLA Ops:
  0.0 8.5 %copy-start.2 = (bf16[512,512]{1,0:T(8,128)(2,1)S(1)}, bf16[512,512]{1,0:T(8,128)(2,1)}, u32[]{:S(2)}) copy-start(bf16[512,512]{1,0:T(8,128)(2,1)} %constant.2.clone.table_ref) | copy-start | bytes 1572868
  0.0 8.5 %copy-start = (f32[12,256,128]{2,1,0:T(8,128)S(1)}, f32[12,256,128]{2,1,0:T(8,128)}, u32[]{:S(2)}) copy-start(f32[12,256,128]{2,1,0:T(8,128)} %rest_ref.5) | copy-start | bytes 4718596
  0.0 1.1 %copy-start.3 = (bf16[8,8,8,256]{3,2,1,0:T(8,128)(2,1)S(1)}, bf16[8,8,8,256]{3,2,1,0:T(8,128)(2,1)}, u32[]{:S(2)}) copy-start(bf16[8,8,8,256]{3,2,1,0:T(8,128)(2,1)} %u_ref.1) | copy-start | bytes 786436
  1.1 7.4 %copy-start.10 = (f32[256,64]{0,1:T(8,128)S(1)}, f32[256,64]{0,1:T(8,128)}, u32[]{:S(2)}) copy-start(f32[256,64]{0,1:T(8,128)} %param.21) | copy-start | bytes 196612
  1.1 7.4 %copy-start.11 = (f32[128,128]{1,0:T(8,128)S(1)}, f32[128,128]{1,0:T(8,128)}, u32[]{:S(2)}) copy-start(f32[128,128]{1,0:T(8,128)} %second_ref.1) | copy-start | bytes 196612
  1.1 7.4 %copy-start.12 = (f32[128,64]{0,1:T(8,128)S(1)}, f32[128,64]{0,1:T(8,128)}, u32[]{:S(2)}) copy-start(f32[128,64]{0,1:T(8,128)} %param.23) | copy-start | bytes 98308
  1.1 7.4 %copy-start.14 = (s32[4,8,8]{2,1,0:T(8,128)S(1)}, s32[4,8,8]{2,1,0:T(8,128)}, u32[]{:S(2)}) copy-start(s32[4,8,8]{2,1,0:T(8,128)} %flow_ref.1) | copy-start | bytes 3076
  1.1 7.4 %copy-start.15 = (f32[2,8,8]{2,1,0:T(8,128)S(1)}, f32[2,8,8]{2,1,0:T(8,128)}, u32[]{:S(2)}) copy-start(f32[2,8,8]{2,1,0:T(8,128)} %vel_ref.1) | copy-start | bytes 1540
  1.4 7.1 %collective-permute-start = (bf16[8,8,256]{2,1,0:T(8,128)(2,1)S(1)}, bf16[8,8,256]{2,1,0:T(8,128)(2,1)S(1)}, u32[]{:S(2)}, u32[]{:S(2)}) collective-permute-start(bf16[8,8,256]{2,1,0:T(8,128)(2,1)S(1)} %get-tuple-element.29), channel_id=1, source_target_pairs={{0,16},{16,0},{32,48},{48,32},{64,80},{80,64},{96,112},{112,96},{1... | collective-permute-start | bytes 98312 | tf_op jit(solution)/shard_map/ppermute | solution.py:294
  4.7 5.2 %collective-permute-start.1 = (bf16[8,8,256]{2,1,0:T(8,128)(2,1)S(1)}, bf16[8,8,256]{2,1,0:T(8,128)(2,1)S(1)}, u32[]{:S(2)}, u32[]{:S(2)}) collective-permute-start(bf16[8,8,256]{2,1,0:T(8,128)(2,1)S(1)} %get-tuple-element.33), channel_id=1, source_target_pairs={{16,32},{48,64},{80,96},{112,128},{144,160},{176,192},{208,224},{3... | collective-permute-start | bytes 98312 | tf_op jit(solution)/shard_map/ppermute | solution.py:292
  6.6 3.3 %collective-permute-start.2 = (bf16[8,8,256]{2,1,0:T(8,128)(2,1)S(1)}, bf16[8,8,256]{2,1,0:T(8,128)(2,1)S(1)}, u32[]{:S(2)}, u32[]{:S(2)}) collective-permute-start(bf16[8,8,256]{2,1,0:T(8,128)(2,1)S(1)} %get-tuple-element.34), channel_id=1, source_target_pairs={{0,1},{1,0},{2,3},{3,2},{4,5},{5,4},{6,7},{7,6},{8,9},{9,8},{10,11... | collective-permute-start | bytes 98312 | tf_op jit(solution)/shard_map/ppermute | solution.py:293
  7.8 2.1 %collective-permute-start.3 = (bf16[8,8,256]{2,1,0:T(8,128)(2,1)S(1)}, bf16[8,8,256]{2,1,0:T(8,128)(2,1)S(1)}, u32[]{:S(2)}, u32[]{:S(2)}) collective-permute-start(bf16[8,8,256]{2,1,0:T(8,128)(2,1)S(1)} %get-tuple-element.35), channel_id=1, source_target_pairs={{1,2},{3,4},{5,6},{7,8},{9,10},{11,12},{13,14},{2,1},{4,3},{6,5},{... | collective-permute-start | bytes 98312 | tf_op jit(solution)/shard_map/ppermute | solution.py:291
  9.9 37.4 %copy-start.1 = (f32[12,128,256]{2,1,0:T(8,128)S(1)}, f32[12,128,256]{2,1,0:T(8,128)}, u32[]{:S(2)}) copy-start(f32[12,128,256]{2,1,0:T(8,128)} %prest_ref.1) | copy-start | bytes 4718596
  9.9 37.4 %copy-start.4 = (f32[256,256]{1,0:T(8,128)S(1)}, f32[256,256]{1,0:T(8,128)}, u32[]{:S(2)}) copy-start(f32[256,256]{1,0:T(8,128)} %solve_ref.1) | copy-start | bytes 786436
  9.9 37.4 %copy-start.5 = (f32[128,128]{1,0:T(8,128)S(1)}, f32[128,128]{1,0:T(8,128)}, u32[]{:S(2)}) copy-start(f32[128,128]{1,0:T(8,128)} %psecond_ref.1) | copy-start | bytes 196612
  9.9 37.4 %copy-start.6 = (f32[128,128]{1,0:T(8,128)S(1)}, f32[128,128]{1,0:T(8,128)}, u32[]{:S(2)}) copy-start(f32[128,128]{1,0:T(8,128)} %sfirst_ref.1) | copy-start | bytes 196612
  10.0 37.4 %copy-start.7 = (f32[128,128]{1,0:T(8,128)S(1)}, f32[128,128]{1,0:T(8,128)}, u32[]{:S(2)}) copy-start(f32[128,128]{1,0:T(8,128)} %ssecond_ref.1) | copy-start | bytes 196612
  10.0 37.4 %copy-start.8 = (f32[128,128]{1,0:T(8,128)S(1)}, f32[128,128]{1,0:T(8,128)}, u32[]{:S(2)}) copy-start(f32[128,128]{1,0:T(8,128)} %rootmap_ref.1) | copy-start | bytes 196612
  10.0 37.4 %copy-start.9 = (f32[64,256]{1,0:T(8,128)S(1)}, f32[64,256]{1,0:T(8,128)}, u32[]{:S(2)}) copy-start(f32[64,256]{1,0:T(8,128)} %lift_ref.1) | copy-start | bytes 196612
  10.0 37.4 %copy-start.13 = (f32[64,128]{1,0:T(8,128)S(1)}, f32[64,128]{1,0:T(8,128)}, u32[]{:S(2)}) copy-start(f32[64,128]{1,0:T(8,128)} %pfirst_ref.1) | copy-start | bytes 98308

commit v3 on v2

--- a/solution.py
+++ b/solution.py
@@ -16,6 +16,7 @@
 F32 = jnp.float32
 BITS = (16, 1, 32, 2, 64, 4, 128, 8)
 PARAMS = pltpu.CompilerParams(vmem_limit_bytes=48 * 1024 * 1024)
+WORK = pl.CostEstimate(flops=10**10, transcendentals=0, bytes_accessed=2**25)
 VM = pl.BlockSpec(memory_space=pltpu.VMEM)
 
 
@@ -197,40 +198,107 @@
 
 
 def mid_kernel(got_ref, rest_ref, s0_ref, s1_ref, s2_ref, s3_ref, root_ref):
-    current = merge_all(
+    root_ref[...] = merge_all(
         got_ref[...].reshape(128, 128), [rest_ref[k] for k in range(4, 8)], (s0_ref, s1_ref, s2_ref, s3_ref)
     )
-    for g in range(16):
-        root_ref[g] = current
-
-
-def down_kernel(got_ref, s0_ref, s1_ref, s2_ref, s3_ref, c0_ref, c1_ref, c2_ref, c3_ref, c4_ref, c5_ref, forcing_ref,
-                rest_ref, pfirst_ref, psecond_ref, prest_ref, sfirst_ref, ssecond_ref, srest_ref, rootmap_ref,
-                solve_ref, lift_ref, out_ref, h0_ref, h1_ref, h2_ref, h3_ref, turn_ref):
+
+
+def path_bits():
     spot = lax.axis_index("gx") * 16 + lax.axis_index("gy")
-    top = merge_all(got_ref[...].reshape(128, 128), [rest_ref[k] for k in range(8, 12)], (h0_ref, h1_ref, h2_ref, h3_ref))
-    boundary = mm(top, rootmap_ref[...])
-    levels = (s0_ref, s1_ref, s2_ref, s3_ref, h0_ref, h1_ref, h2_ref, h3_ref)
-    bit = [(spot // b) % 2 for b in BITS]
-    for k in range(7, -1, -1):
-        first = 4 * (k // 4)
+    return [(spot // b) % 2 for b in BITS]
+
+
+def halves(bit, former, latter):
+    return jnp.where(bit == 1, latter, former), jnp.where(bit == 1, former, latter)
+
+
+def ordered(bit, own, sibling):
+    return jnp.concatenate([jnp.where(bit == 1, sibling, own), jnp.where(bit == 1, own, sibling)], axis=1)
+
+
+def plan_kernel(s0_ref, s1_ref, s2_ref, s3_ref, rest_ref, prest_ref, srest_ref, rootmap_ref, plan_ref, known_ref):
+    bit = path_bits()
+
+    def mine(operators, k):
+        operator = operators[k + 4]
+        return jnp.where(bit[k] == 1, operator[:, 128:], operator[:, :128])
+
+    levels = (s0_ref, s1_ref, s2_ref, s3_ref)
+    known = jnp.zeros((8, 128), F32)
+    chain = [None, mine(prest_ref, 0)]
+    for k in range(1, 8):
+        chain.append(mm(mine(prest_ref, k), chain[k]))
+    for k in range(4):
         pair = jnp.int32(0)
-        for q in range(first + 3, k, -1):
+        for q in range(3, k, -1):
             pair = pair * 2 + bit[q]
         both = levels[k][pl.ds(pl.multiple_of(pair * 16, 16), 16), :]
         both = jnp.concatenate([both[:8], both[8:]], axis=1)
-        joined = mm(boundary, prest_ref[k + 4]) + mm(both, srest_ref[k + 4])
-        boundary = jnp.where(bit[k] == 1, joined[:, 128:], joined[:, :128])
+        term = mm(both, mine(srest_ref, k))
+        known = known + (term if k == 0 else mm(term, chain[k]))
+    known_ref[...] = known
+    above = mm(rootmap_ref[...], chain[8])
+    plan = [None] * 6
+    for k in (7, 6, 5):
+        full = mm(rest_ref[k + 4], above) + mm(mine(srest_ref, k), chain[k])
+        above, plan[k - 2] = halves(bit[k], full[:128], full[128:])
+    plan[2] = above
+    lowest = mm(mine(srest_ref, 4), chain[4])
+    plan[0], plan[1] = lowest[:128], lowest[128:]
+    for k in range(6):
+        plan_ref[0, k], plan_ref[1, k] = split(plan[k])
+
+
+def z_kernel(root_ref, a_ref, b_ref, c_ref, rest_ref, both_ref, pair_ref, last_ref):
+    bit = path_bits()
+    both = ordered(bit[4], root_ref[...], a_ref[...])
+    both_ref[...] = both
+    over = ordered(bit[4], b_ref[...], c_ref[...])
+    boxes = mm(jnp.concatenate([both, over], axis=0), rest_ref[8])
+    operator = rest_ref[9]
+    parts = mm(boxes, jnp.where(bit[5] == 1, operator[128:], operator[:128]))
+    pair_ref[0] = boxes[:8]
+    pair_ref[1] = parts[8:]
+    last_ref[...] = mm(ordered(bit[6], parts[:8], parts[8:]), rest_ref[10])
+
+
+def known_kernel(c0_ref, c1_ref, c2_ref, c3_ref, c4_ref, c5_ref, forcing_ref, pfirst_ref, psecond_ref, prest_ref,
+                 sfirst_ref, ssecond_ref, srest_ref, solve_ref, lift_ref, after_ref,
+                 part_ref, pfirst_out, psecond_out, prest_out, lift_out, turn_ref):
+    pfirst_out[0], pfirst_out[1] = split(pfirst_ref[...])
+    psecond_out[0], psecond_out[1] = split(psecond_ref[...])
+    for k in range(4):
+        prest_out[0, k], prest_out[1, k] = split(prest_ref[k])
+    lift_out[0], lift_out[1] = split(lift_ref[...])
+    downs = [pfirst_out, psecond_out] + [prest_out.at[:, k] for k in range(4)]
     saved = (c0_ref, c1_ref, c2_ref, c3_ref, c4_ref, c5_ref)
+    boundary = None
     for k in range(5, -1, -1):
-        down = pfirst_ref[...] if k == 0 else psecond_ref[...] if k == 1 else prest_ref[k - 2]
         across = sfirst_ref[...] if k == 0 else ssecond_ref[...] if k == 1 else srest_ref[k - 2]
-        boundary = pair_down(mm(boundary, down) + mm(saved[k][...], across), *LOCAL[k])
+        joined = mm(saved[k][...], across)
+        if boundary is not None:
+            joined = joined + mm(boundary, (downs[k][0], downs[k][1]))
+        boundary = pair_down(joined, *LOCAL[k])
     wide = jnp.concatenate([boundary, jnp.zeros_like(boundary)], axis=1)
     for q in range(64):
         turn_ref[pl.ds(q, 8, stride=64), :] = wide[8 * q : 8 * q + 8]
-    updated = mm(forcing_ref[...], solve_ref[...]) + mm(turn_ref[:, :64], lift_ref[...])
-    out_ref[...] = updated.astype(BF)
+    part_ref[...] = mm(forcing_ref[...], solve_ref[...]) + mm(turn_ref[:, :64], (lift_out[0], lift_out[1]))
+
+
+def last_kernel(both_ref, pair_ref, near_ref, far_ref, farther_ref, plan_ref, known_ref,
+                part_ref, pfirst_ref, psecond_ref, prest_ref, lift_ref, out_ref, turn_ref):
+    sources = [both_ref[...], pair_ref[0], near_ref[0], pair_ref[1] + near_ref[1], far_ref[...] + farther_ref[...]]
+    gathered = jnp.concatenate(sources, axis=1)
+    plan = plan_ref[...].reshape(2, 768, 128)
+    boundary = known_ref[...] + mm(gathered, (plan[0], plan[1]))
+    for k in range(5, 1, -1):
+        boundary = pair_down(mm(boundary, (prest_ref[0, k - 2], prest_ref[1, k - 2])), *LOCAL[k])
+    boundary = pair_down(mm(boundary, (psecond_ref[0], psecond_ref[1])), *LOCAL[1])
+    boundary = pair_down(mm(boundary, (pfirst_ref[0], pfirst_ref[1])), *LOCAL[0])
+    wide = jnp.concatenate([boundary, jnp.zeros_like(boundary)], axis=1)
+    for q in range(64):
+        turn_ref[pl.ds(q, 8, stride=64), :] = wide[8 * q : 8 * q + 8]
+    out_ref[...] = (part_ref[...] + mm(turn_ref[:, :64], (lift_ref[0], lift_ref[1]))).astype(BF)
 
 
 def groups_of(bits):
@@ -246,12 +314,12 @@
     return lax.all_to_all(copies, BOTH, 0, 0, axis_index_groups=groups_of(bits))
 
 
+def swap(value, mask):
+    return lax.ppermute(value, BOTH, [(i, i ^ mask) for i in range(256)])
+
+
 def shape(*dims, dtype=F32):
     return jax.ShapeDtypeStruct(dims, dtype)
-
-
-def cost_of(mebibytes):
-    return pl.CostEstimate(flops=0, transcendentals=0, bytes_accessed=mebibytes * 2**20)
 
 
 def call(kernel, outs, scratch=(), cost=None):
@@ -284,14 +352,14 @@
     sibling_rest,
     root_map,
 ):
-    swap = [(i, i ^ 1) for i in range(16)]
+    beside = [(i, i ^ 1) for i in range(16)]
     across = [(i, i + 1) for i in range(1, 15, 2)] + [(i + 1, i) for i in range(1, 15, 2)]
     edge = shape(8, SIDE, 256, dtype=BF)
-    xa, xb, ya, yb = call(pack_kernel, [edge] * 4, cost=pl.CostEstimate(flops=10**10, transcendentals=0, bytes_accessed=2**25))(tracers)
+    xa, xb, ya, yb = call(pack_kernel, [edge] * 4, cost=WORK)(tracers)
     yb = lax.ppermute(yb, "gy", across)
     xb = lax.ppermute(xb, "gx", across)
-    ya = lax.ppermute(ya, "gy", swap)
-    xa = lax.ppermute(xa, "gx", swap)
+    ya = lax.ppermute(ya, "gy", beside)
+    xa = lax.ppermute(xa, "gx", beside)
     table = jnp.asarray(derivative_pieces())
     base, str_i, str_j, skel, first, second, rest = call(
         base_kernel,
@@ -305,18 +373,26 @@
         [pltpu.VMEM((512, 128), F32)],
     )(base, str_i, str_j, xb, ya, yb, skel, first, second, rest)
     got = swap_roots(roots, BITS[:4])
-    s0, s1, s2, s3, roots = call(
+    s0, s1, s2, s3, root = call(
         mid_kernel,
-        [shape(128, 128), shape(64, 128), shape(32, 128), shape(16, 128), shape(16, 8, 128)],
+        [shape(128, 128), shape(64, 128), shape(32, 128), shape(16, 128), shape(8, 128)],
     )(got, merge_rest)
-    got = swap_roots(roots, BITS[4:])
-    out = call(
-        down_kernel,
-        shape(512, 256, dtype=BF),
-        [pltpu.VMEM((128, 128), F32), pltpu.VMEM((64, 128), F32), pltpu.VMEM((32, 128), F32),
-         pltpu.VMEM((16, 128), F32), pltpu.VMEM((512, 128), F32)],
-    )(got, s0, s1, s2, s3, c0, c1, c2, c3, c4, c5, forcing, merge_rest, parent_first, parent_second, parent_rest,
-      sibling_first, sibling_second, sibling_rest, root_map, leaf_solve, leaf_lift)
+    third, second_z, first_z = swap(root, 192), swap(root, 128), swap(root, 64)
+    plan, known = call(plan_kernel, [shape(2, 6, 128, 128, dtype=BF), shape(8, 128)], cost=WORK)(
+        s0, s1, s2, s3, merge_rest, parent_rest, sibling_rest, root_map)
+    both, pair, last = call(z_kernel, [shape(8, 256), shape(2, 8, 128), shape(8, 128)])(
+        root, first_z, second_z, third, merge_rest)
+    farther, far, near = swap(last, 12), swap(last, 8), swap(pair, 4)
+    part, pfirst, psecond, prest, lift = call(
+        known_kernel,
+        [shape(512, 256), shape(2, 64, 128, dtype=BF), shape(2, 128, 128, dtype=BF), shape(2, 4, 128, 256, dtype=BF),
+         shape(2, 64, 256, dtype=BF)],
+        [pltpu.VMEM((512, 128), F32)],
+        cost=WORK,
+    )(c0, c1, c2, c3, c4, c5, forcing, parent_first, parent_second, parent_rest, sibling_first, sibling_second,
+      sibling_rest, leaf_solve, leaf_lift, last)
+    out = call(last_kernel, shape(512, 256, dtype=BF), [pltpu.VMEM((512, 128), F32)])(
+        both, pair, near, far, farther, plan, known, part, pfirst, psecond, prest, lift)
     return out.reshape(tracers.shape)
 
 

time: 55.3 us -> 52.6 us (0.951)
  the two profiles are of different devices: /device:TPU:1 before, /device:TPU:2 now
where the time goes in v3:
time: 52.6 us; the launch traced here: 52.3 us
  starting transfers between devices  19.8 us (38%)
  Pallas kernels  14.3 us (27%)
  blocking collectives  12.4 us (24%)
  waiting for transfers between devices  4.35 us (8%)
  local copies, waits for them, and re-layouts  1.17 us (2%)
    ppermute x6, starting transfers between devices, swap(): return lax.ppermute(value, BOTH, [(i, i ^ mask) for i in range(256)])  13.4 us
    all_to_all x1, blocking collectives, swap_roots(): return lax.all_to_all(copies, BOTH, 0, 0, axis_index_groups=groups_of(bits))  12.4 us
    pallas_call x1, Pallas kernels, local(): call(plan_kernel, [shape(2, 6, 128, 128, dtype=BF), shape(8, 128)], cost=...  4.23 us
    ppermute x1, starting transfers between devices, local(): yb = lax.ppermute(yb, 'gy', across)  4.05 us
    pallas_call x1, Pallas kernels, local(): call(known_kernel, [shape(512, 256), shape(2, 64, 128, dtype=BF), shape(2...  3.78 us
    ppermute x1, waiting for transfers between devices, local(): yb = lax.ppermute(yb, 'gy', across)  2.95 us
    pallas_call x1, Pallas kernels, local(): call(last_kernel, shape(512, 256, dtype=BF), [pltpu.VMEM((512, 128), F32)])  2.47 us
    pallas_call x1, Pallas kernels, local(): call(up_kernel, [shape(512, 256), shape(256, 128), shape(128, 128), shape...  1.82 us
  transfers between devices with their start and end apart: 10, of which 2 were waited for; matrix products, arithmetic and copies ran while one was open for 0% of the time, Pallas kernels for 17%

profile of v3, /device:TPU:2, one launch (start us, length us, event | category | flops | bytes accessed | tf_op | source)
XLA Modules:
  0.0 52.3 jit_solution(9662385556545832156)
XLA Ops:
  0.0 1.1 %copy-done.2 = bf16[8,8,8,256]{3,2,1,0:T(8,128)(2,1)S(1)} copy-done((bf16[8,8,8,256]{3,2,1,0:T(8,128)(2,1)S(1)}, bf16[8,8,8,256]{3,2,1,0:T(8,128)(2,1)}, u32[]{:S(2)}) %copy-start.2) | copy-done | bytes 262168
  1.1 0.2 shard_map.163
  1.4 0.1 collective-permute-start
  1.5 0.7 %collective-permute-start.1 = (bf16[8,8,256]{2,1,0:T(8,128)(2,1)S(1)}, bf16[8,8,256]{2,1,0:T(8,128)(2,1)S(1)}, u32[]{:S(2)}, u32[]{:S(2)}) collective-permute-start(bf16[8,8,256]{2,1,0:T(8,128)(2,1)S(1)} %get-tuple-element.43), channel_id=1, source_target_pairs={{16,32},{48,64},{80,96},{112,128},{144,160},{176,192},{208,224},{3... | collective-permute-start | bytes 98312 | tf_op jit(solution)/shard_map/ppermute | solution.py:360
  2.1 1.7 %collective-permute-start.2 = (bf16[8,8,256]{2,1,0:T(8,128)(2,1)S(1)}, bf16[8,8,256]{2,1,0:T(8,128)(2,1)S(1)}, u32[]{:S(2)}, u32[]{:S(2)}) collective-permute-start(bf16[8,8,256]{2,1,0:T(8,128)(2,1)S(1)} %get-tuple-element.44), channel_id=1, source_target_pairs={{0,1},{1,0},{2,3},{3,2},{4,5},{5,4},{6,7},{7,6},{8,9},{9,8},{10,11... | collective-permute-start | bytes 98312 | tf_op jit(solution)/shard_map/ppermute | solution.py:361
  3.8 4.0 %collective-permute-start.3 = (bf16[8,8,256]{2,1,0:T(8,128)(2,1)S(1)}, bf16[8,8,256]{2,1,0:T(8,128)(2,1)S(1)}, u32[]{:S(2)}, u32[]{:S(2)}) collective-permute-start(bf16[8,8,256]{2,1,0:T(8,128)(2,1)S(1)} %get-tuple-element.45), channel_id=1, source_target_pairs={{1,2},{3,4},{5,6},{7,8},{9,10},{11,12},{13,14},{2,1},{4,3},{6,5},{... | collective-permute-start | bytes 98312 | tf_op jit(solution)/shard_map/ppermute | solution.py:359
  7.9 0.8 %shard_map.164 = (f32[512,256]{1,0:T(8,128)S(1)}, f32[64,256]{1,0:T(8,128)S(1)}, f32[64,256]{1,0:T(8,128)S(1)}, bf16[2,128,256]{2,1,0:T(8,128)(2,1)S(1)}, bf16[2...) custom-call(bf16[512,256]{1,0:T(8,128)(2,1)S(1)} %bitcast.4, ...), custom_call_target="tpu_custom_call" | custom-call | tf_op jit(solution)/shard_map/pallas_call | solution.py:364
  8.8 3.0 %collective-permute-done.3.yb_ref = bf16[8,8,256]{2,1,0:T(8,128)(2,1)S(1)} collective-permute-done((bf16[8,8,256]{2,1,0:T(8,128)(2,1)S(1)}, bf16[8,8,256]{2,1,0:T(8,128)(2,1)S(1)}, u32[]{:S(2)}, u32[]{:S(2)}) %collective-permute-start.3) | collective-permute-done | bytes 32800 | tf_op jit(solution)/shard_map/ppermute | solution.py:359
  11.7 1.8 %shard_map.165 = (f32[512,256]{1,0:T(8,128)S(1)}, f32[256,128]{1,0:T(8,128)S(1)}, f32[128,128]{1,0:T(8,128)S(1)}, f32[64,256]{1,0:T(8,128)S(1)}, f32[32,256]{1,0...) custom-call(f32[512,256]{1,0:T(8,128)S(1)} %get-tuple-element.40.base_ref, ...), custom_call_target="tpu_custom_call" | custom-call | tf_op jit(solution)/shard_map/pallas_call | solution.py:369
  13.5 12.4 %all_to_all.5.got_ref = f32[16,8,128]{2,1,0:T(8,128)S(1)} all-to-all(f32[16,8,128]{2,1,0:T(8,128)S(1)} %get-tuple-element.50), channel_id=1, replica_groups={{0,16,1,17,32,48,33,49,2,18,3,19,34,50,35,51},{4,20,5,21,36,52,37,53,6,..., dimensions={0} | all-to-all | bytes 131072 | tf_op jit(solution)/shard_map/all_to_all | solution.py:314
  25.9 0.6 %shard_map.166 = (f32[128,128]{1,0:T(8,128)S(1)}, f32[64,128]{1,0:T(8,128)S(1)}, f32[32,128]{1,0:T(8,128)S(1)}, f32[16,128]{1,0:T(8,128)S(1)}, f32[8,128]{1,0:T(8,128)S(1)}) custom-call(f32[16,8,128]{2,1,0:T(8,128)S(1)} %all_to_all.5.got_ref, f32[12,256,128]{2,1,0:T(8,128)S(1)} %copy-done), custom_call_target="tpu_custom_call" | custom-call | tf_op jit(solution)/shard_map/pallas_call | solution.py:376
  26.5 4.5 %collective-permute-start.4 = (f32[8,128]{1,0:T(8,128)S(1)}, f32[8,128]{1,0:T(8,128)S(1)}, u32[]{:S(2)}, u32[]{:S(2)}) collective-permute-start(f32[8,128]{1,0:T(8,128)S(1)} %get-tuple-element.51.root_ref), channel_id=1, source_target_pairs={{0,64},{1,65},{2,66},{3,67},{4,68},{5,69},{6,70},{7,71},{8,72},{9,... | collective-permute-start | bytes 12296 | tf_op jit(solution)/shard_map/ppermute | solution.py:318
  30.9 4.2 %collective-permute-start.5 = (f32[8,128]{1,0:T(8,128)S(1)}, f32[8,128]{1,0:T(8,128)S(1)}, u32[]{:S(2)}, u32[]{:S(2)}) collective-permute-start(f32[8,128]{1,0:T(8,128)S(1)} %get-tuple-element.51.root_ref), channel_id=1, source_target_pairs={{0,128},{1,129},{2,130},{3,131},{4,132},{5,133},{6,134},{7,135},{8... | collective-permute-start | bytes 12296 | tf_op jit(solution)/shard_map/ppermute | solution.py:318
  35.1 4.2 %shard_map.168 = (bf16[2,6,128,128]{3,2,1,0:T(8,128)(2,1)S(1)}, f32[8,128]{1,0:T(8,128)S(1)}) custom-call(f32[128,128]{1,0:T(8,128)S(1)} %get-tuple-element.55.s0_ref, f32[64,128]{1,0:T(8,128)S(1)} %get-tuple-element.56.s1_ref, f32[32,128]{1,0:T(8,128)S(1)} %get-tuple-element.57.s2_ref, f32[16,128]{1,0:T(8,128)S(1)} %get-tuple-element.58.s3_ref, ...), custom_call_target="tpu_custom_call" | custom-call | flops 10000000000 | bytes 33554432 | tf_op jit(solution)/shard_map/pallas_call | solution.py:381
  39.4 0.0 copy-start.9
  39.4 0.0 copy-start.13
  39.4 0.0 copy-start.14
  39.5 1.4 %collective-permute-done.6.c_ref = f32[8,128]{1,0:T(8,128)S(1)} collective-permute-done((f32[8,128]{1,0:T(8,128)S(1)}, f32[8,128]{1,0:T(8,128)S(1)}, u32[]{:S(2)}, u32[]{:S(2)}) %collective-permute-start.6) | collective-permute-done | bytes 4128 | tf_op jit(solution)/shard_map/ppermute | solution.py:318
  40.8 0.5 shard_map.167
  41.3 0.9 %collective-permute-start.8 = (f32[8,128]{1,0:T(8,128)S(1)}, f32[8,128]{1,0:T(8,128)S(1)}, u32[]{:S(2)}, u32[]{:S(2)}) collective-permute-start(f32[8,128]{1,0:T(8,128)S(1)} %get-tuple-element.54.after_ref), channel_id=1, source_target_pairs={{0,8},{1,9},{2,10},{3,11},{4,12},{5,13},{6,14},{7,15},{8,0},{9,1},... | collective-permute-start | bytes 12296 | tf_op jit(solution)/shard_map/ppermute | solution.py:318
  42.2 1.1 %collective-permute-start.9 = (f32[8,128]{1,0:T(8,128)S(1)}, f32[8,128]{1,0:T(8,128)S(1)}, u32[]{:S(2)}, u32[]{:S(2)}) collective-permute-start(f32[8,128]{1,0:T(8,128)S(1)} %get-tuple-element.54.after_ref), channel_id=1, source_target_pairs={{0,12},{1,13},{2,14},{3,15},{4,8},{5,9},{6,10},{7,11},{8,4},{9,5},... | collective-permute-start | bytes 12296 | tf_op jit(solution)/shard_map/ppermute | solution.py:318
  43.3 2.7 %collective-permute-start.7 = (f32[2,8,128]{2,1,0:T(8,128)S(1)}, f32[2,8,128]{2,1,0:T(8,128)S(1)}, u32[]{:S(2)}, u32[]{:S(2)}) collective-permute-start(f32[2,8,128]{2,1,0:T(8,128)S(1)} %get-tuple-element.53.pair_ref), channel_id=1, source_target_pairs={{0,4},{1,5},{2,6},{3,7},{4,0},{5,1},{6,2},{7,3},{8,12},{9,13},{10,... | collective-permute-start | bytes 24584 | tf_op jit(solution)/shard_map/ppermute | solution.py:318
  46.0 3.8 %shard_map.169 = (f32[512,256]{1,0:T(8,128)S(1)}, bf16[2,64,128]{2,1,0:T(8,128)(2,1)S(1)}, bf16[2,128,128]{2,1,0:T(8,128)(2,1)S(1)}, bf16[2,4,128,256]{3,2,1,0:T(8,128)(2,1)S(1)}, bf16[2,64,256]{2,1,0:T(8,128)(2,1)S(1)}) custom-call(f32[256,128]{1,0:T(8,128)S(1)} %get-tuple-element.61.c0_ref, f32[128,128]{1,0:T(8,128)S(1)} %get-tuple-element.62.c1_ref, ...), custom_call_target="tpu_custom_call" | custom-call | flops 10000000000 | bytes 33554432 | tf_op jit(solution)/shard_map/pallas_call | solution.py:386
  49.9 2.5 %shard_map.170 = bf16[512,256]{1,0:T(8,128)(2,1)} custom-call(f32[8,256]{1,0:T(8,128)S(1)} %get-tuple-element.52.both_ref, f32[2,8,128]{2,1,0:T(8,128)S(1)} %get-tuple-element.53.pair_ref, f32[2,8,128]{2,1,0:T(8,128)S(1)} %collective-permute-done.7.near_ref, f32[8,128]{1,0:T(8,128)S(1)} %collective-permute-done.8.far_ref, ...), custom_call_target="tpu_custom_call" | custom-call | tf_op jit(solution)/shard_map/pallas_call | solution.py:394
  (37 shorter events, 0.1 us)
Async XLA Ops:
  0.0 7.9 %copy-start.1 = (bf16[512,512]{1,0:T(8,128)(2,1)S(1)}, bf16[512,512]{1,0:T(8,128)(2,1)}, u32[]{:S(2)}) copy-start(bf16[512,512]{1,0:T(8,128)(2,1)} %constant.2.clone.table_ref) | copy-start | bytes 1572868
  0.0 7.9 %copy-start = (f32[12,256,128]{2,1,0:T(8,128)S(1)}, f32[12,256,128]{2,1,0:T(8,128)}, u32[]{:S(2)}) copy-start(f32[12,256,128]{2,1,0:T(8,128)} %rest_ref.7) | copy-start | bytes 4718596
  1.1 6.8 %copy-start.3 = (f32[256,64]{0,1:T(8,128)S(1)}, f32[256,64]{0,1:T(8,128)}, u32[]{:S(2)}) copy-start(f32[256,64]{0,1:T(8,128)} %param.21) | copy-start | bytes 196612
  1.1 6.8 %copy-start.4 = (f32[128,128]{1,0:T(8,128)S(1)}, f32[128,128]{1,0:T(8,128)}, u32[]{:S(2)}) copy-start(f32[128,128]{1,0:T(8,128)} %second_ref.1) | copy-start | bytes 196612
  1.1 6.8 %copy-start.5 = (f32[128,64]{0,1:T(8,128)S(1)}, f32[128,64]{0,1:T(8,128)}, u32[]{:S(2)}) copy-start(f32[128,64]{0,1:T(8,128)} %param.23) | copy-start | bytes 98308
  1.1 6.8 %copy-start.6 = (s32[4,8,8]{2,1,0:T(8,128)S(1)}, s32[4,8,8]{2,1,0:T(8,128)}, u32[]{:S(2)}) copy-start(s32[4,8,8]{2,1,0:T(8,128)} %flow_ref.1) | copy-start | bytes 3076
  1.1 6.8 %copy-start.7 = (f32[2,8,8]{2,1,0:T(8,128)S(1)}, f32[2,8,8]{2,1,0:T(8,128)}, u32[]{:S(2)}) copy-start(f32[2,8,8]{2,1,0:T(8,128)} %vel_ref.1) | copy-start | bytes 1540
  1.4 6.5 %collective-permute-start = (bf16[8,8,256]{2,1,0:T(8,128)(2,1)S(1)}, bf16[8,8,256]{2,1,0:T(8,128)(2,1)S(1)}, u32[]{:S(2)}, u32[]{:S(2)}) collective-permute-start(bf16[8,8,256]{2,1,0:T(8,128)(2,1)S(1)} %get-tuple-element.39), channel_id=1, source_target_pairs={{0,16},{16,0},{32,48},{48,32},{64,80},{80,64},{96,112},{112,96},{1... | collective-permute-start | bytes 98312 | tf_op jit(solution)/shard_map/ppermute | solution.py:362
  1.5 7.3 %collective-permute-start.1 = (bf16[8,8,256]{2,1,0:T(8,128)(2,1)S(1)}, bf16[8,8,256]{2,1,0:T(8,128)(2,1)S(1)}, u32[]{:S(2)}, u32[]{:S(2)}) collective-permute-start(bf16[8,8,256]{2,1,0:T(8,128)(2,1)S(1)} %get-tuple-element.43), channel_id=1, source_target_pairs={{16,32},{48,64},{80,96},{112,128},{144,160},{176,192},{208,224},{3... | collective-permute-start | bytes 98312 | tf_op jit(solution)/shard_map/ppermute | solution.py:360
  2.1 6.6 %collective-permute-start.2 = (bf16[8,8,256]{2,1,0:T(8,128)(2,1)S(1)}, bf16[8,8,256]{2,1,0:T(8,128)(2,1)S(1)}, u32[]{:S(2)}, u32[]{:S(2)}) collective-permute-start(bf16[8,8,256]{2,1,0:T(8,128)(2,1)S(1)} %get-tuple-element.44), channel_id=1, source_target_pairs={{0,1},{1,0},{2,3},{3,2},{4,5},{5,4},{6,7},{7,6},{8,9},{9,8},{10,11... | collective-permute-start | bytes 98312 | tf_op jit(solution)/shard_map/ppermute | solution.py:361
  3.8 7.9 %collective-permute-start.3 = (bf16[8,8,256]{2,1,0:T(8,128)(2,1)S(1)}, bf16[8,8,256]{2,1,0:T(8,128)(2,1)S(1)}, u32[]{:S(2)}, u32[]{:S(2)}) collective-permute-start(bf16[8,8,256]{2,1,0:T(8,128)(2,1)S(1)} %get-tuple-element.45), channel_id=1, source_target_pairs={{1,2},{3,4},{5,6},{7,8},{9,10},{11,12},{13,14},{2,1},{4,3},{6,5},{... | collective-permute-start | bytes 98312 | tf_op jit(solution)/shard_map/ppermute | solution.py:359
  11.7 23.4 %copy-start.8 = (f32[12,128,256]{2,1,0:T(8,128)S(1)}, f32[12,128,256]{2,1,0:T(8,128)}, u32[]{:S(2)}) copy-start(f32[12,128,256]{2,1,0:T(8,128)} %prest_ref.3) | copy-start | bytes 4718596
  11.7 23.4 %copy-start.10 = (f32[128,128]{1,0:T(8,128)S(1)}, f32[128,128]{1,0:T(8,128)}, u32[]{:S(2)}) copy-start(f32[128,128]{1,0:T(8,128)} %rootmap_ref.1) | copy-start | bytes 196612
  26.5 13.0 %collective-permute-start.4 = (f32[8,128]{1,0:T(8,128)S(1)}, f32[8,128]{1,0:T(8,128)S(1)}, u32[]{:S(2)}, u32[]{:S(2)}) collective-permute-start(f32[8,128]{1,0:T(8,128)S(1)} %get-tuple-element.51.root_ref), channel_id=1, source_target_pairs={{0,64},{1,65},{2,66},{3,67},{4,68},{5,69},{6,70},{7,71},{8,72},{9,... | collective-permute-start | bytes 12296 | tf_op jit(solution)/shard_map/ppermute | solution.py:318
  30.9 8.5 %collective-permute-start.5 = (f32[8,128]{1,0:T(8,128)S(1)}, f32[8,128]{1,0:T(8,128)S(1)}, u32[]{:S(2)}, u32[]{:S(2)}) collective-permute-start(f32[8,128]{1,0:T(8,128)S(1)} %get-tuple-element.51.root_ref), channel_id=1, source_target_pairs={{0,128},{1,129},{2,130},{3,131},{4,132},{5,133},{6,134},{7,135},{8... | collective-permute-start | bytes 12296 | tf_op jit(solution)/shard_map/ppermute | solution.py:318
  35.1 5.7 %collective-permute-start.6 = (f32[8,128]{1,0:T(8,128)S(1)}, f32[8,128]{1,0:T(8,128)S(1)}, u32[]{:S(2)}, u32[]{:S(2)}) collective-permute-start(f32[8,128]{1,0:T(8,128)S(1)} %get-tuple-element.51.root_ref), channel_id=1, source_target_pairs={{0,192},{1,193},{2,194},{3,195},{4,196},{5,197},{6,198},{7,199},{8... | collective-permute-start | bytes 12296 | tf_op jit(solution)/shard_map/ppermute | solution.py:318
  39.4 6.6 %copy-start.9 = (f32[256,256]{1,0:T(8,128)S(1)}, f32[256,256]{1,0:T(8,128)}, u32[]{:S(2)}) copy-start(f32[256,256]{1,0:T(8,128)} %solve_ref.1) | copy-start | bytes 786436
  39.4 6.6 %copy-start.11 = (f32[128,128]{1,0:T(8,128)S(1)}, f32[128,128]{1,0:T(8,128)}, u32[]{:S(2)}) copy-start(f32[128,128]{1,0:T(8,128)} %psecond_ref.1) | copy-start | bytes 196612
  39.4 6.6 %copy-start.12 = (f32[128,128]{1,0:T(8,128)S(1)}, f32[128,128]{1,0:T(8,128)}, u32[]{:S(2)}) copy-start(f32[128,128]{1,0:T(8,128)} %sfirst_ref.1) | copy-start | bytes 196612
  39.4 6.6 %copy-start.13 = (f32[128,128]{1,0:T(8,128)S(1)}, f32[128,128]{1,0:T(8,128)}, u32[]{:S(2)}) copy-start(f32[128,128]{1,0:T(8,128)} %ssecond_ref.1) | copy-start | bytes 196612
  39.4 6.6 %copy-start.14 = (f32[64,256]{1,0:T(8,128)S(1)}, f32[64,256]{1,0:T(8,128)}, u32[]{:S(2)}) copy-start(f32[64,256]{1,0:T(8,128)} %lift_ref.1) | copy-start | bytes 196612
  41.3 8.5 %collective-permute-start.8 = (f32[8,128]{1,0:T(8,128)S(1)}, f32[8,128]{1,0:T(8,128)S(1)}, u32[]{:S(2)}, u32[]{:S(2)}) collective-permute-start(f32[8,128]{1,0:T(8,128)S(1)} %get-tuple-element.54.after_ref), channel_id=1, source_target_pairs={{0,8},{1,9},{2,10},{3,11},{4,12},{5,13},{6,14},{7,15},{8,0},{9,1},... | collective-permute-start | bytes 12296 | tf_op jit(solution)/shard_map/ppermute | solution.py:318
  42.2 7.7 %collective-permute-start.9 = (f32[8,128]{1,0:T(8,128)S(1)}, f32[8,128]{1,0:T(8,128)S(1)}, u32[]{:S(2)}, u32[]{:S(2)}) collective-permute-start(f32[8,128]{1,0:T(8,128)S(1)} %get-tuple-element.54.after_ref), channel_id=1, source_target_pairs={{0,12},{1,13},{2,14},{3,15},{4,8},{5,9},{6,10},{7,11},{8,4},{9,5},... | collective-permute-start | bytes 12296 | tf_op jit(solution)/shard_map/ppermute | solution.py:318
  43.3 6.5 %collective-permute-start.7 = (f32[2,8,128]{2,1,0:T(8,128)S(1)}, f32[2,8,128]{2,1,0:T(8,128)S(1)}, u32[]{:S(2)}, u32[]{:S(2)}) collective-permute-start(f32[2,8,128]{2,1,0:T(8,128)S(1)} %get-tuple-element.53.pair_ref), channel_id=1, source_target_pairs={{0,4},{1,5},{2,6},{3,7},{4,0},{5,1},{6,2},{7,3},{8,12},{9,13},{10,... | collective-permute-start | bytes 24584 | tf_op jit(solution)/shard_map/ppermute | solution.py:318
  (2 other events, 7.7 us)

commit v4 on v3

--- a/solution.py
+++ b/solution.py
@@ -77,7 +77,7 @@
 LOCAL = ((4, 64), (16, 8), (2, 32), (4, 8), (1, 16), (1, 8))
 
 
-def pack_kernel(u_ref, xa_ref, xb_ref, ya_ref, yb_ref):
+def pack_kernel(u_ref, yb_ref, xb_ref, ya_ref, xa_ref):
     even_x = lax.axis_index("gx") % 2 == 0
     even_y = lax.axis_index("gy") % 2 == 0
     u = u_ref[...].astype(F32)
@@ -153,7 +153,7 @@
         rest_out[0, k], rest_out[1, k] = split(rest_ref[k])
 
 
-def up_kernel(base_ref, stri_ref, strj_ref, xb_ref, ya_ref, yb_ref, skel_ref, first_ref, second_ref, rest_ref,
+def up_kernel(base_ref, stri_ref, strj_ref, yb_ref, xb_ref, ya_ref, skel_ref, first_ref, second_ref, rest_ref,
               forcing_ref, c0_ref, c1_ref, c2_ref, c3_ref, c4_ref, c5_ref, root_ref, turn_ref):
     even_x = lax.axis_index("gx") % 2 == 0
     even_y = lax.axis_index("gy") % 2 == 0
@@ -225,9 +225,13 @@
 
     levels = (s0_ref, s1_ref, s2_ref, s3_ref)
     known = jnp.zeros((8, 128), F32)
-    chain = [None, mine(prest_ref, 0)]
-    for k in range(1, 8):
-        chain.append(mm(mine(prest_ref, k), chain[k]))
+    step = [mine(prest_ref, k) for k in range(8)]
+    twice = [mm(step[k + 1], step[k]) for k in (2, 4, 6)]
+    chain = [None, step[0], mm(step[1], step[0])]
+    for k in (2, 4):
+        chain.append(mm(step[k], chain[k]))
+        chain.append(mm(twice[k // 2 - 1], chain[k]))
+    chain.append(mm(step[6], chain[6]))
     for k in range(4):
         pair = jnp.int32(0)
         for q in range(3, k, -1):
@@ -237,7 +241,7 @@
         term = mm(both, mine(srest_ref, k))
         known = known + (term if k == 0 else mm(term, chain[k]))
     known_ref[...] = known
-    above = mm(rootmap_ref[...], chain[8])
+    above = mm(mm(rootmap_ref[...], twice[2]), chain[6])
     plan = [None] * 6
     for k in (7, 6, 5):
         full = mm(rest_ref[k + 4], above) + mm(mine(srest_ref, k), chain[k])
@@ -249,7 +253,7 @@
         plan_ref[0, k], plan_ref[1, k] = split(plan[k])
 
 
-def z_kernel(root_ref, a_ref, b_ref, c_ref, rest_ref, both_ref, pair_ref, last_ref):
+def z_kernel(root_ref, b_ref, c_ref, a_ref, rest_ref, both_ref, pair_ref, last_ref):
     bit = path_bits()
     both = ordered(bit[4], root_ref[...], a_ref[...])
     both_ref[...] = both
@@ -264,37 +268,31 @@
 
 def known_kernel(c0_ref, c1_ref, c2_ref, c3_ref, c4_ref, c5_ref, forcing_ref, pfirst_ref, psecond_ref, prest_ref,
                  sfirst_ref, ssecond_ref, srest_ref, solve_ref, lift_ref, after_ref,
-                 part_ref, pfirst_out, psecond_out, prest_out, lift_out, turn_ref):
+                 part_ref, t0_ref, t1_ref, t2_ref, t3_ref, t4_ref, t5_ref, pfirst_out, psecond_out, prest_out, lift_out):
     pfirst_out[0], pfirst_out[1] = split(pfirst_ref[...])
     psecond_out[0], psecond_out[1] = split(psecond_ref[...])
     for k in range(4):
         prest_out[0, k], prest_out[1, k] = split(prest_ref[k])
     lift_out[0], lift_out[1] = split(lift_ref[...])
-    downs = [pfirst_out, psecond_out] + [prest_out.at[:, k] for k in range(4)]
     saved = (c0_ref, c1_ref, c2_ref, c3_ref, c4_ref, c5_ref)
-    boundary = None
-    for k in range(5, -1, -1):
+    terms = (t0_ref, t1_ref, t2_ref, t3_ref, t4_ref, t5_ref)
+    for k in range(6):
         across = sfirst_ref[...] if k == 0 else ssecond_ref[...] if k == 1 else srest_ref[k - 2]
-        joined = mm(saved[k][...], across)
-        if boundary is not None:
-            joined = joined + mm(boundary, (downs[k][0], downs[k][1]))
-        boundary = pair_down(joined, *LOCAL[k])
-    wide = jnp.concatenate([boundary, jnp.zeros_like(boundary)], axis=1)
-    for q in range(64):
-        turn_ref[pl.ds(q, 8, stride=64), :] = wide[8 * q : 8 * q + 8]
-    part_ref[...] = mm(forcing_ref[...], solve_ref[...]) + mm(turn_ref[:, :64], (lift_out[0], lift_out[1]))
-
-
-def last_kernel(both_ref, pair_ref, near_ref, far_ref, farther_ref, plan_ref, known_ref,
-                part_ref, pfirst_ref, psecond_ref, prest_ref, lift_ref, out_ref, turn_ref):
+        terms[k][...] = mm(saved[k][...], across)
+    part_ref[...] = mm(forcing_ref[...], solve_ref[...])
+
+
+def last_kernel(both_ref, pair_ref, near_ref, far_ref, farther_ref, plan_ref, known_ref, part_ref,
+                t0_ref, t1_ref, t2_ref, t3_ref, t4_ref, t5_ref,
+                pfirst_ref, psecond_ref, prest_ref, lift_ref, out_ref, turn_ref):
     sources = [both_ref[...], pair_ref[0], near_ref[0], pair_ref[1] + near_ref[1], far_ref[...] + farther_ref[...]]
     gathered = jnp.concatenate(sources, axis=1)
     plan = plan_ref[...].reshape(2, 768, 128)
     boundary = known_ref[...] + mm(gathered, (plan[0], plan[1]))
-    for k in range(5, 1, -1):
-        boundary = pair_down(mm(boundary, (prest_ref[0, k - 2], prest_ref[1, k - 2])), *LOCAL[k])
-    boundary = pair_down(mm(boundary, (psecond_ref[0], psecond_ref[1])), *LOCAL[1])
-    boundary = pair_down(mm(boundary, (pfirst_ref[0], pfirst_ref[1])), *LOCAL[0])
+    terms = (t0_ref, t1_ref, t2_ref, t3_ref, t4_ref, t5_ref)
+    downs = [pfirst_ref, psecond_ref] + [prest_ref.at[:, k] for k in range(4)]
+    for k in range(5, -1, -1):
+        boundary = pair_down(terms[k][...] + mm(boundary, (downs[k][0], downs[k][1])), *LOCAL[k])
     wide = jnp.concatenate([boundary, jnp.zeros_like(boundary)], axis=1)
     for q in range(64):
         turn_ref[pl.ds(q, 8, stride=64), :] = wide[8 * q : 8 * q + 8]
@@ -355,11 +353,11 @@
     beside = [(i, i ^ 1) for i in range(16)]
     across = [(i, i + 1) for i in range(1, 15, 2)] + [(i + 1, i) for i in range(1, 15, 2)]
     edge = shape(8, SIDE, 256, dtype=BF)
-    xa, xb, ya, yb = call(pack_kernel, [edge] * 4, cost=WORK)(tracers)
+    yb, xb, ya, xa = call(pack_kernel, [edge] * 4, cost=WORK)(tracers)
+    xa = lax.ppermute(xa, "gx", beside)
+    ya = lax.ppermute(ya, "gy", beside)
+    xb = lax.ppermute(xb, "gx", across)
     yb = lax.ppermute(yb, "gy", across)
-    xb = lax.ppermute(xb, "gx", across)
-    ya = lax.ppermute(ya, "gy", beside)
-    xa = lax.ppermute(xa, "gx", beside)
     table = jnp.asarray(derivative_pieces())
     base, str_i, str_j, skel, first, second, rest = call(
         base_kernel,
@@ -371,28 +369,28 @@
         [shape(512, 256), shape(256, 128), shape(128, 128), shape(64, 256), shape(32, 256), shape(16, 256),
          shape(8, 256), shape(16, 8, 128)],
         [pltpu.VMEM((512, 128), F32)],
-    )(base, str_i, str_j, xb, ya, yb, skel, first, second, rest)
+    )(base, str_i, str_j, yb, xb, ya, skel, first, second, rest)
     got = swap_roots(roots, BITS[:4])
     s0, s1, s2, s3, root = call(
         mid_kernel,
         [shape(128, 128), shape(64, 128), shape(32, 128), shape(16, 128), shape(8, 128)],
     )(got, merge_rest)
-    third, second_z, first_z = swap(root, 192), swap(root, 128), swap(root, 64)
+    first_z, third, second_z = swap(root, 64), swap(root, 192), swap(root, 128)
     plan, known = call(plan_kernel, [shape(2, 6, 128, 128, dtype=BF), shape(8, 128)], cost=WORK)(
         s0, s1, s2, s3, merge_rest, parent_rest, sibling_rest, root_map)
     both, pair, last = call(z_kernel, [shape(8, 256), shape(2, 8, 128), shape(8, 128)])(
-        root, first_z, second_z, third, merge_rest)
+        root, second_z, third, first_z, merge_rest)
     farther, far, near = swap(last, 12), swap(last, 8), swap(pair, 4)
-    part, pfirst, psecond, prest, lift = call(
+    part, *rest_of = call(
         known_kernel,
-        [shape(512, 256), shape(2, 64, 128, dtype=BF), shape(2, 128, 128, dtype=BF), shape(2, 4, 128, 256, dtype=BF),
+        [shape(512, 256), shape(256, 128), shape(128, 128), shape(64, 256), shape(32, 256), shape(16, 256), shape(8, 256),
+         shape(2, 64, 128, dtype=BF), shape(2, 128, 128, dtype=BF), shape(2, 4, 128, 256, dtype=BF),
          shape(2, 64, 256, dtype=BF)],
-        [pltpu.VMEM((512, 128), F32)],
         cost=WORK,
     )(c0, c1, c2, c3, c4, c5, forcing, parent_first, parent_second, parent_rest, sibling_first, sibling_second,
       sibling_rest, leaf_solve, leaf_lift, last)
     out = call(last_kernel, shape(512, 256, dtype=BF), [pltpu.VMEM((512, 128), F32)])(
-        both, pair, near, far, farther, plan, known, part, pfirst, psecond, prest, lift)
+        both, pair, near, far, farther, plan, known, part, *rest_of)
     return out.reshape(tracers.shape)
 
 

time: 52.6 us -> 48.3 us (0.918)
  Pallas kernels: 14.3 us -> 13 us
  starting transfers between devices: 19.8 us -> 18.7 us
  waiting for transfers between devices: 4.35 us -> 3.31 us
  blocking collectives: 12.4 us -> 11.6 us
    ppermute x1, waiting for transfers between devices: 2.95 us -> 1.24 us  [local(): yb = lax.ppermute(yb, 'gy', across)]
    ppermute x1, waiting for transfers between devices: 0.01 us -> 1.65 us  [local(): ya = lax.ppermute(ya, 'gy', beside)]
    ppermute x1, starting transfers between devices: 1.66 us -> 0.25 us  [local(): ya = lax.ppermute(ya, 'gy', beside)]
    pallas_call x2, Pallas kernels: 4.01 us -> 2.91 us  [the longest x1 2.68 us: local(): call(known_kernel, [shape(512, 256), shape(256, 128), shape(128, 128), sh...]
    ppermute x6, waiting for transfers between devices: 1.39 us -> 0.41 us  [swap(): return lax.ppermute(value, BOTH, [(i, i ^ mask) for i in range(256)])]
    ppermute x1, starting transfers between devices: 4.05 us -> 4.89 us  [local(): yb = lax.ppermute(yb, 'gy', across)]
    all_to_all x1, blocking collectives: 12.4 us -> 11.6 us  [swap_roots(): return lax.all_to_all(copies, BOTH, 0, 0, axis_index_groups=groups_of(bits))]
    ppermute x6, starting transfers between devices: 13.4 us -> 12.8 us  [swap(): return lax.ppermute(value, BOTH, [(i, i ^ mask) for i in range(256)])]
  transfers between devices with their start and end apart: 10 -> 10, of which waited for: 2 -> 4; matrix products, arithmetic and copies ran while one was open for 0% -> 0% of each run, Pallas kernels for 17% -> 15%
where the time goes in v4:
time: 48.3 us; the launch traced here: 48 us
  starting transfers between devices  18.7 us (39%)
  Pallas kernels  13 us (27%)
  blocking collectives  11.6 us (24%)
  waiting for transfers between devices  3.31 us (7%)
  local copies, waits for them, and re-layouts  1.17 us (2%)
    ppermute x6, starting transfers between devices, swap(): return lax.ppermute(value, BOTH, [(i, i ^ mask) for i in range(256)])  12.8 us
    all_to_all x1, blocking collectives, swap_roots(): return lax.all_to_all(copies, BOTH, 0, 0, axis_index_groups=groups_of(bits))  11.6 us
    ppermute x1, starting transfers between devices, local(): yb = lax.ppermute(yb, 'gy', across)  4.89 us
    pallas_call x1, Pallas kernels, local(): call(plan_kernel, [shape(2, 6, 128, 128, dtype=BF), shape(8, 128)], cost=...  3.97 us
    pallas_call x1, Pallas kernels, local(): call(known_kernel, [shape(512, 256), shape(256, 128), shape(128, 128), sh...  2.68 us
    pallas_call x1, Pallas kernels, local(): call(last_kernel, shape(512, 256, dtype=BF), [pltpu.VMEM((512, 128), F32)])  2.49 us
    pallas_call x1, Pallas kernels, local(): call(up_kernel, [shape(512, 256), shape(256, 128), shape(128, 128), shape...  1.82 us
    ppermute x1, waiting for transfers between devices, local(): ya = lax.ppermute(ya, 'gy', beside)  1.65 us
  transfers between devices with their start and end apart: 10, of which 4 were waited for; matrix products, arithmetic and copies ran while one was open for 0% of the time, Pallas kernels for 15%

profile of v4, /device:TPU:2, one launch (start us, length us, event | category | flops | bytes accessed | tf_op | source)
XLA Modules:
  0.0 48.0 jit_solution(15334429711783058516)
XLA Ops:
  0.0 1.1 %copy-done.2 = bf16[8,8,8,256]{3,2,1,0:T(8,128)(2,1)S(1)} copy-done((bf16[8,8,8,256]{3,2,1,0:T(8,128)(2,1)S(1)}, bf16[8,8,8,256]{3,2,1,0:T(8,128)(2,1)}, u32[]{:S(2)}) %copy-start.2) | copy-done | bytes 262168
  1.1 0.2 shard_map.163
  1.4 0.1 collective-permute-start
  1.5 4.9 %collective-permute-start.1 = (bf16[8,8,256]{2,1,0:T(8,128)(2,1)S(1)}, bf16[8,8,256]{2,1,0:T(8,128)(2,1)S(1)}, u32[]{:S(2)}, u32[]{:S(2)}) collective-permute-start(bf16[8,8,256]{2,1,0:T(8,128)(2,1)S(1)} %get-tuple-element.49), channel_id=1, source_target_pairs={{1,2},{3,4},{5,6},{7,8},{9,10},{11,12},{13,14},{2,1},{4,3},{6,5},{... | collective-permute-start | bytes 98312 | tf_op jit(solution)/shard_map/ppermute | solution.py:360
  6.4 0.7 %collective-permute-start.2 = (bf16[8,8,256]{2,1,0:T(8,128)(2,1)S(1)}, bf16[8,8,256]{2,1,0:T(8,128)(2,1)S(1)}, u32[]{:S(2)}, u32[]{:S(2)}) collective-permute-start(bf16[8,8,256]{2,1,0:T(8,128)(2,1)S(1)} %get-tuple-element.50), channel_id=1, source_target_pairs={{16,32},{48,64},{80,96},{112,128},{144,160},{176,192},{208,224},{3... | collective-permute-start | bytes 98312 | tf_op jit(solution)/shard_map/ppermute | solution.py:359
  7.0 0.3 collective-permute-start.3
  7.4 0.8 %shard_map.164 = (f32[512,256]{1,0:T(8,128)S(1)}, f32[64,256]{1,0:T(8,128)S(1)}, f32[64,256]{1,0:T(8,128)S(1)}, bf16[2,128,256]{2,1,0:T(8,128)(2,1)S(1)}, bf16[2...) custom-call(bf16[512,256]{1,0:T(8,128)(2,1)S(1)} %bitcast.4, ...), custom_call_target="tpu_custom_call" | custom-call | tf_op jit(solution)/shard_map/pallas_call | solution.py:362
  8.1 1.2 %collective-permute-done.1.yb_ref = bf16[8,8,256]{2,1,0:T(8,128)(2,1)S(1)} collective-permute-done((bf16[8,8,256]{2,1,0:T(8,128)(2,1)S(1)}, bf16[8,8,256]{2,1,0:T(8,128)(2,1)S(1)}, u32[]{:S(2)}, u32[]{:S(2)}) %collective-permute-start.1) | collective-permute-done | bytes 32800 | tf_op jit(solution)/shard_map/ppermute | solution.py:360
  9.4 1.7 %collective-permute-done.3.ya_ref = bf16[8,8,256]{2,1,0:T(8,128)(2,1)S(1)} collective-permute-done((bf16[8,8,256]{2,1,0:T(8,128)(2,1)S(1)}, bf16[8,8,256]{2,1,0:T(8,128)(2,1)S(1)}, u32[]{:S(2)}, u32[]{:S(2)}) %collective-permute-start.3) | collective-permute-done | bytes 32800 | tf_op jit(solution)/shard_map/ppermute | solution.py:358
  11.0 1.8 %shard_map.165 = (f32[512,256]{1,0:T(8,128)S(1)}, f32[256,128]{1,0:T(8,128)S(1)}, f32[128,128]{1,0:T(8,128)S(1)}, f32[64,256]{1,0:T(8,128)S(1)}, f32[32,256]{1,0...) custom-call(f32[512,256]{1,0:T(8,128)S(1)} %get-tuple-element.46.base_ref, ...), custom_call_target="tpu_custom_call" | custom-call | tf_op jit(solution)/shard_map/pallas_call | solution.py:367
  12.9 11.6 %all_to_all.5.got_ref = f32[16,8,128]{2,1,0:T(8,128)S(1)} all-to-all(f32[16,8,128]{2,1,0:T(8,128)S(1)} %get-tuple-element.56), channel_id=1, replica_groups={{0,16,1,17,32,48,33,49,2,18,3,19,34,50,35,51},{4,20,5,21,36,52,37,53,6,..., dimensions={0} | all-to-all | bytes 131072 | tf_op jit(solution)/shard_map/all_to_all | solution.py:312
  24.5 0.6 %shard_map.166 = (f32[128,128]{1,0:T(8,128)S(1)}, f32[64,128]{1,0:T(8,128)S(1)}, f32[32,128]{1,0:T(8,128)S(1)}, f32[16,128]{1,0:T(8,128)S(1)}, f32[8,128]{1,0:T(8,128)S(1)}) custom-call(f32[16,8,128]{2,1,0:T(8,128)S(1)} %all_to_all.5.got_ref, f32[12,256,128]{2,1,0:T(8,128)S(1)} %copy-done), custom_call_target="tpu_custom_call" | custom-call | tf_op jit(solution)/shard_map/pallas_call | solution.py:374
  25.1 6.6 %collective-permute-start.4 = (f32[8,128]{1,0:T(8,128)S(1)}, f32[8,128]{1,0:T(8,128)S(1)}, u32[]{:S(2)}, u32[]{:S(2)}) collective-permute-start(f32[8,128]{1,0:T(8,128)S(1)} %get-tuple-element.57.root_ref), channel_id=1, source_target_pairs={{0,128},{1,129},{2,130},{3,131},{4,132},{5,133},{6,134},{7,135},{8... | collective-permute-start | bytes 12296 | tf_op jit(solution)/shard_map/ppermute | solution.py:316
  31.7 1.4 %collective-permute-start.5 = (f32[8,128]{1,0:T(8,128)S(1)}, f32[8,128]{1,0:T(8,128)S(1)}, u32[]{:S(2)}, u32[]{:S(2)}) collective-permute-start(f32[8,128]{1,0:T(8,128)S(1)} %get-tuple-element.57.root_ref), channel_id=1, source_target_pairs={{0,192},{1,193},{2,194},{3,195},{4,196},{5,197},{6,198},{7,199},{8... | collective-permute-start | bytes 12296 | tf_op jit(solution)/shard_map/ppermute | solution.py:316
  33.1 0.0 collective-permute-start.6
  33.2 4.0 %shard_map.168 = (bf16[2,6,128,128]{3,2,1,0:T(8,128)(2,1)S(1)}, f32[8,128]{1,0:T(8,128)S(1)}) custom-call(f32[128,128]{1,0:T(8,128)S(1)} %get-tuple-element.61.s0_ref, f32[64,128]{1,0:T(8,128)S(1)} %get-tuple-element.62.s1_ref, f32[32,128]{1,0:T(8,128)S(1)} %get-tuple-element.63.s2_ref, f32[16,128]{1,0:T(8,128)S(1)} %get-tuple-element.64.s3_ref, ...), custom_call_target="tpu_custom_call" | custom-call | flops 10000000000 | bytes 33554432 | tf_op jit(solution)/shard_map/pallas_call | solution.py:379
  37.2 0.2 collective-permute-done.5.c_ref
  37.4 0.2 collective-permute-done.6.a_ref
  37.6 0.5 shard_map.167
  38.1 1.8 %collective-permute-start.8 = (f32[8,128]{1,0:T(8,128)S(1)}, f32[8,128]{1,0:T(8,128)S(1)}, u32[]{:S(2)}, u32[]{:S(2)}) collective-permute-start(f32[8,128]{1,0:T(8,128)S(1)} %get-tuple-element.60.after_ref), channel_id=1, source_target_pairs={{0,8},{1,9},{2,10},{3,11},{4,12},{5,13},{6,14},{7,15},{8,0},{9,1},... | collective-permute-start | bytes 12296 | tf_op jit(solution)/shard_map/ppermute | solution.py:316
  39.9 0.2 collective-permute-start.9
  40.1 2.7 %collective-permute-start.7 = (f32[2,8,128]{2,1,0:T(8,128)S(1)}, f32[2,8,128]{2,1,0:T(8,128)S(1)}, u32[]{:S(2)}, u32[]{:S(2)}) collective-permute-start(f32[2,8,128]{2,1,0:T(8,128)S(1)} %get-tuple-element.59.pair_ref), channel_id=1, source_target_pairs={{0,4},{1,5},{2,6},{3,7},{4,0},{5,1},{6,2},{7,3},{8,12},{9,13},{10,... | collective-permute-start | bytes 24584 | tf_op jit(solution)/shard_map/ppermute | solution.py:316
  42.8 2.7 %shard_map.169 = (f32[512,256]{1,0:T(8,128)S(1)}, f32[256,128]{1,0:T(8,128)S(1)}, f32[128,128]{1,0:T(8,128)S(1)}, f32[64,256]{1,0:T(8,128)S(1)}, f32[32,256]{1,0...) custom-call(f32[256,128]{1,0:T(8,128)S(1)} %get-tuple-element.67.c0_, ...), custom_call_target="tpu_custom_call" | custom-call | flops 10000000000 | bytes 33554432 | tf_op jit(solution)/shard_map/pallas_call | solution.py:384
  45.6 2.5 %shard_map.170 = bf16[512,256]{1,0:T(8,128)(2,1)} custom-call(f32[8,256]{1,0:T(8,128)S(1)} %get-tuple-element.58.both_ref, f32[2,8,128]{2,1,0:T(8,128)S(1)} %get-tuple-element.59.pair_ref, f32[2,8,128]{2,1,0:T(8,128)S(1)} %collective-permute-done.7.near_ref, f32[8,128]{1,0:T(8,128)S(1)} %collective-permute-done.8.far_ref, ...), custom_call_target="tpu_custom_call" | custom-call | tf_op jit(solution)/shard_map/pallas_call | solution.py:392
  (37 shorter events, 0.1 us)
Async XLA Ops:
  0.0 7.3 %copy-start.1 = (bf16[512,512]{1,0:T(8,128)(2,1)S(1)}, bf16[512,512]{1,0:T(8,128)(2,1)}, u32[]{:S(2)}) copy-start(bf16[512,512]{1,0:T(8,128)(2,1)} %constant.2.clone.table_ref) | copy-start | bytes 1572868
  0.0 7.3 %copy-start = (f32[12,256,128]{2,1,0:T(8,128)S(1)}, f32[12,256,128]{2,1,0:T(8,128)}, u32[]{:S(2)}) copy-start(f32[12,256,128]{2,1,0:T(8,128)} %rest_ref.7) | copy-start | bytes 4718596
  1.1 6.2 %copy-start.3 = (f32[256,64]{0,1:T(8,128)S(1)}, f32[256,64]{0,1:T(8,128)}, u32[]{:S(2)}) copy-start(f32[256,64]{0,1:T(8,128)} %param.21) | copy-start | bytes 196612
  1.1 6.2 %copy-start.4 = (f32[128,128]{1,0:T(8,128)S(1)}, f32[128,128]{1,0:T(8,128)}, u32[]{:S(2)}) copy-start(f32[128,128]{1,0:T(8,128)} %second_ref.1) | copy-start | bytes 196612
  1.1 6.2 %copy-start.5 = (f32[128,64]{0,1:T(8,128)S(1)}, f32[128,64]{0,1:T(8,128)}, u32[]{:S(2)}) copy-start(f32[128,64]{0,1:T(8,128)} %param.23) | copy-start | bytes 98308
  1.1 6.2 %copy-start.6 = (s32[4,8,8]{2,1,0:T(8,128)S(1)}, s32[4,8,8]{2,1,0:T(8,128)}, u32[]{:S(2)}) copy-start(s32[4,8,8]{2,1,0:T(8,128)} %flow_ref.1) | copy-start | bytes 3076
  1.1 6.2 %copy-start.7 = (f32[2,8,8]{2,1,0:T(8,128)S(1)}, f32[2,8,8]{2,1,0:T(8,128)}, u32[]{:S(2)}) copy-start(f32[2,8,8]{2,1,0:T(8,128)} %vel_ref.1) | copy-start | bytes 1540
  1.4 5.9 %collective-permute-start = (bf16[8,8,256]{2,1,0:T(8,128)(2,1)S(1)}, bf16[8,8,256]{2,1,0:T(8,128)(2,1)S(1)}, u32[]{:S(2)}, u32[]{:S(2)}) collective-permute-start(bf16[8,8,256]{2,1,0:T(8,128)(2,1)S(1)} %get-tuple-element.45), channel_id=1, source_target_pairs={{0,16},{16,0},{32,48},{48,32},{64,80},{80,64},{96,112},{112,96},{1... | collective-permute-start | bytes 98312 | tf_op jit(solution)/shard_map/ppermute | solution.py:357
  1.5 7.9 %collective-permute-start.1 = (bf16[8,8,256]{2,1,0:T(8,128)(2,1)S(1)}, bf16[8,8,256]{2,1,0:T(8,128)(2,1)S(1)}, u32[]{:S(2)}, u32[]{:S(2)}) collective-permute-start(bf16[8,8,256]{2,1,0:T(8,128)(2,1)S(1)} %get-tuple-element.49), channel_id=1, source_target_pairs={{1,2},{3,4},{5,6},{7,8},{9,10},{11,12},{13,14},{2,1},{4,3},{6,5},{... | collective-permute-start | bytes 98312 | tf_op jit(solution)/shard_map/ppermute | solution.py:360
  6.4 3.0 %collective-permute-start.2 = (bf16[8,8,256]{2,1,0:T(8,128)(2,1)S(1)}, bf16[8,8,256]{2,1,0:T(8,128)(2,1)S(1)}, u32[]{:S(2)}, u32[]{:S(2)}) collective-permute-start(bf16[8,8,256]{2,1,0:T(8,128)(2,1)S(1)} %get-tuple-element.50), channel_id=1, source_target_pairs={{16,32},{48,64},{80,96},{112,128},{144,160},{176,192},{208,224},{3... | collective-permute-start | bytes 98312 | tf_op jit(solution)/shard_map/ppermute | solution.py:359
  7.0 4.0 %collective-permute-start.3 = (bf16[8,8,256]{2,1,0:T(8,128)(2,1)S(1)}, bf16[8,8,256]{2,1,0:T(8,128)(2,1)S(1)}, u32[]{:S(2)}, u32[]{:S(2)}) collective-permute-start(bf16[8,8,256]{2,1,0:T(8,128)(2,1)S(1)} %get-tuple-element.51), channel_id=1, source_target_pairs={{0,1},{1,0},{2,3},{3,2},{4,5},{5,4},{6,7},{7,6},{8,9},{9,8},{10,11... | collective-permute-start | bytes 98312 | tf_op jit(solution)/shard_map/ppermute | solution.py:358
  11.0 22.1 %copy-start.8 = (f32[12,128,256]{2,1,0:T(8,128)S(1)}, f32[12,128,256]{2,1,0:T(8,128)}, u32[]{:S(2)}) copy-start(f32[12,128,256]{2,1,0:T(8,128)} %prest_ref.3) | copy-start | bytes 4718596
  11.0 22.1 %copy-start.10 = (f32[128,128]{1,0:T(8,128)S(1)}, f32[128,128]{1,0:T(8,128)}, u32[]{:S(2)}) copy-start(f32[128,128]{1,0:T(8,128)} %rootmap_ref.1) | copy-start | bytes 196612
  25.1 12.2 %collective-permute-start.4 = (f32[8,128]{1,0:T(8,128)S(1)}, f32[8,128]{1,0:T(8,128)S(1)}, u32[]{:S(2)}, u32[]{:S(2)}) collective-permute-start(f32[8,128]{1,0:T(8,128)S(1)} %get-tuple-element.57.root_ref), channel_id=1, source_target_pairs={{0,128},{1,129},{2,130},{3,131},{4,132},{5,133},{6,134},{7,135},{8... | collective-permute-start | bytes 12296 | tf_op jit(solution)/shard_map/ppermute | solution.py:316
  31.7 5.7 %collective-permute-start.5 = (f32[8,128]{1,0:T(8,128)S(1)}, f32[8,128]{1,0:T(8,128)S(1)}, u32[]{:S(2)}, u32[]{:S(2)}) collective-permute-start(f32[8,128]{1,0:T(8,128)S(1)} %get-tuple-element.57.root_ref), channel_id=1, source_target_pairs={{0,192},{1,193},{2,194},{3,195},{4,196},{5,197},{6,198},{7,199},{8... | collective-permute-start | bytes 12296 | tf_op jit(solution)/shard_map/ppermute | solution.py:316
  33.1 4.5 %collective-permute-start.6 = (f32[8,128]{1,0:T(8,128)S(1)}, f32[8,128]{1,0:T(8,128)S(1)}, u32[]{:S(2)}, u32[]{:S(2)}) collective-permute-start(f32[8,128]{1,0:T(8,128)S(1)} %get-tuple-element.57.root_ref), channel_id=1, source_target_pairs={{0,64},{1,65},{2,66},{3,67},{4,68},{5,69},{6,70},{7,71},{8,72},{9,... | collective-permute-start | bytes 12296 | tf_op jit(solution)/shard_map/ppermute | solution.py:316
  37.1 5.7 %copy-start.9 = (f32[256,256]{1,0:T(8,128)S(1)}, f32[256,256]{1,0:T(8,128)}, u32[]{:S(2)}) copy-start(f32[256,256]{1,0:T(8,128)} %solve_ref.1) | copy-start | bytes 786436
  37.2 5.6 %copy-start.11 = (f32[128,128]{1,0:T(8,128)S(1)}, f32[128,128]{1,0:T(8,128)}, u32[]{:S(2)}) copy-start(f32[128,128]{1,0:T(8,128)} %psecond_ref.1) | copy-start | bytes 196612
  37.2 5.6 %copy-start.12 = (f32[128,128]{1,0:T(8,128)S(1)}, f32[128,128]{1,0:T(8,128)}, u32[]{:S(2)}) copy-start(f32[128,128]{1,0:T(8,128)} %sfirst_ref.1) | copy-start | bytes 196612
  37.2 5.6 %copy-start.13 = (f32[128,128]{1,0:T(8,128)S(1)}, f32[128,128]{1,0:T(8,128)}, u32[]{:S(2)}) copy-start(f32[128,128]{1,0:T(8,128)} %ssecond_ref.1) | copy-start | bytes 196612
  37.2 5.6 %copy-start.14 = (f32[64,256]{1,0:T(8,128)S(1)}, f32[64,256]{1,0:T(8,128)}, u32[]{:S(2)}) copy-start(f32[64,256]{1,0:T(8,128)} %lift_ref.1) | copy-start | bytes 196612
  38.1 7.4 %collective-permute-start.8 = (f32[8,128]{1,0:T(8,128)S(1)}, f32[8,128]{1,0:T(8,128)S(1)}, u32[]{:S(2)}, u32[]{:S(2)}) collective-permute-start(f32[8,128]{1,0:T(8,128)S(1)} %get-tuple-element.60.after_ref), channel_id=1, source_target_pairs={{0,8},{1,9},{2,10},{3,11},{4,12},{5,13},{6,14},{7,15},{8,0},{9,1},... | collective-permute-start | bytes 12296 | tf_op jit(solution)/shard_map/ppermute | solution.py:316
  39.9 5.6 %collective-permute-start.9 = (f32[8,128]{1,0:T(8,128)S(1)}, f32[8,128]{1,0:T(8,128)S(1)}, u32[]{:S(2)}, u32[]{:S(2)}) collective-permute-start(f32[8,128]{1,0:T(8,128)S(1)} %get-tuple-element.60.after_ref), channel_id=1, source_target_pairs={{0,12},{1,13},{2,14},{3,15},{4,8},{5,9},{6,10},{7,11},{8,4},{9,5},... | collective-permute-start | bytes 12296 | tf_op jit(solution)/shard_map/ppermute | solution.py:316
  40.1 5.4 %collective-permute-start.7 = (f32[2,8,128]{2,1,0:T(8,128)S(1)}, f32[2,8,128]{2,1,0:T(8,128)S(1)}, u32[]{:S(2)}, u32[]{:S(2)}) collective-permute-start(f32[2,8,128]{2,1,0:T(8,128)S(1)} %get-tuple-element.59.pair_ref), channel_id=1, source_target_pairs={{0,4},{1,5},{2,6},{3,7},{4,0},{5,1},{6,2},{7,3},{8,12},{9,13},{10,... | collective-permute-start | bytes 24584 | tf_op jit(solution)/shard_map/ppermute | solution.py:316
  (2 other events, 6.7 us)

commit v5 on v4

--- a/solution.py
+++ b/solution.py
@@ -15,7 +15,7 @@
 BF = jnp.bfloat16
 F32 = jnp.float32
 BITS = (16, 1, 32, 2, 64, 4, 128, 8)
-PARAMS = pltpu.CompilerParams(vmem_limit_bytes=48 * 1024 * 1024)
+PARAMS = pltpu.CompilerParams(vmem_limit_bytes=32 * 1024 * 1024)
 WORK = pl.CostEstimate(flops=10**10, transcendentals=0, bytes_accessed=2**25)
 VM = pl.BlockSpec(memory_space=pltpu.VMEM)
 

time: 48.3 us -> 47.6 us (0.986)
  Pallas kernels: 13 us -> 9.24 us
  waiting for transfers between devices: 3.31 us -> 5.93 us
    ppermute x6, waiting for transfers between devices: 0.41 us -> 3.05 us  [swap(): return lax.ppermute(value, BOTH, [(i, i ^ mask) for i in range(256)])]
    pallas_call x1, Pallas kernels: 2.68 us -> 0.8 us  [local(): call(known_kernel, [shape(512, 256), shape(256, 128), shape(128, 128), sh...]
    pallas_call x1, Pallas kernels: 3.97 us -> 2.1 us  [local(): call(plan_kernel, [shape(2, 6, 128, 128, dtype=BF), shape(8, 128)], cost=...]
    unnamed x32 -> x34, local copies, waits for them, and re-layouts: 1.17 us -> 1.17 us
  transfers between devices with their start and end apart: 10 -> 10, of which waited for: 4 -> 5; matrix products, arithmetic and copies ran while one was open for 0% -> 0% of each run, Pallas kernels for 15% -> 8%
where the time goes in v5:
time: 47.6 us; the launch traced here: 46.9 us
  starting transfers between devices  18.7 us (39%)
  blocking collectives  11.6 us (24%)
  Pallas kernels  9.24 us (19%)
  waiting for transfers between devices  5.93 us (12%)
  local copies, waits for them, and re-layouts  1.17 us (2%)
    ppermute x6, starting transfers between devices, swap(): return lax.ppermute(value, BOTH, [(i, i ^ mask) for i in range(256)])  12.8 us
    all_to_all x1, blocking collectives, swap_roots(): return lax.all_to_all(copies, BOTH, 0, 0, axis_index_groups=groups_of(bits))  11.6 us
    ppermute x1, starting transfers between devices, local(): yb = lax.ppermute(yb, 'gy', across)  4.89 us
    ppermute x6, waiting for transfers between devices, swap(): return lax.ppermute(value, BOTH, [(i, i ^ mask) for i in range(256)])  3.05 us
    pallas_call x1, Pallas kernels, local(): call(last_kernel, shape(512, 256, dtype=BF), [pltpu.VMEM((512, 128), F32)])  2.48 us
    pallas_call x1, Pallas kernels, local(): call(plan_kernel, [shape(2, 6, 128, 128, dtype=BF), shape(8, 128)], cost=...  2.1 us
    pallas_call x1, Pallas kernels, local(): call(up_kernel, [shape(512, 256), shape(256, 128), shape(128, 128), shape...  1.82 us
    ppermute x1, waiting for transfers between devices, local(): ya = lax.ppermute(ya, 'gy', beside)  1.65 us
  transfers between devices with their start and end apart: 10, of which 5 were waited for; matrix products, arithmetic and copies ran while one was open for 0% of the time, Pallas kernels for 8%

profile of v5, /device:TPU:2, one launch (start us, length us, event | category | flops | bytes accessed | tf_op | source)
XLA Modules:
  0.0 46.9 jit_solution(13520347224313287905)
XLA Ops:
  0.0 1.1 %copy-done.2 = bf16[8,8,8,256]{3,2,1,0:T(8,128)(2,1)S(1)} copy-done((bf16[8,8,8,256]{3,2,1,0:T(8,128)(2,1)S(1)}, bf16[8,8,8,256]{3,2,1,0:T(8,128)(2,1)}, u32[]{:S(2)}) %copy-start.2) | copy-done | bytes 262168
  1.1 0.2 shard_map.163
  1.4 0.1 collective-permute-start
  1.5 4.9 %collective-permute-start.1 = (bf16[8,8,256]{2,1,0:T(8,128)(2,1)S(1)}, bf16[8,8,256]{2,1,0:T(8,128)(2,1)S(1)}, u32[]{:S(2)}, u32[]{:S(2)}) collective-permute-start(bf16[8,8,256]{2,1,0:T(8,128)(2,1)S(1)} %get-tuple-element.49), channel_id=1, source_target_pairs={{1,2},{3,4},{5,6},{7,8},{9,10},{11,12},{13,14},{2,1},{4,3},{6,5},{... | collective-permute-start | bytes 98312 | tf_op jit(solution)/shard_map/ppermute | solution.py:360
  6.4 0.7 %collective-permute-start.2 = (bf16[8,8,256]{2,1,0:T(8,128)(2,1)S(1)}, bf16[8,8,256]{2,1,0:T(8,128)(2,1)S(1)}, u32[]{:S(2)}, u32[]{:S(2)}) collective-permute-start(bf16[8,8,256]{2,1,0:T(8,128)(2,1)S(1)} %get-tuple-element.50), channel_id=1, source_target_pairs={{16,32},{48,64},{80,96},{112,128},{144,160},{176,192},{208,224},{3... | collective-permute-start | bytes 98312 | tf_op jit(solution)/shard_map/ppermute | solution.py:359
  7.0 0.3 collective-permute-start.3
  7.4 0.8 %shard_map.164 = (f32[512,256]{1,0:T(8,128)S(1)}, f32[64,256]{1,0:T(8,128)S(1)}, f32[64,256]{1,0:T(8,128)S(1)}, bf16[2,128,256]{2,1,0:T(8,128)(2,1)S(1)}, bf16[2...) custom-call(bf16[512,256]{1,0:T(8,128)(2,1)S(1)} %bitcast.4, ...), custom_call_target="tpu_custom_call" | custom-call | tf_op jit(solution)/shard_map/pallas_call | solution.py:362
  8.2 1.2 %collective-permute-done.1.yb_ref = bf16[8,8,256]{2,1,0:T(8,128)(2,1)S(1)} collective-permute-done((bf16[8,8,256]{2,1,0:T(8,128)(2,1)S(1)}, bf16[8,8,256]{2,1,0:T(8,128)(2,1)S(1)}, u32[]{:S(2)}, u32[]{:S(2)}) %collective-permute-start.1) | collective-permute-done | bytes 32800 | tf_op jit(solution)/shard_map/ppermute | solution.py:360
  9.4 1.7 %collective-permute-done.3.ya_ref = bf16[8,8,256]{2,1,0:T(8,128)(2,1)S(1)} collective-permute-done((bf16[8,8,256]{2,1,0:T(8,128)(2,1)S(1)}, bf16[8,8,256]{2,1,0:T(8,128)(2,1)S(1)}, u32[]{:S(2)}, u32[]{:S(2)}) %collective-permute-start.3) | collective-permute-done | bytes 32800 | tf_op jit(solution)/shard_map/ppermute | solution.py:358
  11.0 1.8 %shard_map.165 = (f32[512,256]{1,0:T(8,128)S(1)}, f32[256,128]{1,0:T(8,128)S(1)}, f32[128,128]{1,0:T(8,128)S(1)}, f32[64,256]{1,0:T(8,128)S(1)}, f32[32,256]{1,0...) custom-call(f32[512,256]{1,0:T(8,128)S(1)} %get-tuple-element.46.base_ref, ...), custom_call_target="tpu_custom_call" | custom-call | tf_op jit(solution)/shard_map/pallas_call | solution.py:367
  12.9 11.6 %all_to_all.5.got_ref = f32[16,8,128]{2,1,0:T(8,128)S(1)} all-to-all(f32[16,8,128]{2,1,0:T(8,128)S(1)} %get-tuple-element.56), channel_id=1, replica_groups={{0,16,1,17,32,48,33,49,2,18,3,19,34,50,35,51},{4,20,5,21,36,52,37,53,6,..., dimensions={0} | all-to-all | bytes 131072 | tf_op jit(solution)/shard_map/all_to_all | solution.py:312
  24.5 0.6 %shard_map.166 = (f32[128,128]{1,0:T(8,128)S(1)}, f32[64,128]{1,0:T(8,128)S(1)}, f32[32,128]{1,0:T(8,128)S(1)}, f32[16,128]{1,0:T(8,128)S(1)}, f32[8,128]{1,0:T(8,128)S(1)}) custom-call(f32[16,8,128]{2,1,0:T(8,128)S(1)} %all_to_all.5.got_ref, f32[12,256,128]{2,1,0:T(8,128)S(1)} %copy-done), custom_call_target="tpu_custom_call" | custom-call | tf_op jit(solution)/shard_map/pallas_call | solution.py:374
  25.1 6.6 %collective-permute-start.4 = (f32[8,128]{1,0:T(8,128)S(1)}, f32[8,128]{1,0:T(8,128)S(1)}, u32[]{:S(2)}, u32[]{:S(2)}) collective-permute-start(f32[8,128]{1,0:T(8,128)S(1)} %get-tuple-element.57.root_ref), channel_id=1, source_target_pairs={{0,128},{1,129},{2,130},{3,131},{4,132},{5,133},{6,134},{7,135},{8... | collective-permute-start | bytes 12296 | tf_op jit(solution)/shard_map/ppermute | solution.py:316
  31.7 1.4 %collective-permute-start.5 = (f32[8,128]{1,0:T(8,128)S(1)}, f32[8,128]{1,0:T(8,128)S(1)}, u32[]{:S(2)}, u32[]{:S(2)}) collective-permute-start(f32[8,128]{1,0:T(8,128)S(1)} %get-tuple-element.57.root_ref), channel_id=1, source_target_pairs={{0,192},{1,193},{2,194},{3,195},{4,196},{5,197},{6,198},{7,199},{8... | collective-permute-start | bytes 12296 | tf_op jit(solution)/shard_map/ppermute | solution.py:316
  33.2 2.1 %shard_map.168 = (bf16[2,6,128,128]{3,2,1,0:T(8,128)(2,1)S(1)}, f32[8,128]{1,0:T(8,128)S(1)}) custom-call(f32[128,128]{1,0:T(8,128)S(1)} %get-tuple-element.61.s0_ref, f32[64,128]{1,0:T(8,128)S(1)} %get-tuple-element.62.s1_ref, f32[32,128]{1,0:T(8,128)S(1)} %get-tuple-element.63.s2_ref, f32[16,128]{1,0:T(8,128)S(1)} %get-tuple-element.64.s3_ref, ...), custom_call_target="tpu_custom_call" | custom-call | flops 10000000000 | bytes 33554432 | tf_op jit(solution)/shard_map/pallas_call | solution.py:379
  35.4 2.0 %collective-permute-done.5.c_ref = f32[8,128]{1,0:T(8,128)S(1)} collective-permute-done((f32[8,128]{1,0:T(8,128)S(1)}, f32[8,128]{1,0:T(8,128)S(1)}, u32[]{:S(2)}, u32[]{:S(2)}) %collective-permute-start.5) | collective-permute-done | bytes 4128 | tf_op jit(solution)/shard_map/ppermute | solution.py:316
  37.4 0.2 collective-permute-done.6.a_ref
  37.6 0.5 shard_map.167
  38.1 1.8 %collective-permute-start.8 = (f32[8,128]{1,0:T(8,128)S(1)}, f32[8,128]{1,0:T(8,128)S(1)}, u32[]{:S(2)}, u32[]{:S(2)}) collective-permute-start(f32[8,128]{1,0:T(8,128)S(1)} %get-tuple-element.60.after_ref), channel_id=1, source_target_pairs={{0,8},{1,9},{2,10},{3,11},{4,12},{5,13},{6,14},{7,15},{8,0},{9,1},... | collective-permute-start | bytes 12296 | tf_op jit(solution)/shard_map/ppermute | solution.py:316
  39.9 0.2 collective-permute-start.9
  40.1 2.7 %collective-permute-start.7 = (f32[2,8,128]{2,1,0:T(8,128)S(1)}, f32[2,8,128]{2,1,0:T(8,128)S(1)}, u32[]{:S(2)}, u32[]{:S(2)}) collective-permute-start(f32[2,8,128]{2,1,0:T(8,128)S(1)} %get-tuple-element.59.pair_ref), channel_id=1, source_target_pairs={{0,4},{1,5},{2,6},{3,7},{4,0},{5,1},{6,2},{7,3},{8,12},{9,13},{10,... | collective-permute-start | bytes 24584 | tf_op jit(solution)/shard_map/ppermute | solution.py:316
  42.8 0.8 %shard_map.169 = (f32[512,256]{1,0:T(8,128)S(1)}, f32[256,128]{1,0:T(8,128)S(1)}, f32[128,128]{1,0:T(8,128)S(1)}, f32[64,256]{1,0:T(8,128)S(1)}, f32[32,256]{1,0...) custom-call(f32[256,128]{1,0:T(8,128)S(1)} %get-tuple-element.67.c0_, ...), custom_call_target="tpu_custom_call" | custom-call | flops 10000000000 | bytes 33554432 | tf_op jit(solution)/shard_map/pallas_call | solution.py:384
  43.7 0.8 %collective-permute-done.7.near_ref = f32[2,8,128]{2,1,0:T(8,128)S(1)} collective-permute-done((f32[2,8,128]{2,1,0:T(8,128)S(1)}, f32[2,8,128]{2,1,0:T(8,128)S(1)}, u32[]{:S(2)}, u32[]{:S(2)}) %collective-permute-start.7) | collective-permute-done | bytes 8224 | tf_op jit(solution)/shard_map/ppermute | solution.py:316
  44.4 2.5 %shard_map.170 = bf16[512,256]{1,0:T(8,128)(2,1)} custom-call(f32[8,256]{1,0:T(8,128)S(1)} %get-tuple-element.58.both_ref, f32[2,8,128]{2,1,0:T(8,128)S(1)} %get-tuple-element.59.pair_ref, f32[2,8,128]{2,1,0:T(8,128)S(1)} %collective-permute-done.7.near_ref, f32[8,128]{1,0:T(8,128)S(1)} %collective-permute-done.8.far_ref, ...), custom_call_target="tpu_custom_call" | custom-call | tf_op jit(solution)/shard_map/pallas_call | solution.py:392
  (39 shorter events, 0.1 us)
Async XLA Ops:
  0.0 7.3 %copy-start.1 = (bf16[512,512]{1,0:T(8,128)(2,1)S(1)}, bf16[512,512]{1,0:T(8,128)(2,1)}, u32[]{:S(2)}) copy-start(bf16[512,512]{1,0:T(8,128)(2,1)} %constant.2.clone.table_ref) | copy-start | bytes 1572868
  0.0 7.3 %copy-start = (f32[12,256,128]{2,1,0:T(8,128)S(1)}, f32[12,256,128]{2,1,0:T(8,128)}, u32[]{:S(2)}) copy-start(f32[12,256,128]{2,1,0:T(8,128)} %rest_ref.7) | copy-start | bytes 4718596
  1.1 6.2 %copy-start.5 = (f32[128,64]{0,1:T(8,128)S(1)}, f32[128,64]{0,1:T(8,128)}, u32[]{:S(2)}) copy-start(f32[128,64]{0,1:T(8,128)} %param.23) | copy-start | bytes 98308
  1.1 6.2 %copy-start.6 = (s32[4,8,8]{2,1,0:T(8,128)S(1)}, s32[4,8,8]{2,1,0:T(8,128)}, u32[]{:S(2)}) copy-start(s32[4,8,8]{2,1,0:T(8,128)} %flow_ref.1) | copy-start | bytes 3076
  1.1 6.2 %copy-start.7 = (f32[2,8,8]{2,1,0:T(8,128)S(1)}, f32[2,8,8]{2,1,0:T(8,128)}, u32[]{:S(2)}) copy-start(f32[2,8,8]{2,1,0:T(8,128)} %vel_ref.1) | copy-start | bytes 1540
  1.4 5.9 %collective-permute-start = (bf16[8,8,256]{2,1,0:T(8,128)(2,1)S(1)}, bf16[8,8,256]{2,1,0:T(8,128)(2,1)S(1)}, u32[]{:S(2)}, u32[]{:S(2)}) collective-permute-start(bf16[8,8,256]{2,1,0:T(8,128)(2,1)S(1)} %get-tuple-element.45), channel_id=1, source_target_pairs={{0,16},{16,0},{32,48},{48,32},{64,80},{80,64},{96,112},{112,96},{1... | collective-permute-start | bytes 98312 | tf_op jit(solution)/shard_map/ppermute | solution.py:357
  1.5 7.9 %collective-permute-start.1 = (bf16[8,8,256]{2,1,0:T(8,128)(2,1)S(1)}, bf16[8,8,256]{2,1,0:T(8,128)(2,1)S(1)}, u32[]{:S(2)}, u32[]{:S(2)}) collective-permute-start(bf16[8,8,256]{2,1,0:T(8,128)(2,1)S(1)} %get-tuple-element.49), channel_id=1, source_target_pairs={{1,2},{3,4},{5,6},{7,8},{9,10},{11,12},{13,14},{2,1},{4,3},{6,5},{... | collective-permute-start | bytes 98312 | tf_op jit(solution)/shard_map/ppermute | solution.py:360
  6.4 3.0 %collective-permute-start.2 = (bf16[8,8,256]{2,1,0:T(8,128)(2,1)S(1)}, bf16[8,8,256]{2,1,0:T(8,128)(2,1)S(1)}, u32[]{:S(2)}, u32[]{:S(2)}) collective-permute-start(bf16[8,8,256]{2,1,0:T(8,128)(2,1)S(1)} %get-tuple-element.50), channel_id=1, source_target_pairs={{16,32},{48,64},{80,96},{112,128},{144,160},{176,192},{208,224},{3... | collective-permute-start | bytes 98312 | tf_op jit(solution)/shard_map/ppermute | solution.py:359
  7.0 4.0 %collective-permute-start.3 = (bf16[8,8,256]{2,1,0:T(8,128)(2,1)S(1)}, bf16[8,8,256]{2,1,0:T(8,128)(2,1)S(1)}, u32[]{:S(2)}, u32[]{:S(2)}) collective-permute-start(bf16[8,8,256]{2,1,0:T(8,128)(2,1)S(1)} %get-tuple-element.51), channel_id=1, source_target_pairs={{0,1},{1,0},{2,3},{3,2},{4,5},{5,4},{6,7},{7,6},{8,9},{9,8},{10,11... | collective-permute-start | bytes 98312 | tf_op jit(solution)/shard_map/ppermute | solution.py:358
  7.4 25.8 %copy-start.9 = (f32[12,128,256]{2,1,0:T(8,128)S(1)}, f32[12,128,256]{2,1,0:T(8,128)}, u32[]{:S(2)}) copy-start(f32[12,128,256]{2,1,0:T(8,128)} %prest_ref.3) | copy-start | bytes 4718596
  11.0 22.1 %copy-start.8 = (f32[12,256,256]{2,1,0:T(8,128)S(1)}, f32[12,256,256]{2,1,0:T(8,128)}, u32[]{:S(2)}) copy-start(f32[12,256,256]{2,1,0:T(8,128)} %srest_ref.3) | copy-start | bytes 9437188
  11.0 22.1 %copy-start.11 = (f32[128,128]{1,0:T(8,128)S(1)}, f32[128,128]{1,0:T(8,128)}, u32[]{:S(2)}) copy-start(f32[128,128]{1,0:T(8,128)} %rootmap_ref.1) | copy-start | bytes 196612
  25.1 10.3 %collective-permute-start.4 = (f32[8,128]{1,0:T(8,128)S(1)}, f32[8,128]{1,0:T(8,128)S(1)}, u32[]{:S(2)}, u32[]{:S(2)}) collective-permute-start(f32[8,128]{1,0:T(8,128)S(1)} %get-tuple-element.57.root_ref), channel_id=1, source_target_pairs={{0,128},{1,129},{2,130},{3,131},{4,132},{5,133},{6,134},{7,135},{8... | collective-permute-start | bytes 12296 | tf_op jit(solution)/shard_map/ppermute | solution.py:316
  31.7 5.7 %collective-permute-start.5 = (f32[8,128]{1,0:T(8,128)S(1)}, f32[8,128]{1,0:T(8,128)S(1)}, u32[]{:S(2)}, u32[]{:S(2)}) collective-permute-start(f32[8,128]{1,0:T(8,128)S(1)} %get-tuple-element.57.root_ref), channel_id=1, source_target_pairs={{0,192},{1,193},{2,194},{3,195},{4,196},{5,197},{6,198},{7,199},{8... | collective-permute-start | bytes 12296 | tf_op jit(solution)/shard_map/ppermute | solution.py:316
  33.1 4.5 %collective-permute-start.6 = (f32[8,128]{1,0:T(8,128)S(1)}, f32[8,128]{1,0:T(8,128)S(1)}, u32[]{:S(2)}, u32[]{:S(2)}) collective-permute-start(f32[8,128]{1,0:T(8,128)S(1)} %get-tuple-element.57.root_ref), channel_id=1, source_target_pairs={{0,64},{1,65},{2,66},{3,67},{4,68},{5,69},{6,70},{7,71},{8,72},{9,... | collective-permute-start | bytes 12296 | tf_op jit(solution)/shard_map/ppermute | solution.py:316
  35.3 7.5 %copy-start.10 = (f32[256,256]{1,0:T(8,128)S(1)}, f32[256,256]{1,0:T(8,128)}, u32[]{:S(2)}) copy-start(f32[256,256]{1,0:T(8,128)} %solve_ref.1) | copy-start | bytes 786436
  35.3 7.5 %copy-start.12 = (f32[128,128]{1,0:T(8,128)S(1)}, f32[128,128]{1,0:T(8,128)}, u32[]{:S(2)}) copy-start(f32[128,128]{1,0:T(8,128)} %psecond_ref.1) | copy-start | bytes 196612
  35.3 7.5 %copy-start.13 = (f32[128,128]{1,0:T(8,128)S(1)}, f32[128,128]{1,0:T(8,128)}, u32[]{:S(2)}) copy-start(f32[128,128]{1,0:T(8,128)} %sfirst_ref.1) | copy-start | bytes 196612
  35.3 7.5 %copy-start.14 = (f32[128,128]{1,0:T(8,128)S(1)}, f32[128,128]{1,0:T(8,128)}, u32[]{:S(2)}) copy-start(f32[128,128]{1,0:T(8,128)} %ssecond_ref.1) | copy-start | bytes 196612
  35.3 7.5 %copy-start.15 = (f32[64,256]{1,0:T(8,128)S(1)}, f32[64,256]{1,0:T(8,128)}, u32[]{:S(2)}) copy-start(f32[64,256]{1,0:T(8,128)} %lift_ref.1) | copy-start | bytes 196612
  35.3 7.5 %copy-start.16 = (f32[64,128]{1,0:T(8,128)S(1)}, f32[64,128]{1,0:T(8,128)}, u32[]{:S(2)}) copy-start(f32[64,128]{1,0:T(8,128)} %pfirst_ref.1) | copy-start | bytes 98308
  38.1 5.6 %collective-permute-start.8 = (f32[8,128]{1,0:T(8,128)S(1)}, f32[8,128]{1,0:T(8,128)S(1)}, u32[]{:S(2)}, u32[]{:S(2)}) collective-permute-start(f32[8,128]{1,0:T(8,128)S(1)} %get-tuple-element.60.after_ref), channel_id=1, source_target_pairs={{0,8},{1,9},{2,10},{3,11},{4,12},{5,13},{6,14},{7,15},{8,0},{9,1},... | collective-permute-start | bytes 12296 | tf_op jit(solution)/shard_map/ppermute | solution.py:316
  39.9 3.7 %collective-permute-start.9 = (f32[8,128]{1,0:T(8,128)S(1)}, f32[8,128]{1,0:T(8,128)S(1)}, u32[]{:S(2)}, u32[]{:S(2)}) collective-permute-start(f32[8,128]{1,0:T(8,128)S(1)} %get-tuple-element.60.after_ref), channel_id=1, source_target_pairs={{0,12},{1,13},{2,14},{3,15},{4,8},{5,9},{6,10},{7,11},{8,4},{9,5},... | collective-permute-start | bytes 12296 | tf_op jit(solution)/shard_map/ppermute | solution.py:316
  40.1 4.3 %collective-permute-start.7 = (f32[2,8,128]{2,1,0:T(8,128)S(1)}, f32[2,8,128]{2,1,0:T(8,128)S(1)}, u32[]{:S(2)}, u32[]{:S(2)}) collective-permute-start(f32[2,8,128]{2,1,0:T(8,128)S(1)} %get-tuple-element.59.pair_ref), channel_id=1, source_target_pairs={{0,4},{1,5},{2,6},{3,7},{4,0},{5,1},{6,2},{7,3},{8,12},{9,13},{10,... | collective-permute-start | bytes 24584 | tf_op jit(solution)/shard_map/ppermute | solution.py:316
  (3 other events, 13.5 us)

commit v6 on v5

--- a/solution.py
+++ b/solution.py
@@ -282,7 +282,7 @@
     part_ref[...] = mm(forcing_ref[...], solve_ref[...])
 
 
-def last_kernel(both_ref, pair_ref, near_ref, far_ref, farther_ref, plan_ref, known_ref, part_ref,
+def last_kernel(both_ref, pair_ref, farther_ref, far_ref, near_ref, plan_ref, known_ref, part_ref,
                 t0_ref, t1_ref, t2_ref, t3_ref, t4_ref, t5_ref,
                 pfirst_ref, psecond_ref, prest_ref, lift_ref, out_ref, turn_ref):
     sources = [both_ref[...], pair_ref[0], near_ref[0], pair_ref[1] + near_ref[1], far_ref[...] + farther_ref[...]]
@@ -363,7 +363,7 @@
         base_kernel,
         [shape(512, 256), shape(64, 256), shape(64, 256), shape(2, 128, 256, dtype=BF),
          shape(2, 64, 128, dtype=BF), shape(2, 128, 128, dtype=BF), shape(2, 4, 256, 128, dtype=BF)],
-    )(tracers.reshape(512, 256), velocity, inflow, table, leaf_skeleton.T, merge_first.T, merge_second, merge_rest, xa)
+    )(tracers.reshape(512, 256), velocity, inflow, table, leaf_skeleton.T, merge_first.T, merge_second, merge_rest[:4], xa)
     forcing, c0, c1, c2, c3, c4, c5, roots = call(
         up_kernel,
         [shape(512, 256), shape(256, 128), shape(128, 128), shape(64, 256), shape(32, 256), shape(16, 256),
@@ -380,7 +380,7 @@
         s0, s1, s2, s3, merge_rest, parent_rest, sibling_rest, root_map)
     both, pair, last = call(z_kernel, [shape(8, 256), shape(2, 8, 128), shape(8, 128)])(
         root, second_z, third, first_z, merge_rest)
-    farther, far, near = swap(last, 12), swap(last, 8), swap(pair, 4)
+    near, far, farther = swap(pair, 4), swap(last, 8), swap(last, 12)
     part, *rest_of = call(
         known_kernel,
         [shape(512, 256), shape(256, 128), shape(128, 128), shape(64, 256), shape(32, 256), shape(16, 256), shape(8, 256),
@@ -390,7 +390,7 @@
     )(c0, c1, c2, c3, c4, c5, forcing, parent_first, parent_second, parent_rest, sibling_first, sibling_second,
       sibling_rest, leaf_solve, leaf_lift, last)
     out = call(last_kernel, shape(512, 256, dtype=BF), [pltpu.VMEM((512, 128), F32)])(
-        both, pair, near, far, farther, plan, known, part, *rest_of)
+        both, pair, farther, far, near, plan, known, part, *rest_of)
     return out.reshape(tracers.shape)
 
 

time: 47.6 us -> 47.4 us (level)
  starting transfers between devices: 18.7 us -> 18.1 us
  waiting for transfers between devices: 5.93 us -> 6.47 us
    ppermute x6, starting transfers between devices: 12.8 us -> 12.2 us  [swap(): return lax.ppermute(value, BOTH, [(i, i ^ mask) for i in range(256)])]
    ppermute x6, waiting for transfers between devices: 3.05 us -> 3.64 us  [swap(): return lax.ppermute(value, BOTH, [(i, i ^ mask) for i in range(256)])]
where the time goes in v6:
time: 47.4 us; the launch traced here: 46.9 us
  starting transfers between devices  18.1 us (38%)
  blocking collectives  11.6 us (24%)
  Pallas kernels  9.24 us (19%)
  waiting for transfers between devices  6.47 us (14%)
  local copies, waits for them, and re-layouts  1.21 us (3%)
    ppermute x6, starting transfers between devices, swap(): return lax.ppermute(value, BOTH, [(i, i ^ mask) for i in range(256)])  12.2 us
    all_to_all x1, blocking collectives, swap_roots(): return lax.all_to_all(copies, BOTH, 0, 0, axis_index_groups=groups_of(bits))  11.6 us
    ppermute x1, starting transfers between devices, local(): yb = lax.ppermute(yb, 'gy', across)  4.89 us
    ppermute x6, waiting for transfers between devices, swap(): return lax.ppermute(value, BOTH, [(i, i ^ mask) for i in range(256)])  3.64 us
    pallas_call x1, Pallas kernels, local(): call(last_kernel, shape(512, 256, dtype=BF), [pltpu.VMEM((512, 128), F32)])  2.49 us
    pallas_call x1, Pallas kernels, local(): call(plan_kernel, [shape(2, 6, 128, 128, dtype=BF), shape(8, 128)], cost=...  2.09 us
    pallas_call x1, Pallas kernels, local(): call(up_kernel, [shape(512, 256), shape(256, 128), shape(128, 128), shape...  1.82 us
    ppermute x1, waiting for transfers between devices, local(): ya = lax.ppermute(ya, 'gy', beside)  1.65 us
  transfers between devices with their start and end apart: 10, of which 5 were waited for; matrix products, arithmetic and copies ran while one was open for 0% of the time, Pallas kernels for 8%

profile of v6, /device:TPU:2, one launch (start us, length us, event | category | flops | bytes accessed | tf_op | source)
XLA Modules:
  0.0 46.9 jit_solution(3392396848333846298)
XLA Ops:
  0.0 1.1 %copy-done.2 = bf16[8,8,8,256]{3,2,1,0:T(8,128)(2,1)S(1)} copy-done((bf16[8,8,8,256]{3,2,1,0:T(8,128)(2,1)S(1)}, bf16[8,8,8,256]{3,2,1,0:T(8,128)(2,1)}, u32[]{:S(2)}) %copy-start.2) | copy-done | bytes 262168
  1.1 0.2 shard_map.163
  1.4 0.1 collective-permute-start
  1.5 4.9 %collective-permute-start.1 = (bf16[8,8,256]{2,1,0:T(8,128)(2,1)S(1)}, bf16[8,8,256]{2,1,0:T(8,128)(2,1)S(1)}, u32[]{:S(2)}, u32[]{:S(2)}) collective-permute-start(bf16[8,8,256]{2,1,0:T(8,128)(2,1)S(1)} %get-tuple-element.49), channel_id=1, source_target_pairs={{1,2},{3,4},{5,6},{7,8},{9,10},{11,12},{13,14},{2,1},{4,3},{6,5},{... | collective-permute-start | bytes 98312 | tf_op jit(solution)/shard_map/ppermute | solution.py:360
  6.4 0.7 %collective-permute-start.2 = (bf16[8,8,256]{2,1,0:T(8,128)(2,1)S(1)}, bf16[8,8,256]{2,1,0:T(8,128)(2,1)S(1)}, u32[]{:S(2)}, u32[]{:S(2)}) collective-permute-start(bf16[8,8,256]{2,1,0:T(8,128)(2,1)S(1)} %get-tuple-element.50), channel_id=1, source_target_pairs={{16,32},{48,64},{80,96},{112,128},{144,160},{176,192},{208,224},{3... | collective-permute-start | bytes 98312 | tf_op jit(solution)/shard_map/ppermute | solution.py:359
  7.0 0.3 collective-permute-start.3
  7.4 0.8 %shard_map.164 = (f32[512,256]{1,0:T(8,128)S(1)}, f32[64,256]{1,0:T(8,128)S(1)}, f32[64,256]{1,0:T(8,128)S(1)}, bf16[2,128,256]{2,1,0:T(8,128)(2,1)S(1)}, bf16[2...) custom-call(bf16[512,256]{1,0:T(8,128)(2,1)S(1)} %bitcast.4, ...), custom_call_target="tpu_custom_call" | custom-call | tf_op jit(solution)/shard_map/pallas_call | solution.py:362
  8.2 1.2 %collective-permute-done.1.yb_ref = bf16[8,8,256]{2,1,0:T(8,128)(2,1)S(1)} collective-permute-done((bf16[8,8,256]{2,1,0:T(8,128)(2,1)S(1)}, bf16[8,8,256]{2,1,0:T(8,128)(2,1)S(1)}, u32[]{:S(2)}, u32[]{:S(2)}) %collective-permute-start.1) | collective-permute-done | bytes 32800 | tf_op jit(solution)/shard_map/ppermute | solution.py:360
  9.4 1.7 %collective-permute-done.3.ya_ref = bf16[8,8,256]{2,1,0:T(8,128)(2,1)S(1)} collective-permute-done((bf16[8,8,256]{2,1,0:T(8,128)(2,1)S(1)}, bf16[8,8,256]{2,1,0:T(8,128)(2,1)S(1)}, u32[]{:S(2)}, u32[]{:S(2)}) %collective-permute-start.3) | collective-permute-done | bytes 32800 | tf_op jit(solution)/shard_map/ppermute | solution.py:358
  11.0 1.8 %shard_map.165 = (f32[512,256]{1,0:T(8,128)S(1)}, f32[256,128]{1,0:T(8,128)S(1)}, f32[128,128]{1,0:T(8,128)S(1)}, f32[64,256]{1,0:T(8,128)S(1)}, f32[32,256]{1,0...) custom-call(f32[512,256]{1,0:T(8,128)S(1)} %get-tuple-element.46.base_ref, ...), custom_call_target="tpu_custom_call" | custom-call | tf_op jit(solution)/shard_map/pallas_call | solution.py:367
  12.9 11.6 %all_to_all.5.got_ref = f32[16,8,128]{2,1,0:T(8,128)S(1)} all-to-all(f32[16,8,128]{2,1,0:T(8,128)S(1)} %get-tuple-element.56), channel_id=1, replica_groups={{0,16,1,17,32,48,33,49,2,18,3,19,34,50,35,51},{4,20,5,21,36,52,37,53,6,..., dimensions={0} | all-to-all | bytes 131072 | tf_op jit(solution)/shard_map/all_to_all | solution.py:312
  24.5 0.6 %shard_map.166 = (f32[128,128]{1,0:T(8,128)S(1)}, f32[64,128]{1,0:T(8,128)S(1)}, f32[32,128]{1,0:T(8,128)S(1)}, f32[16,128]{1,0:T(8,128)S(1)}, f32[8,128]{1,0:T(8,128)S(1)}) custom-call(f32[16,8,128]{2,1,0:T(8,128)S(1)} %all_to_all.5.got_ref, f32[12,256,128]{2,1,0:T(8,128)S(1)} %copy-done), custom_call_target="tpu_custom_call" | custom-call | tf_op jit(solution)/shard_map/pallas_call | solution.py:374
  25.1 6.6 %collective-permute-start.4 = (f32[8,128]{1,0:T(8,128)S(1)}, f32[8,128]{1,0:T(8,128)S(1)}, u32[]{:S(2)}, u32[]{:S(2)}) collective-permute-start(f32[8,128]{1,0:T(8,128)S(1)} %get-tuple-element.57.root_ref), channel_id=1, source_target_pairs={{0,128},{1,129},{2,130},{3,131},{4,132},{5,133},{6,134},{7,135},{8... | collective-permute-start | bytes 12296 | tf_op jit(solution)/shard_map/ppermute | solution.py:316
  31.7 1.4 %collective-permute-start.5 = (f32[8,128]{1,0:T(8,128)S(1)}, f32[8,128]{1,0:T(8,128)S(1)}, u32[]{:S(2)}, u32[]{:S(2)}) collective-permute-start(f32[8,128]{1,0:T(8,128)S(1)} %get-tuple-element.57.root_ref), channel_id=1, source_target_pairs={{0,192},{1,193},{2,194},{3,195},{4,196},{5,197},{6,198},{7,199},{8... | collective-permute-start | bytes 12296 | tf_op jit(solution)/shard_map/ppermute | solution.py:316
  33.2 2.1 %shard_map.168 = (bf16[2,6,128,128]{3,2,1,0:T(8,128)(2,1)S(1)}, f32[8,128]{1,0:T(8,128)S(1)}) custom-call(f32[128,128]{1,0:T(8,128)S(1)} %get-tuple-element.61.s0_ref, f32[64,128]{1,0:T(8,128)S(1)} %get-tuple-element.62.s1_ref, f32[32,128]{1,0:T(8,128)S(1)} %get-tuple-element.63.s2_ref, f32[16,128]{1,0:T(8,128)S(1)} %get-tuple-element.64.s3_ref, ...), custom_call_target="tpu_custom_call" | custom-call | flops 10000000000 | bytes 33554432 | tf_op jit(solution)/shard_map/pallas_call | solution.py:379
  35.4 2.0 %collective-permute-done.5.c_ref = f32[8,128]{1,0:T(8,128)S(1)} collective-permute-done((f32[8,128]{1,0:T(8,128)S(1)}, f32[8,128]{1,0:T(8,128)S(1)}, u32[]{:S(2)}, u32[]{:S(2)}) %collective-permute-start.5) | collective-permute-done | bytes 4128 | tf_op jit(solution)/shard_map/ppermute | solution.py:316
  37.4 0.2 collective-permute-done.6.a_ref
  37.6 0.5 shard_map.167
  38.1 1.2 %collective-permute-start.7 = (f32[8,128]{1,0:T(8,128)S(1)}, f32[8,128]{1,0:T(8,128)S(1)}, u32[]{:S(2)}, u32[]{:S(2)}) collective-permute-start(f32[8,128]{1,0:T(8,128)S(1)} %get-tuple-element.60.after_ref), channel_id=1, source_target_pairs={{0,12},{1,13},{2,14},{3,15},{4,8},{5,9},{6,10},{7,11},{8,4},{9,5},... | collective-permute-start | bytes 12296 | tf_op jit(solution)/shard_map/ppermute | solution.py:316
  39.3 1.4 %collective-permute-start.8 = (f32[8,128]{1,0:T(8,128)S(1)}, f32[8,128]{1,0:T(8,128)S(1)}, u32[]{:S(2)}, u32[]{:S(2)}) collective-permute-start(f32[8,128]{1,0:T(8,128)S(1)} %get-tuple-element.60.after_ref), channel_id=1, source_target_pairs={{0,8},{1,9},{2,10},{3,11},{4,12},{5,13},{6,14},{7,15},{8,0},{9,1},... | collective-permute-start | bytes 12296 | tf_op jit(solution)/shard_map/ppermute | solution.py:316
  40.7 1.5 %collective-permute-start.9 = (f32[2,8,128]{2,1,0:T(8,128)S(1)}, f32[2,8,128]{2,1,0:T(8,128)S(1)}, u32[]{:S(2)}, u32[]{:S(2)}) collective-permute-start(f32[2,8,128]{2,1,0:T(8,128)S(1)} %get-tuple-element.59.pair_ref), channel_id=1, source_target_pairs={{0,4},{1,5},{2,6},{3,7},{4,0},{5,1},{6,2},{7,3},{8,12},{9,13},{10,... | collective-permute-start | bytes 24584 | tf_op jit(solution)/shard_map/ppermute | solution.py:316
  42.2 0.8 %shard_map.169 = (f32[512,256]{1,0:T(8,128)S(1)}, f32[256,128]{1,0:T(8,128)S(1)}, f32[128,128]{1,0:T(8,128)S(1)}, f32[64,256]{1,0:T(8,128)S(1)}, f32[32,256]{1,0...) custom-call(f32[256,128]{1,0:T(8,128)S(1)} %get-tuple-element.67.c0_, ...), custom_call_target="tpu_custom_call" | custom-call | flops 10000000000 | bytes 33554432 | tf_op jit(solution)/shard_map/pallas_call | solution.py:384
  43.0 1.4 %collective-permute-done.8.far_ref = f32[8,128]{1,0:T(8,128)S(1)} collective-permute-done((f32[8,128]{1,0:T(8,128)S(1)}, f32[8,128]{1,0:T(8,128)S(1)}, u32[]{:S(2)}, u32[]{:S(2)}) %collective-permute-start.8) | collective-permute-done | bytes 4128 | tf_op jit(solution)/shard_map/ppermute | solution.py:316
  44.4 2.5 %shard_map.170 = bf16[512,256]{1,0:T(8,128)(2,1)} custom-call(f32[8,256]{1,0:T(8,128)S(1)} %get-tuple-element.58.both_ref, f32[2,8,128]{2,1,0:T(8,128)S(1)} %get-tuple-element.59.pair_ref, f32[8,128]{1,0:T(8,128)S(1)} %collective-permute-done.7.farther_ref, f32[8,128]{1,0:T(8,128)S(1)} %collective-permute-done.8.far_ref, ...), custom_call_target="tpu_custom_call" | custom-call | tf_op jit(solution)/shard_map/pallas_call | solution.py:392
  (40 shorter events, 0.2 us)
Async XLA Ops:
  0.0 7.3 %copy-start.1 = (bf16[512,512]{1,0:T(8,128)(2,1)S(1)}, bf16[512,512]{1,0:T(8,128)(2,1)}, u32[]{:S(2)}) copy-start(bf16[512,512]{1,0:T(8,128)(2,1)} %constant.2.clone.table_ref) | copy-start | bytes 1572868
  0.0 7.3 %copy-start = (f32[12,256,128]{2,1,0:T(8,128)S(1)}, f32[12,256,128]{2,1,0:T(8,128)}, u32[]{:S(2)}) copy-start(f32[12,256,128]{2,1,0:T(8,128)} %rest_ref.5) | copy-start | bytes 4718596
  1.1 6.3 %copy-start.5 = (f32[128,64]{0,1:T(8,128)S(1)}, f32[128,64]{0,1:T(8,128)}, u32[]{:S(2)}) copy-start(f32[128,64]{0,1:T(8,128)} %param.23) | copy-start | bytes 98308
  1.1 6.3 %copy-start.6 = (s32[4,8,8]{2,1,0:T(8,128)S(1)}, s32[4,8,8]{2,1,0:T(8,128)}, u32[]{:S(2)}) copy-start(s32[4,8,8]{2,1,0:T(8,128)} %flow_ref.1) | copy-start | bytes 3076
  1.1 6.3 %copy-start.7 = (f32[2,8,8]{2,1,0:T(8,128)S(1)}, f32[2,8,8]{2,1,0:T(8,128)}, u32[]{:S(2)}) copy-start(f32[2,8,8]{2,1,0:T(8,128)} %vel_ref.1) | copy-start | bytes 1540
  1.4 6.0 %collective-permute-start = (bf16[8,8,256]{2,1,0:T(8,128)(2,1)S(1)}, bf16[8,8,256]{2,1,0:T(8,128)(2,1)S(1)}, u32[]{:S(2)}, u32[]{:S(2)}) collective-permute-start(bf16[8,8,256]{2,1,0:T(8,128)(2,1)S(1)} %get-tuple-element.45), channel_id=1, source_target_pairs={{0,16},{16,0},{32,48},{48,32},{64,80},{80,64},{96,112},{112,96},{1... | collective-permute-start | bytes 98312 | tf_op jit(solution)/shard_map/ppermute | solution.py:357
  1.5 7.9 %collective-permute-start.1 = (bf16[8,8,256]{2,1,0:T(8,128)(2,1)S(1)}, bf16[8,8,256]{2,1,0:T(8,128)(2,1)S(1)}, u32[]{:S(2)}, u32[]{:S(2)}) collective-permute-start(bf16[8,8,256]{2,1,0:T(8,128)(2,1)S(1)} %get-tuple-element.49), channel_id=1, source_target_pairs={{1,2},{3,4},{5,6},{7,8},{9,10},{11,12},{13,14},{2,1},{4,3},{6,5},{... | collective-permute-start | bytes 98312 | tf_op jit(solution)/shard_map/ppermute | solution.py:360
  6.4 3.0 %collective-permute-start.2 = (bf16[8,8,256]{2,1,0:T(8,128)(2,1)S(1)}, bf16[8,8,256]{2,1,0:T(8,128)(2,1)S(1)}, u32[]{:S(2)}, u32[]{:S(2)}) collective-permute-start(bf16[8,8,256]{2,1,0:T(8,128)(2,1)S(1)} %get-tuple-element.50), channel_id=1, source_target_pairs={{16,32},{48,64},{80,96},{112,128},{144,160},{176,192},{208,224},{3... | collective-permute-start | bytes 98312 | tf_op jit(solution)/shard_map/ppermute | solution.py:359
  7.0 4.0 %collective-permute-start.3 = (bf16[8,8,256]{2,1,0:T(8,128)(2,1)S(1)}, bf16[8,8,256]{2,1,0:T(8,128)(2,1)S(1)}, u32[]{:S(2)}, u32[]{:S(2)}) collective-permute-start(bf16[8,8,256]{2,1,0:T(8,128)(2,1)S(1)} %get-tuple-element.51), channel_id=1, source_target_pairs={{0,1},{1,0},{2,3},{3,2},{4,5},{5,4},{6,7},{7,6},{8,9},{9,8},{10,11... | collective-permute-start | bytes 98312 | tf_op jit(solution)/shard_map/ppermute | solution.py:358
  7.4 25.8 %copy-start.9 = (f32[12,128,256]{2,1,0:T(8,128)S(1)}, f32[12,128,256]{2,1,0:T(8,128)}, u32[]{:S(2)}) copy-start(f32[12,128,256]{2,1,0:T(8,128)} %prest_ref.3) | copy-start | bytes 4718596
  11.0 22.1 %copy-start.8 = (f32[12,256,256]{2,1,0:T(8,128)S(1)}, f32[12,256,256]{2,1,0:T(8,128)}, u32[]{:S(2)}) copy-start(f32[12,256,256]{2,1,0:T(8,128)} %srest_ref.3) | copy-start | bytes 9437188
  11.0 22.1 %copy-start.11 = (f32[128,128]{1,0:T(8,128)S(1)}, f32[128,128]{1,0:T(8,128)}, u32[]{:S(2)}) copy-start(f32[128,128]{1,0:T(8,128)} %rootmap_ref.1) | copy-start | bytes 196612
  25.1 10.3 %collective-permute-start.4 = (f32[8,128]{1,0:T(8,128)S(1)}, f32[8,128]{1,0:T(8,128)S(1)}, u32[]{:S(2)}, u32[]{:S(2)}) collective-permute-start(f32[8,128]{1,0:T(8,128)S(1)} %get-tuple-element.57.root_ref), channel_id=1, source_target_pairs={{0,128},{1,129},{2,130},{3,131},{4,132},{5,133},{6,134},{7,135},{8... | collective-permute-start | bytes 12296 | tf_op jit(solution)/shard_map/ppermute | solution.py:316
  31.7 5.7 %collective-permute-start.5 = (f32[8,128]{1,0:T(8,128)S(1)}, f32[8,128]{1,0:T(8,128)S(1)}, u32[]{:S(2)}, u32[]{:S(2)}) collective-permute-start(f32[8,128]{1,0:T(8,128)S(1)} %get-tuple-element.57.root_ref), channel_id=1, source_target_pairs={{0,192},{1,193},{2,194},{3,195},{4,196},{5,197},{6,198},{7,199},{8... | collective-permute-start | bytes 12296 | tf_op jit(solution)/shard_map/ppermute | solution.py:316
  33.1 4.5 %collective-permute-start.6 = (f32[8,128]{1,0:T(8,128)S(1)}, f32[8,128]{1,0:T(8,128)S(1)}, u32[]{:S(2)}, u32[]{:S(2)}) collective-permute-start(f32[8,128]{1,0:T(8,128)S(1)} %get-tuple-element.57.root_ref), channel_id=1, source_target_pairs={{0,64},{1,65},{2,66},{3,67},{4,68},{5,69},{6,70},{7,71},{8,72},{9,... | collective-permute-start | bytes 12296 | tf_op jit(solution)/shard_map/ppermute | solution.py:316
  35.3 6.9 %copy-start.10 = (f32[256,256]{1,0:T(8,128)S(1)}, f32[256,256]{1,0:T(8,128)}, u32[]{:S(2)}) copy-start(f32[256,256]{1,0:T(8,128)} %solve_ref.1) | copy-start | bytes 786436
  35.3 6.9 %copy-start.12 = (f32[128,128]{1,0:T(8,128)S(1)}, f32[128,128]{1,0:T(8,128)}, u32[]{:S(2)}) copy-start(f32[128,128]{1,0:T(8,128)} %psecond_ref.1) | copy-start | bytes 196612
  35.3 6.9 %copy-start.13 = (f32[128,128]{1,0:T(8,128)S(1)}, f32[128,128]{1,0:T(8,128)}, u32[]{:S(2)}) copy-start(f32[128,128]{1,0:T(8,128)} %sfirst_ref.1) | copy-start | bytes 196612
  35.3 6.9 %copy-start.14 = (f32[128,128]{1,0:T(8,128)S(1)}, f32[128,128]{1,0:T(8,128)}, u32[]{:S(2)}) copy-start(f32[128,128]{1,0:T(8,128)} %ssecond_ref.1) | copy-start | bytes 196612
  35.3 6.9 %copy-start.15 = (f32[64,256]{1,0:T(8,128)S(1)}, f32[64,256]{1,0:T(8,128)}, u32[]{:S(2)}) copy-start(f32[64,256]{1,0:T(8,128)} %lift_ref.1) | copy-start | bytes 196612
  35.3 6.9 %copy-start.16 = (f32[64,128]{1,0:T(8,128)S(1)}, f32[64,128]{1,0:T(8,128)}, u32[]{:S(2)}) copy-start(f32[64,128]{1,0:T(8,128)} %pfirst_ref.1) | copy-start | bytes 98308
  38.1 5.0 %collective-permute-start.7 = (f32[8,128]{1,0:T(8,128)S(1)}, f32[8,128]{1,0:T(8,128)S(1)}, u32[]{:S(2)}, u32[]{:S(2)}) collective-permute-start(f32[8,128]{1,0:T(8,128)S(1)} %get-tuple-element.60.after_ref), channel_id=1, source_target_pairs={{0,12},{1,13},{2,14},{3,15},{4,8},{5,9},{6,10},{7,11},{8,4},{9,5},... | collective-permute-start | bytes 12296 | tf_op jit(solution)/shard_map/ppermute | solution.py:316
  39.3 5.1 %collective-permute-start.8 = (f32[8,128]{1,0:T(8,128)S(1)}, f32[8,128]{1,0:T(8,128)S(1)}, u32[]{:S(2)}, u32[]{:S(2)}) collective-permute-start(f32[8,128]{1,0:T(8,128)S(1)} %get-tuple-element.60.after_ref), channel_id=1, source_target_pairs={{0,8},{1,9},{2,10},{3,11},{4,12},{5,13},{6,14},{7,15},{8,0},{9,1},... | collective-permute-start | bytes 12296 | tf_op jit(solution)/shard_map/ppermute | solution.py:316
  40.7 3.7 %collective-permute-start.9 = (f32[2,8,128]{2,1,0:T(8,128)S(1)}, f32[2,8,128]{2,1,0:T(8,128)S(1)}, u32[]{:S(2)}, u32[]{:S(2)}) collective-permute-start(f32[2,8,128]{2,1,0:T(8,128)S(1)} %get-tuple-element.59.pair_ref), channel_id=1, source_target_pairs={{0,4},{1,5},{2,6},{3,7},{4,0},{5,1},{6,2},{7,3},{8,12},{9,13},{10,... | collective-permute-start | bytes 24584 | tf_op jit(solution)/shard_map/ppermute | solution.py:316
  (3 other events, 13.6 us)
